TPU v7x, 32 devices: a whole 2x2x4 slice. The times are simulated.
32 devices in a mesh: rep: 2 (over x), shard: 16 (over z, y, core).
Axes of the slice: x: 2, y: 2, z: 4, core: 2. Of those that a mesh axis runs over, the one named last changes fastest.
Arguments:
- tokens: bfloat16 [8192, 2048], P(('rep', 'shard')), may hold values from -6 to 6
- doc_ids: int32 [8192], P(('rep', 'shard')), may hold values from 0 to 31, as said below
- cotangent: bfloat16 [8192, 2048], P(('rep', 'shard')), may hold values from -6 to 6
- ln1_gain: bfloat16 [2048], P('shard'), may hold values from 0.5 to 1.5
- ln1_bias: bfloat16 [2048], P('shard'), may hold values from -1.25 to 1.25
- w_qkv: bfloat16 [2048, 6144], P('shard'), may hold values from -0.125 to 0.125
- b_qkv: bfloat16 [6144], P('shard'), may hold values from -1.75 to 1.75
- w_out: bfloat16 [2048, 2048], P('shard'), may hold values from -0.5 to 0.5
- ln2_gain: bfloat16 [2048], P('shard'), may hold values from 0.5 to 1.5
- ln2_bias: bfloat16 [2048], P('shard'), may hold values from -1.25 to 1.25
- w_gate: bfloat16 [2048, 5632], P('shard'), may hold values from -0.125 to 0.125
- w_up: bfloat16 [2048, 5632], P('shard'), may hold values from -0.125 to 0.125
- w_down: bfloat16 [5632, 2048], P('shard'), may hold values from -0.078125 to 0.078125
Outputs:
- activations: bfloat16 [8192, 2048], P(('rep', 'shard'))
- d_tokens: float32 [8192, 2048], P(('rep', 'shard'))
- grad_ln1_gain: float32 [2048], P('shard')
- grad_ln1_bias: float32 [2048], P('shard')
- grad_w_qkv: float32 [2048, 6144], P('shard')
- grad_b_qkv: float32 [6144], P('shard')
- grad_w_out: float32 [2048, 2048], P('shard')
- grad_ln2_gain: float32 [2048], P('shard')
- grad_ln2_bias: float32 [2048], P('shard')
- grad_w_gate: float32 [2048, 5632], P('shard')
- grad_w_up: float32 [2048, 5632], P('shard')
- grad_w_down: float32 [5632, 2048], P('shard')
Inputs may be any that keep to these rules, and one draw needn't show every extreme that they name: `doc_ids`: within each device's 256 tokens the numbers start at 0 and rise by one at each new document; documents never cross devices; in every draw some device holds a single document of 256 tokens, and some device holds the largest number of documents.
All inputs are finite; a program needn't handle non-finite values.
Results may differ from a plain program's by a relative error of at most 0.014.
Values may be sent and summed in bfloat16 or wider, within the bound.
No kernel may reach another device: no remote copies, remote signals or barrier semaphores. Data moves between devices by JAX's collectives and lax.ppermute only.
A program may use at most 640 MiB of HBM per device.

v0:
```python
import jax
import jax.numpy as jnp
from jax import lax
from jax.sharding import PartitionSpec as P

D = 2048
FF = 5632
HEADS = 32
HEAD_DIM = 64
ROT = 16


def layer_norm(values, gain_vec, bias_vec):
    average = jnp.mean(values, -1, keepdims=True)
    centered = values - average
    recip_std = lax.rsqrt(jnp.mean(centered * centered, -1, keepdims=True) + 1e-05)
    unit_vals = centered * recip_std
    return (unit_vals * gain_vec + bias_vec, unit_vals, recip_std)


def norm_back(grad_in, unit_vals, recip_std, gain_vec):
    scaled = grad_in * gain_vec
    return recip_std * (
        scaled
        - jnp.mean(scaled, -1, keepdims=True)
        - unit_vals * jnp.mean(scaled * unit_vals, -1, keepdims=True)
    )


def rotate(values, cos_table, sin_table):
    half_rot = ROT // 2
    cos_heads = cos_table[:, None, :]
    sin_heads = sin_table[:, None, :]
    first_part = values[..., :half_rot]
    second = values[..., half_rot:ROT]
    return jnp.concatenate(
        [
            first_part * cos_heads - second * sin_heads,
            second * cos_heads + first_part * sin_heads,
            values[..., ROT:],
        ],
        -1,
    )


def contract_last(left, right):
    return lax.dot_general(
        left, right, (((1,), (1,)), ((), ())), preferred_element_type=jnp.float32
    )


def score_block(query_low, key_low, allowed):
    scores = (
        jnp.einsum("thd,shd->hts", query_low, key_low, preferred_element_type=jnp.float32) * 0.125
    )
    return jnp.where(allowed[None], scores, -1e30)


def per_device(
    tokens,
    doc_ids,
    cotangent,
    ln1_gain,
    ln1_bias,
    w_qkv,
    b_qkv,
    w_out,
    ln2_gain,
    ln2_bias,
    w_gate,
    w_up,
    w_down,
):
    length = tokens.shape[0]
    indices = jnp.arange(length, dtype=jnp.int32)
    same_doc = doc_ids[:, None] == doc_ids[None, :]
    first_row = jnp.min(jnp.where(same_doc, indices[None, :], length), axis=1)
    allowed = same_doc & (indices[None, :] <= indices[:, None])
    frequency = 10000.0 ** (-(jnp.arange(ROT // 2, dtype=jnp.float32) * 2.0 / ROT))
    angles = (indices - first_row).astype(jnp.float32)[:, None] * frequency
    cos_table = jnp.cos(angles)
    sin_table = jnp.sin(angles)
    gain_one, bias_one, full_qkv, full_bqkv, full_out = (
        lax.all_gather(ln1_gain, "shard", axis=0, tiled=True),
        lax.all_gather(ln1_bias, "shard", axis=0, tiled=True),
        lax.all_gather(w_qkv, "shard", axis=0, tiled=True),
        lax.all_gather(b_qkv, "shard", axis=0, tiled=True),
        lax.all_gather(w_out, "shard", axis=0, tiled=True),
    )
    gain_two, bias_two, full_gate, full_up, full_down = (
        lax.all_gather(ln2_gain, "shard", axis=0, tiled=True),
        lax.all_gather(ln2_bias, "shard", axis=0, tiled=True),
        lax.all_gather(w_gate, "shard", axis=0, tiled=True),
        lax.all_gather(w_up, "shard", axis=0, tiled=True),
        lax.all_gather(w_down, "shard", axis=0, tiled=True),
    )
    inputs = tokens.astype(jnp.float32)
    normed_one, unit_one, scale_one = layer_norm(
        inputs, gain_one.astype(jnp.float32), bias_one.astype(jnp.float32)
    )
    normed_low = normed_one.astype(jnp.bfloat16)
    projected = jnp.dot(
        normed_low, full_qkv, preferred_element_type=jnp.float32
    ) + full_bqkv.astype(jnp.float32)
    head_split = projected.reshape(length, 3, HEADS, HEAD_DIM)
    query_low = rotate(head_split[:, 0], cos_table, sin_table).astype(jnp.bfloat16)
    key_low = rotate(head_split[:, 1], cos_table, sin_table).astype(jnp.bfloat16)
    value_low = head_split[:, 2].astype(jnp.bfloat16)
    scores = score_block(query_low, key_low, allowed)
    highest = jnp.max(scores, -1, keepdims=True)
    exp_scores = jnp.exp(scores - highest)
    denominator = jnp.sum(exp_scores, -1, keepdims=True)
    attn_probs = exp_scores / denominator
    log_total = highest + jnp.log(denominator)
    attended_low = (
        jnp.einsum(
            "hts,shd->thd",
            attn_probs.astype(jnp.bfloat16),
            value_low,
            preferred_element_type=jnp.float32,
        )
        .reshape(length, D)
        .astype(jnp.bfloat16)
    )
    hidden = inputs + jnp.dot(attended_low, full_out, preferred_element_type=jnp.float32)
    normed_two, unit_two, scale_two = layer_norm(
        hidden, gain_two.astype(jnp.float32), bias_two.astype(jnp.float32)
    )
    two_low = normed_two.astype(jnp.bfloat16)
    gate_val = jnp.dot(two_low, full_gate, preferred_element_type=jnp.float32)
    up_val = jnp.dot(two_low, full_up, preferred_element_type=jnp.float32)
    sigmoid_gate = jax.nn.sigmoid(gate_val)
    silu_gate = gate_val * sigmoid_gate
    mixed_low = (silu_gate * up_val).astype(jnp.bfloat16)
    activations = (
        hidden + jnp.dot(mixed_low, full_down, preferred_element_type=jnp.float32)
    ).astype(jnp.bfloat16)
    (
        gain_one,
        bias_one,
        full_qkv,
        full_bqkv,
        full_out,
        gain_two,
        bias_two,
        full_gate,
        full_up,
        full_down,
    ) = (
        lax.all_gather(ln1_gain, "shard", axis=0, tiled=True),
        lax.all_gather(ln1_bias, "shard", axis=0, tiled=True),
        lax.all_gather(w_qkv, "shard", axis=0, tiled=True),
        lax.all_gather(b_qkv, "shard", axis=0, tiled=True),
        lax.all_gather(w_out, "shard", axis=0, tiled=True),
        lax.all_gather(ln2_gain, "shard", axis=0, tiled=True),
        lax.all_gather(ln2_bias, "shard", axis=0, tiled=True),
        lax.all_gather(w_gate, "shard", axis=0, tiled=True),
        lax.all_gather(w_up, "shard", axis=0, tiled=True),
        lax.all_gather(w_down, "shard", axis=0, tiled=True),
    )
    grad_mixed = contract_last(cotangent, full_down)
    dgate_low = (
        grad_mixed * up_val * sigmoid_gate * (1.0 + gate_val * (1.0 - sigmoid_gate))
    ).astype(jnp.bfloat16)
    dup_low = (grad_mixed * silu_gate).astype(jnp.bfloat16)
    grad_norm_two = contract_last(dgate_low, full_gate) + contract_last(dup_low, full_up)
    grad_gain_two = jnp.sum(grad_norm_two * unit_two, 0)
    grad_bias_two = jnp.sum(grad_norm_two, 0)
    grad_hidden = cotangent.astype(jnp.float32) + norm_back(
        grad_norm_two, unit_two, scale_two, gain_two.astype(jnp.float32)
    )
    hidden_low = grad_hidden.astype(jnp.bfloat16)
    datt_low = (
        contract_last(hidden_low, full_out).reshape(length, HEADS, HEAD_DIM).astype(jnp.bfloat16)
    )
    attn_probs = jnp.exp(score_block(query_low, key_low, allowed) - log_total)
    grad_value = jnp.einsum(
        "hts,thd->shd",
        attn_probs.astype(jnp.bfloat16),
        datt_low,
        preferred_element_type=jnp.float32,
    )
    grad_probs = jnp.einsum("thd,shd->hts", datt_low, value_low, preferred_element_type=jnp.float32)
    inner_sum = jnp.sum(attn_probs * grad_probs, -1, keepdims=True)
    grad_scores_low = (0.125 * attn_probs * (grad_probs - inner_sum)).astype(jnp.bfloat16)
    grad_query = jnp.einsum(
        "hts,shd->thd", grad_scores_low, key_low, preferred_element_type=jnp.float32
    )
    grad_key = jnp.einsum(
        "hts,thd->shd", grad_scores_low, query_low, preferred_element_type=jnp.float32
    )
    grad_query = rotate(grad_query, cos_table, -sin_table)
    grad_key = rotate(grad_key, cos_table, -sin_table)
    grad_proj_low = jnp.concatenate(
        [grad_query.reshape(length, D), grad_key.reshape(length, D), grad_value.reshape(length, D)],
        1,
    ).astype(jnp.bfloat16)
    grad_bqkv = jnp.sum(grad_proj_low, 0, dtype=jnp.float32)
    grad_norm_one = contract_last(grad_proj_low, full_qkv)
    grad_gain_one = jnp.sum(grad_norm_one * unit_one, 0)
    grad_bias_one = jnp.sum(grad_norm_one, 0)
    d_tokens = grad_hidden + norm_back(
        grad_norm_one, unit_one, scale_one, gain_one.astype(jnp.float32)
    )
    owned_down = lax.psum_scatter(
        jnp.einsum("tf,td->fd", mixed_low, cotangent, preferred_element_type=jnp.float32),
        "shard",
        scatter_dimension=0,
        tiled=True,
    )
    qkv_part = jnp.einsum(
        "tr,tc->rc", normed_low, grad_proj_low, preferred_element_type=jnp.float32
    )
    out_part = jnp.einsum("tr,tc->rc", attended_low, hidden_low, preferred_element_type=jnp.float32)
    gate_part = jnp.einsum("tr,tc->rc", two_low, dgate_low, preferred_element_type=jnp.float32)
    up_part = jnp.einsum("tr,tc->rc", two_low, dup_low, preferred_element_type=jnp.float32)
    owned_rows = lax.psum_scatter(
        jnp.concatenate([qkv_part, out_part, gate_part, up_part], 1),
        "shard",
        scatter_dimension=0,
        tiled=True,
    )
    owned_gain_two, owned_bias_two, owned_gain_one, owned_bias_one, owned_bqkv = (
        lax.psum_scatter(grad_gain_two, "shard", scatter_dimension=0, tiled=True),
        lax.psum_scatter(grad_bias_two, "shard", scatter_dimension=0, tiled=True),
        lax.psum_scatter(grad_gain_one, "shard", scatter_dimension=0, tiled=True),
        lax.psum_scatter(grad_bias_one, "shard", scatter_dimension=0, tiled=True),
        lax.psum_scatter(grad_bqkv, "shard", scatter_dimension=0, tiled=True),
    )
    owned_qkv = owned_rows[:, : 3 * D]
    owned_out = owned_rows[:, 3 * D : 4 * D]
    owned_gate = owned_rows[:, 4 * D : 4 * D + FF]
    owned_up = owned_rows[:, 4 * D + FF :]
    summed = (
        lax.psum(owned_gain_one.astype(jnp.bfloat16), "rep").astype(jnp.float32),
        lax.psum(owned_bias_one.astype(jnp.bfloat16), "rep").astype(jnp.float32),
        lax.psum(owned_qkv.astype(jnp.bfloat16), "rep").astype(jnp.float32),
        lax.psum(owned_bqkv.astype(jnp.bfloat16), "rep").astype(jnp.float32),
        lax.psum(owned_out.astype(jnp.bfloat16), "rep").astype(jnp.float32),
        lax.psum(owned_gain_two.astype(jnp.bfloat16), "rep").astype(jnp.float32),
        lax.psum(owned_bias_two.astype(jnp.bfloat16), "rep").astype(jnp.float32),
        lax.psum(owned_gate.astype(jnp.bfloat16), "rep").astype(jnp.float32),
        lax.psum(owned_up.astype(jnp.bfloat16), "rep").astype(jnp.float32),
        lax.psum(owned_down.astype(jnp.bfloat16), "rep").astype(jnp.float32),
    )
    return (
        activations,
        d_tokens,
        summed[0],
        summed[1],
        summed[2],
        summed[3],
        summed[4],
        summed[5],
        summed[6],
        summed[7],
        summed[8],
        summed[9],
    )


def solution(mesh):
    return jax.shard_map(
        per_device,
        mesh=mesh,
        in_specs=(
            P(("rep", "shard"), None),
            P(("rep", "shard")),
            P(("rep", "shard"), None),
            P("shard"),
            P("shard"),
            P("shard", None),
            P("shard"),
            P("shard", None),
            P("shard"),
            P("shard"),
            P("shard", None),
            P("shard", None),
            P("shard", None),
        ),
        out_specs=(
            P(("rep", "shard"), None),
            P(("rep", "shard"), None),
            P("shard"),
            P("shard"),
            P("shard", None),
            P("shard"),
            P("shard", None),
            P("shard"),
            P("shard"),
            P("shard", None),
            P("shard", None),
            P("shard", None),
        ),
        check_vma=False,
    )
```

profile of v0, /device:TPU:0, one launch (start us, length us, event | category | flops | bytes accessed | tf_op | source)
XLA Modules:
  0.0 2667.8 jit_solution(14075284288583610899)
XLA Ops:
  10.7 23.0 all-gather
  33.8 17.3 all-gather.1
  51.1 18.7 all-gather.3
  69.9 17.3 all-gather.4
  87.2 19.3 all-gather.2
  108.2 33.0 %all-gather.11.cloned.1.call-done = bf16[2048,6144]{1,0:T(8,128)(2,1)} async-done(((bf16[128,6144]{1,0:T(8,128)(2,1)}), bf16[2048,6144]{1,0:T(8,128)(2,1)}) %all-gather.11.cloned.1.call-update) | async-done | bytes 25165840 | tf_op jit(solution)/shard_map/all_gather | solution.py:86
  141.2 13.4 convolution_add_fusion
  154.7 6.6 copy.42
  161.2 2.5 slice_bitcast_fusion.1
  168.9 5.0 fusion.23
  174.0 44.6 %all-gather.13.cloned.1.call-done = bf16[2048,2048]{1,0:T(8,128)(2,1)} async-done(((bf16[128,2048]{1,0:T(8,128)(2,1)}), bf16[2048,2048]{1,0:T(8,128)(2,1)}) %all-gather.13.cloned.1.call-update) | async-done | bytes 8388624 | tf_op jit(solution)/shard_map/all_gather | solution.py:88
  218.6 6.1 fusion.49
  225.6 111.6 %all-gather.17.cloned.1.call-done = bf16[2048,5632]{1,0:T(8,128)(2,1)} async-done(((bf16[128,5632]{1,0:T(8,128)(2,1)}), bf16[2048,5632]{1,0:T(8,128)(2,1)}) %all-gather.17.cloned.1.call-update) | async-done | bytes 23068688 | tf_op jit(solution)/shard_map/all_gather | solution.py:94
  337.2 13.4 fusion.51
  350.6 106.7 %all-gather.15.cloned.1.call-done = bf16[2048,5632]{1,0:T(8,128)(2,1)} async-done(((bf16[128,5632]{1,0:T(8,128)(2,1)}), bf16[2048,5632]{1,0:T(8,128)(2,1)}) %all-gather.15.cloned.1.call-update) | async-done | bytes 23068688 | tf_op jit(solution)/shard_map/all_gather | solution.py:93
  457.3 13.2 fusion.50
  470.5 107.0 %all-gather.19.cloned.1.call-done = bf16[5632,2048]{1,0:T(8,128)(2,1)} async-done(((bf16[352,2048]{1,0:T(8,128)(2,1)}), bf16[5632,2048]{1,0:T(8,128)(2,1)}) %all-gather.19.cloned.1.call-update) | async-done | bytes 23068688 | tf_op jit(solution)/shard_map/all_gather | solution.py:95
  577.5 17.5 multiply_convert_fusion.1
  596.6 19.0 fusion.55
  615.6 15.6 fusion.52
  631.2 20.7 multiply_reduce_fusion.1
  651.9 3.6 multiply_add_fusion
  656.8 7.8 convolution_convert_fusion
  665.2 8.2 multiply_reduce_fusion
  674.8 3.0 multiply_convert_fusion
  680.8 2.0 fusion.24
  683.9 8.2 fusion.28
  692.2 20.0 fusion.54
  712.2 20.8 fusion.53
  733.1 19.9 fusion.44
  753.0 105.7 %pad_maximum_fusion = f32[2048,19456]{1,0:T(8,128)} fusion(f32[2048,5632]{1,0:T(8,128)} %fusion.54, f32[2048,5632]{1,0:T(8,128)} %fusion.53, f32[2048,2048]{1,0:T(8,128)} %fusion.28, f32[2048,6144]{1,0:T(8,128)} %fusion.44), kind=kLoop, calls=%fused_computation | loop fusion | flops 119537664 | bytes 318767104 | tf_op jit(solution)/shard_map/concatenate | solution.py:218
  858.8 190.0 %reduce-scatter.5.cloned.1.call-done = f32[352,2048]{1,0:T(8,128)} async-done(((f32[5632,2048]{1,0:T(8,128)}), f32[352,2048]{1,0:T(8,128)}) %reduce-scatter.5.cloned.1.call-update) | async-done | bytes 2883600 | tf_op jit(solution)/shard_map/reduce_scatter | solution.py:205
  1048.8 3.2 convert_element_type.176
  1052.0 1432.1 %reduce-scatter.3.cloned.1.call-done = f32[128,19456]{1,0:T(8,128)} async-done(((f32[2048,19456]{1,0:T(8,128)}), f32[128,19456]{1,0:T(8,128)}) %reduce-scatter.3.cloned.1.call-update) | async-done | bytes 9961488 | tf_op jit(solution)/shard_map/reduce_scatter | solution.py:217
  2484.1 4.4 convert.72
  2490.6 1.8 fusion.48
  2495.0 2.2 convert_reduce_fusion
  2497.2 14.1 fusion.21
  2511.3 59.6 %all-reduce.5 = (bf16[2048]{0:T(1024)(128)(2,1)S(1)}, bf16[2048]{0:T(1024)(128)(2,1)S(1)}, bf16[6144]{0:T(1024)(128)(2,1)S(1)}, bf16[2048]{0:T(1024)(128)(2,1)S(1)}, bf16[2048]{0:T(1024)(128)(2,1)S(1)}) all-reduce(f32[2048]{0:T(1024)S(1)} %get-tuple-element.14, ...), channel_id=2, replica_groups=mesh['rep'=2,'shard'=16] {'shard'}, use_global_device_ids=true, to_apply=%region_13.14.clone | all-reduce | flops 14336 | bytes 86016
  2571.2 4.9 all-reduce.6
  2578.8 4.0 fusion.20
  2582.8 12.5 fusion.8
  2595.3 53.9 %all-reduce.10.cloned.1.call-done = (bf16[128,6144]{1,0:T(8,128)(2,1)}, bf16[128,2048]{1,0:T(8,128)(2,1)}, bf16[128,5632]{1,0:T(8,128)(2,1)}, bf16[128,5632]{1,0:T(8,128)(2,1)}, bf16[352,2048]{1,0:T(8,128)(2,1)}) async-done(((bf16[128,6144]{1,0:T(8,128)(2,1)}, bf16[128,2048]{1,0:T(8,128)(2,1)}, bf16[128,5632]{1,0:T(8,128)(2,1)}, bf16[128,5632]{1,0:T(8,128)(2,1)}, bf16[352,2048]{1,0:T(8,128)(2,1)}), ...) | async-done | bytes 6422544 | tf_op jit(solution)/shard_map/psum | solution.py:237
  2649.2 2.2 convert_element_type.169
  2651.5 3.4 convert_element_type.165
  2654.9 1.9 convert_element_type.174
  2656.7 1.9 convert_element_type.175
  2658.6 1.9 convert_element_type.177
  (174 shorter events, 26.2 us)
Async XLA Ops:
  7.2 3.5 copy-start.46
  7.2 3.5 copy-start.47
  7.2 26.6 copy-start.48
  7.2 43.9 %copy-start.49 = (bf16[128]{0:T(256)(128)(2,1)S(1)}, bf16[128]{0:T(256)(128)(2,1)}, u32[]{:S(2)}) copy-start(bf16[128]{0:T(256)(128)(2,1)} %param.21) | copy-start | bytes 772
  7.2 62.7 %copy-start.50 = (bf16[128]{0:T(256)(128)(2,1)S(1)}, bf16[128]{0:T(256)(128)(2,1)}, u32[]{:S(2)}) copy-start(bf16[128]{0:T(256)(128)(2,1)} %param.22) | copy-start | bytes 772
  7.2 134.0 %all-gather.11.cloned.1.call-start = ((), (), s32[]{:S(2)}) async-start(), calls=%async_computation.2 | async-start | bytes 26738688 | tf_op jit(solution)/shard_map/all_gather | solution.py:86
  8.0 98.6 %copy-start.43 = (s32[256]{0:T(256)S(1)}, s32[256]{0:T(256)}, u32[]{:S(2)}) copy-start(s32[256]{0:T(256)} %param.14) | copy-start | bytes 3076
  8.0 98.7 %copy-start.3 = (bf16[256,2048]{1,0:T(8,128)(2,1)S(1)}, bf16[256,2048]{1,0:T(8,128)(2,1)}, u32[]{:S(2)}) copy-start(bf16[256,2048]{1,0:T(8,128)(2,1)} %param.13) | copy-start | bytes 3145732
  8.0 210.6 %all-gather.13.cloned.1.call-start = ((), (), s32[]{:S(2)}) async-start(), calls=%async_computation.3 | async-start | bytes 8912896 | tf_op jit(solution)/shard_map/all_gather | solution.py:88
  8.7 328.4 %all-gather.17.cloned.1.call-start = ((), (), s32[]{:S(2)}) async-start(), calls=%async_computation.5 | async-start | bytes 24510464 | tf_op jit(solution)/shard_map/all_gather | solution.py:94
  9.5 447.9 %all-gather.15.cloned.1.call-start = ((), (), s32[]{:S(2)}) async-start(), calls=%async_computation.4 | async-start | bytes 24510464 | tf_op jit(solution)/shard_map/all_gather | solution.py:93
  10.0 567.5 %all-gather.19.cloned.1.call-start = ((), (), s32[]{:S(2)}) async-start(), calls=%async_computation.6 | async-start | bytes 24510464 | tf_op jit(solution)/shard_map/all_gather | solution.py:95
  10.6 1038.2 %reduce-scatter.5.cloned.1.call-start = ((), (), s32[]{:S(2)}) async-start(), calls=%async_computation.8 | async-start | bytes 49020928 | tf_op jit(solution)/shard_map/reduce_scatter | solution.py:205
  33.7 120.9 %copy-start.24 = (f32[16,1,128]{2,1,0:T(1,128)}, f32[16,1,128]{2,1,0:T(1,128)S(1)}, u32[]{:S(2)}) copy-start(f32[16,1,128]{2,1,0:T(1,128)S(1)} %convert_element_type.178) | copy-start | bytes 24580
  51.1 103.6 %copy-start.26 = (f32[16,1,128]{2,1,0:T(1,128)}, f32[16,1,128]{2,1,0:T(1,128)S(1)}, u32[]{:S(2)}) copy-start(f32[16,1,128]{2,1,0:T(1,128)S(1)} %convert_element_type.179) | copy-start | bytes 24580
  106.9 47.7 %copy-start.36 = (f32[256]{0:T(256)}, f32[256]{0:T(256)S(1)}, u32[]{:S(2)}) copy-start(f32[256]{0:T(256)S(1)} %broadcast_multiply_fusion.5) | copy-start | bytes 3076
  107.4 47.3 %copy-start.38 = (f32[256]{0:T(256)}, f32[256]{0:T(256)S(1)}, u32[]{:S(2)}) copy-start(f32[256]{0:T(256)S(1)} %add_rsqrt_fusion.1) | copy-start | bytes 3076
  108.1 55.9 %copy-start.40 = (f32[256,8]{0,1:T(8,128)}, f32[256,8]{0,1:T(8,128)S(1)}, u32[]{:S(2)}) copy-start(f32[256,8]{0,1:T(8,128)S(1)} %get-tuple-element.56) | copy-start | bytes 24580
  165.7 3.2 copy-start
  224.7 427.2 %copy-start.1 = (f32[256,2048]{1,0:T(8,128)}, f32[256,2048]{1,0:T(8,128)S(1)}, u32[]{:S(2)}) copy-start(f32[256,2048]{1,0:T(8,128)S(1)} %get-tuple-element.60) | copy-start | bytes 6291460
  615.6 1868.5 %reduce-scatter.3.cloned.1.call-start = ((), (), s32[]{:S(2)}) async-start(), calls=%async_computation.7 | async-start | bytes 169345024 | tf_op jit(solution)/shard_map/reduce_scatter | solution.py:217
  665.2 8.2 slice-start
  665.2 9.6 slice-start.1
  674.8 3.0 copy-start.20
  674.8 3.0 copy-start.33
  674.8 3.0 copy-start.35
  680.6 1814.3 %copy-start.8 = (bf16[256,32,64]{0,2,1:T(8,128)(2,1)}, bf16[256,32,64]{0,2,1:T(8,128)(2,1)S(1)}, u32[]{:S(2)}) copy-start(bf16[256,32,64]{0,2,1:T(8,128)(2,1)S(1)} %pad_maximum_fusion.4) | copy-start | bytes 3145732
  680.7 52.3 %copy-start.9 = (bf16[256,32,64]{0,2,1:T(8,128)(2,1)}, bf16[256,32,64]{0,2,1:T(8,128)(2,1)S(1)}, u32[]{:S(2)}) copy-start(bf16[256,32,64]{0,2,1:T(8,128)(2,1)S(1)} %pad_maximum_fusion.5) | copy-start | bytes 3145732
  680.8 2.6 copy-start.6
  680.8 3.2 copy-start.12
  683.9 49.1 %copy-start.15 = (bf16[32,64,256]{2,1,0:T(8,128)(2,1)}, bf16[32,64,256]{2,1,0:T(8,128)(2,1)S(1)}, u32[]{:S(2)}) copy-start(bf16[32,64,256]{2,1,0:T(8,128)(2,1)S(1)} %fusion.24) | copy-start | bytes 3145732
  712.1 20.9 copy-start.4
  712.1 20.9 copy-start.25
  712.1 20.9 copy-start.27
  712.1 20.9 copy-start.37
  712.2 20.9 copy-start.39
  858.7 1790.5 %all-reduce.10.cloned.1.call-start = ((), (), s32[]{:S(2)}) async-start(), calls=%async_computation.9 | async-start | bytes 12845056 | tf_op jit(solution)/shard_map/psum | solution.py:237
  2492.4 2.5 copy-start.10
  2495.0 2.2 copy-start.11
  2495.0 2.2 copy-start.16
  2497.2 14.1 copy-start.44
  2497.2 14.1 copy-start.45
  2497.2 81.6 %copy-start.7 = (f32[256,2048]{1,0:T(8,128)S(1)}, f32[256,2048]{1,0:T(8,128)}, u32[]{:S(2)}) copy-start(f32[256,2048]{1,0:T(8,128)} %copy-done.5) | copy-start | bytes 6291460
  2578.8 4.0 copy-start.2
  2578.8 4.0 copy-start.14
  2649.2 5.6 copy-start.23
  2654.9 1.9 copy-start.22
  2656.7 1.9 copy-start.21
  (14 other events, 19.7 us)
Sparse Core Ops, SparseCore 0:
  9.7 131.5 all-gather.10
  143.4 75.1 all-gather.12
  220.2 116.9 all-gather.16
  338.6 118.6 all-gather.14
  458.8 118.6 all-gather.18
  615.7 433.0 reduce-scatter.4
  1053.1 1430.9 reduce-scatter.2
  2492.6 156.6 all-reduce.9
where the time goes:
time: 2680 us; the launch traced here: 2670 us
  waiting for transfers between devices  2080 us (78%)
  matrix products  241 us (9%)
  blocking collectives  160 us (6%)
  other arithmetic  145 us (5%)
    reduce_scatter x1, waiting for transfers between devices, per_device(): lax.psum_scatter(jnp.concatenate([qkv_part, out_part, gate_part, up_part]...  1430 us
    reduce_scatter x1, waiting for transfers between devices, per_device(): lax.psum_scatter(jnp.einsum('tf,td->fd', mixed_low, cotangent, preferred_...  190 us
    all_gather x1, waiting for transfers between devices, per_device(): lax.all_gather(w_up, 'shard', axis=0, tiled=True)  112 us
    all_gather x1, waiting for transfers between devices, per_device(): lax.all_gather(w_down, 'shard', axis=0, tiled=True)  107 us
    all_gather x1, waiting for transfers between devices, per_device(): lax.all_gather(w_gate, 'shard', axis=0, tiled=True)  107 us
    concatenate x1, other arithmetic, per_device(): jnp.concatenate([qkv_part, out_part, gate_part, up_part], 1)  106 us
    dot_general x5, matrix products, contract_last(): lax.dot_general(left, right, (((1,), (1,)), ((), ())), preferred_element_...  75.6 us
    unnamed x1, blocking collectives  59.6 us
  transfers between devices with their start and end apart: 8, of which 8 were waited for; matrix products, arithmetic and copies ran while one was open for 13% of the time, Pallas kernels for 0%

commit v1 on v0

v1 whole, which is shorter than its diff:
```python
import jax
import jax.numpy as jnp
from jax import lax
from jax.sharding import Mesh, PartitionSpec as P

HEAD_DIM = 64
ROT = 16
PLANE = ("x", "y", "c")
EVERY = ("x", "z", "y", "c")
SIBLING = (1, 1)
FIRST = (4, 2)
SECOND = (2, 4)
ACROSS_X = (4, 4)
ACROSS_Y = (2, 2)
ACROSS_YC = (3, 3)


def swap(values, masks):
    pairs = [(i, i ^ masks[i & 1]) for i in range(8)]
    return lax.ppermute(values, PLANE, pairs)


def plane_gather(values):
    near = swap(values, FIRST)
    side = swap(values, SECOND)
    far = swap(near, SECOND)
    own = [values, near, side, far]
    return own + [swap(part, SIBLING) for part in own]


def plane_sum(own, other):
    merged = [
        mine.astype(jnp.float32) + swap(theirs, SIBLING).astype(jnp.float32)
        for mine, theirs in zip(own, other)
    ]
    far = swap(merged[3].astype(jnp.bfloat16), SECOND)
    side = swap(merged[2].astype(jnp.bfloat16), SECOND)
    near = swap((merged[1] + far.astype(jnp.float32)).astype(jnp.bfloat16), FIRST)
    return merged[0] + side.astype(jnp.float32) + near.astype(jnp.float32)


def by_owner(parts, y_index, c_index):
    first, second, third, fourth = parts
    odd = c_index == 1
    first, second = jnp.where(odd, second, first), jnp.where(odd, first, second)
    third, fourth = jnp.where(odd, fourth, third), jnp.where(odd, third, fourth)
    upper = y_index == 1
    return [
        jnp.where(upper, third, first),
        jnp.where(upper, fourth, second),
        jnp.where(upper, first, third),
        jnp.where(upper, second, fourth),
    ]


def exchange(blocks, y_index, c_index):
    mine = by_owner(blocks, y_index, c_index)
    moved = [
        mine[0],
        swap(mine[1], SIBLING),
        swap(mine[2], ACROSS_Y),
        swap(mine[3], ACROSS_YC),
    ]
    return by_owner(moved, y_index, c_index)


def layer_norm(values, gain_vec, bias_vec):
    average = jnp.mean(values, -1, keepdims=True)
    centered = values - average
    recip_std = lax.rsqrt(jnp.mean(centered * centered, -1, keepdims=True) + 1e-05)
    unit_vals = centered * recip_std
    return (unit_vals * gain_vec + bias_vec, unit_vals, recip_std)


def norm_back(grad_in, unit_vals, recip_std, gain_vec):
    scaled = grad_in * gain_vec
    return recip_std * (
        scaled
        - jnp.mean(scaled, -1, keepdims=True)
        - unit_vals * jnp.mean(scaled * unit_vals, -1, keepdims=True)
    )


def rotate(values, cos_table, sin_table):
    half_rot = ROT // 2
    cos_heads = cos_table[:, :, None, :]
    sin_heads = sin_table[:, :, None, :]
    first_part = values[..., :half_rot]
    second = values[..., half_rot:ROT]
    return jnp.concatenate(
        [
            first_part * cos_heads - second * sin_heads,
            second * cos_heads + first_part * sin_heads,
            values[..., ROT:],
        ],
        -1,
    )


def dot(left, right):
    return jnp.dot(left, right, preferred_element_type=jnp.float32)


def contract_last(left, right):
    return lax.dot_general(
        left, right, (((1,), (1,)), ((), ())), preferred_element_type=jnp.float32
    )


def contract_first(left, right):
    return lax.dot_general(
        left, right, (((0,), (0,)), ((), ())), preferred_element_type=jnp.float32
    )


def einsum(spec, left, right):
    return jnp.einsum(spec, left, right, preferred_element_type=jnp.float32)


def gather_z(values):
    return lax.all_gather(values, "z", axis=0, tiled=True)


def scatter_z(values):
    return lax.psum_scatter(values, "z", scatter_dimension=0, tiled=True)


def per_device(
    tokens,
    doc_ids,
    cotangent,
    ln1_gain,
    ln1_bias,
    w_qkv,
    b_qkv,
    w_out,
    ln2_gain,
    ln2_bias,
    w_gate,
    w_up,
    w_down,
):
    x_index, z_index = lax.axis_index("x"), lax.axis_index("z")
    y_index, c_index = lax.axis_index("y"), lax.axis_index("c")
    yc_index = 2 * y_index + c_index
    planes = lax.axis_size("z")
    shards = 4 * planes
    rows = w_qkv.shape[0]
    width = rows * shards
    hidden_dim = w_gate.shape[1]
    piece = hidden_dim // (2 * shards)
    mlp = piece * planes
    head_cols = width // 8
    spread = rows % (2 * HEAD_DIM) == 0
    groups = planes if spread else 1
    unit = head_cols // groups
    length = tokens.shape[0]

    def pick_x(values, axis):
        return lax.dynamic_index_in_dim(values, x_index, axis, keepdims=False)

    def pick_yc(values, axis):
        return lax.dynamic_index_in_dim(values, yc_index, axis, keepdims=False)

    def columns(weight, outer, size):
        view = pick_x(weight.reshape(rows, outer, 4, 2, size), 3)
        blocks = [view[:, :, t].reshape(rows, outer * size) for t in range(4)]
        return jnp.concatenate(exchange(blocks, y_index, c_index), 0)

    full_qkv = gather_z(columns(w_qkv, 3 * groups, unit))
    if spread:
        full_out = gather_z(pick_x(w_out.reshape(2, rows // 2, width), 0))
    else:
        full_out = lax.all_gather(w_out, ("z", "y", "c"), axis=0, tiled=True)
        full_out = pick_x(pick_yc(full_out.reshape(4, 2, unit, width), 0), 0)
    full_gate = gather_z(columns(w_gate, planes, piece))
    full_up = gather_z(columns(w_up, planes, piece))
    full_down = gather_z(pick_x(w_down.reshape(2, piece, width), 0))

    vectors = lax.all_gather(
        jnp.concatenate([ln1_gain, ln1_bias, ln2_gain, ln2_bias, b_qkv]),
        ("z", "y", "c"),
        axis=0,
    ).astype(jnp.float32)
    gain_one, bias_one, gain_two, bias_two = (
        vectors[:, i * rows : (i + 1) * rows].reshape(width) for i in range(4)
    )
    bias_qkv = vectors[:, 4 * rows :].reshape(3 * groups, 4, 2, unit)
    bias_qkv = pick_x(pick_yc(bias_qkv, 1), 1).reshape(3 * head_cols)

    docs = jnp.stack(plane_gather(doc_ids))
    all_tokens = jnp.concatenate(plane_gather(tokens), 0)
    all_cot = jnp.concatenate(plane_gather(cotangent), 0)

    indices = jnp.arange(length, dtype=jnp.int32)
    same_doc = docs[:, :, None] == docs[:, None, :]
    first_row = jnp.min(jnp.where(same_doc, indices[None, None, :], length), axis=2)
    allowed = same_doc & (indices[None, None, :] <= indices[None, :, None])
    frequency = 10000.0 ** (-(jnp.arange(ROT // 2, dtype=jnp.float32) * 2.0 / ROT))
    angles = (indices[None] - first_row).astype(jnp.float32)[:, :, None] * frequency
    cos_table = jnp.cos(angles)
    sin_table = jnp.sin(angles)

    def score_block(query_low, key_low):
        scores = einsum("bthd,bshd->bhts", query_low, key_low) * 0.125
        return jnp.where(allowed[:, None], scores, -1e30)

    def halves(values):
        blocks = values.astype(jnp.bfloat16).reshape(8, length, width)
        return [blocks[i] for i in range(4)], [blocks[i] for i in range(4, 8)]

    normed_one, unit_one, _ = layer_norm(all_tokens.astype(jnp.float32), gain_one, bias_one)
    normed_low = normed_one.astype(jnp.bfloat16)
    projected = dot(normed_low, full_qkv) + bias_qkv
    head_split = projected.reshape(8, length, 3, head_cols // HEAD_DIM, HEAD_DIM)
    query_low = rotate(head_split[:, :, 0], cos_table, sin_table).astype(jnp.bfloat16)
    key_low = rotate(head_split[:, :, 1], cos_table, sin_table).astype(jnp.bfloat16)
    value_low = head_split[:, :, 2].astype(jnp.bfloat16)
    scores = score_block(query_low, key_low)
    highest = jnp.max(scores, -1, keepdims=True)
    exp_scores = jnp.exp(scores - highest)
    denominator = jnp.sum(exp_scores, -1, keepdims=True)
    attn_probs = exp_scores / denominator
    attended_low = (
        einsum("bhts,bshd->bthd", attn_probs.astype(jnp.bfloat16), value_low)
        .reshape(8 * length, head_cols)
        .astype(jnp.bfloat16)
    )
    inputs = tokens.astype(jnp.float32)
    hidden = inputs + plane_sum(*halves(dot(attended_low, full_out)))
    normed_two, unit_two, scale_two = layer_norm(hidden, gain_two, bias_two)
    two_low = jnp.concatenate(plane_gather(normed_two.astype(jnp.bfloat16)), 0)
    gate_val = dot(two_low, full_gate)
    up_val = dot(two_low, full_up)
    sigmoid_gate = jax.nn.sigmoid(gate_val)
    silu_gate = gate_val * sigmoid_gate
    mixed_low = (silu_gate * up_val).astype(jnp.bfloat16)
    down_sum = scatter_z(contract_first(mixed_low, all_cot).astype(jnp.bfloat16))
    grad_mixed = contract_last(all_cot, full_down)
    dgate_low = (
        grad_mixed * up_val * sigmoid_gate * (1.0 + gate_val * (1.0 - sigmoid_gate))
    ).astype(jnp.bfloat16)
    dup_low = (grad_mixed * silu_gate).astype(jnp.bfloat16)
    gate_sum = scatter_z(contract_first(two_low, dgate_low).astype(jnp.bfloat16))
    up_sum = scatter_z(contract_first(two_low, dup_low).astype(jnp.bfloat16))
    grad_norm_two = plane_sum(
        *halves(contract_last(dgate_low, full_gate) + contract_last(dup_low, full_up))
    )
    activations = (hidden + plane_sum(*halves(dot(mixed_low, full_down)))).astype(jnp.bfloat16)
    grad_gain_two = jnp.sum(grad_norm_two * unit_two, 0)
    grad_bias_two = jnp.sum(grad_norm_two, 0)
    grad_hidden = cotangent.astype(jnp.float32) + norm_back(
        grad_norm_two, unit_two, scale_two, gain_two
    )
    hidden_low = jnp.concatenate(plane_gather(grad_hidden.astype(jnp.bfloat16)), 0)
    out_part = contract_first(attended_low, hidden_low).astype(jnp.bfloat16)
    datt_low = (
        contract_last(hidden_low, full_out)
        .reshape(8, length, head_cols // HEAD_DIM, HEAD_DIM)
        .astype(jnp.bfloat16)
    )
    grad_value = einsum("bhts,bthd->bshd", attn_probs.astype(jnp.bfloat16), datt_low)
    grad_probs = einsum("bthd,bshd->bhts", datt_low, value_low)
    inner_sum = jnp.sum(attn_probs * grad_probs, -1, keepdims=True)
    grad_scores_low = (0.125 * attn_probs * (grad_probs - inner_sum)).astype(jnp.bfloat16)
    grad_query = einsum("bhts,bshd->bthd", grad_scores_low, key_low)
    grad_key = einsum("bhts,bthd->bshd", grad_scores_low, query_low)
    grad_query = rotate(grad_query, cos_table, -sin_table)
    grad_key = rotate(grad_key, cos_table, -sin_table)
    grad_proj_low = jnp.concatenate(
        [g.reshape(8 * length, head_cols) for g in (grad_query, grad_key, grad_value)], 1
    ).astype(jnp.bfloat16)
    qkv_sum = scatter_z(contract_first(normed_low, grad_proj_low).astype(jnp.bfloat16))
    grad_bqkv = jnp.sum(grad_proj_low, 0, dtype=jnp.float32)
    placed = lax.dynamic_update_slice(
        jnp.zeros((3 * groups, 4, 2, unit), jnp.float32),
        grad_bqkv.reshape(3 * groups, 1, 1, unit),
        (0, yc_index, x_index, 0),
    )
    own, other = halves(contract_last(grad_proj_low, full_qkv))
    grad_norm_one = plane_sum(own, other)
    _, unit_one, scale_one = layer_norm(inputs, gain_one, bias_one)
    grad_gain_one = jnp.sum(grad_norm_one * unit_one, 0)
    grad_bias_one = jnp.sum(grad_norm_one, 0)
    d_tokens = grad_hidden + norm_back(grad_norm_one, unit_one, scale_one, gain_one)

    sums = lax.psum(
        jnp.concatenate(
            [
                grad_gain_one,
                grad_bias_one,
                grad_gain_two,
                grad_bias_two,
                placed.reshape(3 * width),
            ]
        ),
        EVERY,
    )
    shard_index = 4 * z_index + yc_index
    small = [
        lax.dynamic_slice_in_dim(sums[i * width : (i + 1) * width], shard_index * rows, rows)
        for i in range(4)
    ]
    owned_bqkv = lax.dynamic_slice_in_dim(sums[4 * width :], shard_index * 3 * rows, 3 * rows)

    def whole_rows(half):
        other = swap(half, ACROSS_X)
        odd = x_index == 1
        return jnp.concatenate(
            [jnp.where(odd, other, half), jnp.where(odd, half, other)], 0
        ).astype(jnp.float32)

    if spread:
        owned_out = whole_rows(scatter_z(out_part))
    else:
        placed_out = lax.dynamic_update_slice(
            jnp.zeros((4, 2, unit, width), jnp.bfloat16),
            out_part[None, None],
            (yc_index, x_index, 0, 0),
        )
        owned_out = lax.psum_scatter(
            placed_out.reshape(width, width), ("z", "y", "c"), scatter_dimension=0, tiled=True
        )
        owned_out = lax.psum(owned_out, "x").astype(jnp.float32)

    def whole_columns(summed, outer, size):
        blocks = summed.reshape(4, rows, outer * size)
        half = jnp.stack(exchange([blocks[t] for t in range(4)], y_index, c_index))
        other = swap(half, ACROSS_X)
        odd = x_index == 1
        both = jnp.stack([jnp.where(odd, other, half), jnp.where(odd, half, other)])
        both = both.reshape(2, 4, rows, outer, size)
        return both.transpose(2, 3, 1, 0, 4).reshape(rows, -1).astype(jnp.float32)

    return (
        activations,
        d_tokens,
        small[0],
        small[1],
        whole_columns(qkv_sum, 3 * groups, unit),
        owned_bqkv,
        owned_out,
        small[2],
        small[3],
        whole_columns(gate_sum, planes, piece),
        whole_columns(up_sum, planes, piece),
        whole_rows(down_sum),
    )


def solution(mesh):
    reps, shards = mesh.shape["rep"], mesh.shape["shard"]
    grid = Mesh(mesh.devices.reshape(reps, shards // 4, 2, 2), EVERY)
    tokens, rows, vector = P(EVERY, None), P(("z", "y", "c"), None), P(("z", "y", "c"))
    return jax.shard_map(
        per_device,
        mesh=grid,
        in_specs=(
            tokens,
            P(EVERY),
            tokens,
            vector,
            vector,
            rows,
            vector,
            rows,
            vector,
            vector,
            rows,
            rows,
            rows,
        ),
        out_specs=(
            tokens,
            tokens,
            vector,
            vector,
            rows,
            vector,
            rows,
            vector,
            vector,
            rows,
            rows,
            rows,
        ),
        check_vma=False,
    )
```

time: 2680 us -> 821 us (0.31)
  waiting for transfers between devices: 2080 us -> 251 us
  local copies, waits for them, and re-layouts: 22.5 us -> 153 us
  blocking collectives: 160 us -> 63.2 us
  matrix products: 241 us -> 176 us
  starting transfers between devices: 0.31 us -> 56 us
  other arithmetic: 145 us -> 95.5 us
    reduce_scatter x2 -> x5, waiting for transfers between devices: 1620 us -> 0.01 us  [scatter_z(): return lax.psum_scatter(values, 'z', scatter_dimension=0, tiled=True)]
    all_gather x5, waiting for transfers between devices: 403 us -> 0.03 us  [gather_z(): return lax.all_gather(values, 'z', axis=0, tiled=True)]
    ppermute x0 -> x86, waiting for transfers between devices: none -> 251 us  [swap(): return lax.ppermute(values, PLANE, pairs)]
    concatenate x1 -> x3, other arithmetic: 106 us -> 2.81 us  [columns(): return jnp.concatenate(exchange(blocks, y_index, c_index), 0)]
    unnamed x115 -> x189, local copies, waits for them, and re-layouts: 8.63 us -> 86.4 us
    all_gather x5 -> x1, blocking collectives: 95.7 us -> 21.3 us  [per_device(): lax.all_gather(jnp.concatenate([ln1_gain, ln1_bias, ln2_gain, ln2_bias, b...]
    unnamed x1 -> x0, blocking collectives: 59.6 us -> none
    ppermute x0 -> x86, starting transfers between devices: none -> 55.6 us  [swap(): return lax.ppermute(values, PLANE, pairs)]
  transfers between devices with their start and end apart: 8 -> 96, of which waited for: 8 -> 31; matrix products, arithmetic and copies ran while one was open for 13% -> 46% of each run, Pallas kernels for 0% -> 0%
where the time goes in v1:
time: 821 us; the launch traced here: 811 us
  waiting for transfers between devices  251 us (31%)
  matrix products  176 us (21%)
  local copies, waits for them, and re-layouts  153 us (19%)
  other arithmetic  95.5 us (12%)
  blocking collectives  63.2 us (8%)
  starting transfers between devices  56 us (7%)
  between operations  15.6 us (2%)
    ppermute x86, waiting for transfers between devices, swap(): return lax.ppermute(values, PLANE, pairs)  251 us
    unnamed x189, local copies, waits for them, and re-layouts  86.4 us
    dot_general x5, matrix products, contract_last(): lax.dot_general(left, right, (((1,), (1,)), ((), ())), preferred_element_...  56.1 us
    ppermute x86, starting transfers between devices, swap(): return lax.ppermute(values, PLANE, pairs)  55.6 us
    dot_general x5, matrix products, dot(): return jnp.dot(left, right, preferred_element_type=jnp.float32)  47.5 us
    dot_general x5, matrix products, contract_first(): lax.dot_general(left, right, (((0,), (0,)), ((), ())), preferred_element_...  47.3 us
    psum x1, blocking collectives, per_device(): lax.psum(jnp.concatenate([grad_gain_one, grad_bias_one, grad_gain_two, gr...  41.8 us
    all_gather x1, blocking collectives, per_device(): lax.all_gather(jnp.concatenate([ln1_gain, ln1_bias, ln2_gain, ln2_bias, b...  21.3 us
  transfers between devices with their start and end apart: 96, of which 31 were waited for; matrix products, arithmetic and copies ran while one was open for 46% of the time, Pallas kernels for 0%

profile of v1, /device:TPU:0, one launch (start us, length us, event | category | flops | bytes accessed | tf_op | source)
XLA Modules:
  0.0 810.7 jit_solution(7985115495827199820)
XLA Ops:
  17.4 4.5 collective-permute-done.8
  33.5 21.3 %all-gather.3 = bf16[16,1,896]{2,1,0:T(2,128)(2,1)S(1)} all-gather(bf16[1,1,896]{2,1,0:T(2,128)(2,1)S(1)} %reshape.355), channel_id=2, replica_groups=mesh['x'=2,'z'=4,'y'=2,'c'=2] {'z','y','c'}, dimensions={0}, use_global_device_ids=true | all-gather | bytes 30464 | tf_op jit(solution)/shard_map/all_gather | solution.py:180
  80.6 10.0 %collective-permute-done.34 = bf16[128,704]{0,1:T(8,128)(2,1)} collective-permute-done((bf16[128,704]{0,1:T(8,128)(2,1)}, bf16[128,704]{0,1:T(8,128)(2,1)}, u32[]{:S(2)}, u32[]{:S(2)}) %collective-permute-start.34) | collective-permute-done | bytes 180256 | tf_op jit(solution)/shard_map/ppermute | solution.py:20
  98.4 7.3 collective-permute-done.2
  117.2 4.7 convert_reduce_fusion
  125.4 5.7 fusion.6
  131.0 11.6 %broadcast_add_fusion = f32[2048,768]{1,0:T(8,128)} fusion(f32[768]{0:T(1024)S(1)} %copy-done.56, bf16[2048,2048]{1,0:T(8,128)(2,1)} %fusion.6, bf16[2048,768]{1,0:T(8,128)(2,1)} %all-gather.10.cloned.1.call-done), kind=kOutput, calls=%fused_computation.33 | convolution fusion | flops 6444023808 | bytes 17828864 | tf_op jit(solution)/shard_map/dot_general | solution.py:101
  142.7 11.8 %reshape.359 = f32[8,256,3,4,64]{4,3,2,1,0:T(4,128)} reshape(f32[2048,768]{1,0:T(8,128)} %broadcast_add_fusion) | data formatting | bytes 12582912 | tf_op jit(solution)/shard_map/reshape | solution.py:215
  154.4 7.7 fusion.56
  162.2 4.8 copy.151
  166.9 4.7 copy.152
  178.0 8.3 %fusion.62 = (f32[8,4,256]{2,1,0:T(4,128)}, f32[8,4,256,256]{2,3,1,0:T(8,128)}) fusion(pred[8,256,256]{1,2,0:T(8,128)(4,1)} %compare_and_fusion, bf16[8,256,4,48]{1,3,2,0:T(8,128)(2,1)S(1)} %slice.688, bf16[8,256,4,8]{1,3,2,0:T(8,128)(2,1)S(1)} %get-tuple-element.176, bf16[8,256,4,8]{1,3,2,0:T(8,128)(2,1)S(1)} %get-tuple-element.177, ...), kind=kOutput, calls=%fused_computation.307 | convolution fusion | flops 283115776 | bytes 11042816 | tf_op jit(solution)/shard_map/sub | solution.py:221
  186.2 4.2 slice.380
  193.7 4.6 fusion.40
  211.7 4.5 collective-permute-done.32
  219.4 15.9 %collective-permute-done.22 = bf16[256,2048]{1,0:T(8,128)(2,1)} collective-permute-done((bf16[256,2048]{1,0:T(8,128)(2,1)}, bf16[256,2048]{1,0:T(8,128)(2,1)}, u32[]{:S(2)}, u32[]{:S(2)}) %collective-permute-start.22) | collective-permute-done | bytes 1048608 | tf_op jit(solution)/shard_map/ppermute | solution.py:20
  244.3 13.3 %collective-permute-done.19 = bf16[256,2048]{1,0:T(8,128)(2,1)S(1)} collective-permute-done((bf16[256,2048]{1,0:T(8,128)(2,1)S(1)}, bf16[256,2048]{1,0:T(8,128)(2,1)S(1)}, u32[]{:S(2)}, u32[]{:S(2)}) %collective-permute-start.19) | collective-permute-done | bytes 1048608 | tf_op jit(solution)/shard_map/ppermute | solution.py:20
  257.6 8.5 %collective-permute-done.23 = bf16[256,2048]{1,0:T(8,128)(2,1)S(1)} collective-permute-done((bf16[256,2048]{1,0:T(8,128)(2,1)S(1)}, bf16[256,2048]{1,0:T(8,128)(2,1)S(1)}, u32[]{:S(2)}, u32[]{:S(2)}) %collective-permute-start.23) | collective-permute-done | bytes 1048608 | tf_op jit(solution)/shard_map/ppermute | solution.py:20
  276.4 17.7 %collective-permute-done.46 = bf16[256,2048]{1,0:T(8,128)(2,1)} collective-permute-done((bf16[256,2048]{1,0:T(8,128)(2,1)}, bf16[256,2048]{1,0:T(8,128)(2,1)}, u32[]{:S(2)}, u32[]{:S(2)}) %collective-permute-start.46) | collective-permute-done | bytes 1048608 | tf_op jit(solution)/shard_map/ppermute | solution.py:20
  301.2 9.3 %collective-permute-done.25 = bf16[256,2048]{1,0:T(8,128)(2,1)S(1)} collective-permute-done((bf16[256,2048]{1,0:T(8,128)(2,1)}, bf16[256,2048]{1,0:T(8,128)(2,1)S(1)}, u32[]{:S(2)}, u32[]{:S(2)}) %collective-permute-start.25) | collective-permute-done | bytes 1048608 | tf_op jit(solution)/shard_map/ppermute | solution.py:20
  312.8 8.9 %collective-permute-done.26 = bf16[256,2048]{1,0:T(8,128)(2,1)S(1)} collective-permute-done((bf16[256,2048]{1,0:T(8,128)(2,1)}, bf16[256,2048]{1,0:T(8,128)(2,1)S(1)}, u32[]{:S(2)}, u32[]{:S(2)}) %collective-permute-start.26) | collective-permute-done | bytes 1048608 | tf_op jit(solution)/shard_map/ppermute | solution.py:20
  328.1 11.2 %fusion.64 = f32[2048,704]{0,1:T(8,128)} fusion(bf16[2048,2048]{1,0:T(8,128)(2,1)} %constant_dynamic-update-slice_fusion.8, bf16[2048,704]{0,1:T(8,128)(2,1)} %all-gather.14.cloned.1.call-done), kind=kOutput, calls=%fused_computation.309 | convolution fusion | flops 5905580032 | bytes 17039360 | tf_op jit(solution)/shard_map/dot_general | solution.py:101
  339.3 11.0 %fusion.63 = f32[2048,704]{0,1:T(8,128)} fusion(bf16[2048,2048]{1,0:T(8,128)(2,1)} %constant_dynamic-update-slice_fusion.8, bf16[2048,704]{0,1:T(8,128)(2,1)} %all-gather.12.cloned.1.call-done), kind=kOutput, calls=%fused_computation.308 | convolution fusion | flops 5905580032 | bytes 17039360 | tf_op jit(solution)/shard_map/dot_general | solution.py:101
  350.3 15.6 %multiply_convert_fusion.1 = (bf16[2048,704]{0,1:T(8,128)(2,1)S(1)}, bf16[2048,704]{0,1:T(8,128)(2,1)}, bf16[2048,704]{0,1:T(8,128)(2,1)}) fusion(f32[2048,704]{0,1:T(8,128)} %fusion.63, f32[2048,704]{0,1:T(8,128)} %fusion.64, bf16[2048,2048]{1,0:T(8,128)(2,1)} %copy-done.40, bf16[1,704,2048]{2,1,0:T(8,128)(2,1)} %all-gather.18.cloned.1.call-done), kind=kOutput, calls=%fused_computation.19 | convolution fusion | flops 5927206912 | bytes 31457280 | tf_op jit(solution)/shard_map/dot_general | solution.py:105
  367.5 10.8 %convolution_convert_fusion.4 = bf16[2048,704]{0,1:T(8,128)(2,1)} fusion(bf16[2048,704]{0,1:T(8,128)(2,1)S(1)} %get-tuple-element.76, bf16[2048,2048]{1,0:T(8,128)(2,1)} %constant_dynamic-update-slice_fusion.8), kind=kOutput, calls=%fused_computation.29 | convolution fusion | flops 5907021824 | bytes 14155776 | tf_op jit(solution)/shard_map/dot_general | solution.py:111
  378.4 9.7 %convolution_convert_fusion.1 = bf16[2048,2048]{1,0:T(8,128)(2,1)S(1)} fusion(bf16[2048,704]{0,1:T(8,128)(2,1)} %get-tuple-element.78, bf16[1,704,2048]{2,1,0:T(8,128)(2,1)} %all-gather.18.cloned.1.call-done), kind=kOutput, calls=%fused_computation.15 | convolution fusion | flops 5909774336 | bytes 14155776 | tf_op jit(solution)/shard_map/dot_general | solution.py:101
  394.5 10.3 %fusion.65 = f32[2048,2048]{1,0:T(8,128)} fusion(bf16[2048,704]{0,1:T(8,128)(2,1)S(1)} %copy-done.62, bf16[2048,704]{0,1:T(8,128)(2,1)S(1)} %copy-done.61), kind=kOutput, calls=%fused_computation.310 | convolution fusion | flops 5905580032 | bytes 22544384 | tf_op jit(solution)/shard_map/dot_general | solution.py:105
  404.8 13.9 %add_convert_fusion = bf16[2048,2048]{1,0:T(8,128)(2,1)} fusion(f32[2048,2048]{1,0:T(8,128)} %fusion.65, bf16[2048,704]{0,1:T(8,128)(2,1)} %copy-done.64, bf16[2048,704]{0,1:T(8,128)(2,1)} %all-gather.14.cloned.1.call-done), kind=kOutput, calls=%fused_computation.9 | convolution fusion | flops 5913968640 | bytes 30932992 | tf_op jit(solution)/shard_map/dot_general | solution.py:105
  431.6 6.7 collective-permute-done.42
  441.9 7.7 collective-permute-done.56
  455.3 10.8 %convolution_convert_fusion.5 = bf16[2048,704]{0,1:T(8,128)(2,1)} fusion(bf16[2048,704]{0,1:T(8,128)(2,1)S(1)} %copy-done.63, bf16[2048,2048]{1,0:T(8,128)(2,1)} %constant_dynamic-update-slice_fusion.8), kind=kOutput, calls=%fused_computation.30 | convolution fusion | flops 5907021824 | bytes 14155776 | tf_op jit(solution)/shard_map/dot_general | solution.py:111
  469.7 22.5 %collective-permute-done.53 = bf16[256,2048]{1,0:T(8,128)(2,1)} collective-permute-done((bf16[256,2048]{1,0:T(8,128)(2,1)}, bf16[256,2048]{1,0:T(8,128)(2,1)}, u32[]{:S(2)}, u32[]{:S(2)}) %collective-permute-start.53) | collective-permute-done | bytes 1048608 | tf_op jit(solution)/shard_map/ppermute | solution.py:20
  494.1 5.9 multiply_reduce_fusion.1
  505.8 23.8 %collective-permute-done.58 = bf16[256,2048]{1,0:T(8,128)(2,1)S(1)} collective-permute-done((bf16[256,2048]{1,0:T(8,128)(2,1)S(1)}, bf16[256,2048]{1,0:T(8,128)(2,1)S(1)}, u32[]{:S(2)}, u32[]{:S(2)}) %collective-permute-start.58) | collective-permute-done | bytes 1048608 | tf_op jit(solution)/shard_map/ppermute | solution.py:20
  529.7 10.5 %convolution_convert_fusion.6 = bf16[704,2048]{1,0:T(8,128)(2,1)} fusion(bf16[2048,704]{0,1:T(8,128)(2,1)} %get-tuple-element.78, bf16[2048,2048]{1,0:T(8,128)(2,1)} %copy-done.40), kind=kOutput, calls=%fused_computation.31 | convolution fusion | flops 5907021824 | bytes 14155776 | tf_op jit(solution)/shard_map/dot_general | solution.py:111
  562.4 6.8 convolution_convert_fusion.8
  574.9 4.8 fusion.37
  581.3 5.2 multiply_reduce_fusion
  600.8 11.8 %convolution_convert_fusion.3 = bf16[2048,768]{1,0:T(8,128)(2,1)} fusion(bf16[2048,2048]{1,0:T(8,128)(2,1)} %fusion.6, bf16[2048,768]{0,1:T(8,128)(2,1)} %constant_dynamic-update-slice_fusion.32), kind=kOutput, calls=%fused_computation.28 | convolution fusion | flops 6444023808 | bytes 14680064 | tf_op jit(solution)/shard_map/dot_general | solution.py:111
  612.6 9.4 %convolution_convert_fusion = bf16[2048,2048]{1,0:T(8,128)(2,1)S(1)} fusion(bf16[2048,768]{0,1:T(8,128)(2,1)} %constant_dynamic-update-slice_fusion.32, bf16[2048,768]{1,0:T(8,128)(2,1)} %all-gather.10.cloned.1.call-done), kind=kOutput, calls=%fused_computation.14 | convolution fusion | flops 6446645248 | bytes 14680064 | tf_op jit(solution)/shard_map/dot_general | solution.py:105
  643.0 5.6 collective-permute-done.85
  653.6 10.5 %collective-permute-done.84 = bf16[4,128,704]{1,2,0:T(8,128)(2,1)} collective-permute-done((bf16[4,128,704]{1,2,0:T(8,128)(2,1)}, bf16[4,128,704]{1,2,0:T(8,128)(2,1)}, u32[]{:S(2)}, u32[]{:S(2)}) %collective-permute-start.84) | collective-permute-done | bytes 720928 | tf_op jit(solution)/shard_map/ppermute | solution.py:20
  665.3 14.2 %collective-permute-done.80 = bf16[4,128,704]{1,2,0:T(8,128)(2,1)} collective-permute-done((bf16[4,128,704]{1,2,0:T(8,128)(2,1)}, bf16[4,128,704]{1,2,0:T(8,128)(2,1)}, u32[]{:S(2)}, u32[]{:S(2)}) %collective-permute-start.80) | collective-permute-done | bytes 720928 | tf_op jit(solution)/shard_map/ppermute | solution.py:20
  699.8 14.8 %collective-permute-done.71 = bf16[256,2048]{1,0:T(8,128)(2,1)} collective-permute-done((bf16[256,2048]{1,0:T(8,128)(2,1)}, bf16[256,2048]{1,0:T(8,128)(2,1)}, u32[]{:S(2)}, u32[]{:S(2)}) %collective-permute-start.71) | collective-permute-done | bytes 1048608 | tf_op jit(solution)/shard_map/ppermute | solution.py:20
  714.6 5.4 fusion.24
  720.1 41.8 %psum.7 = f32[14336]{0:T(1024)S(1)} all-reduce(f32[14336]{0:T(1024)S(1)} %constant_dynamic-update-slice_fusion.36), channel_id=1, replica_groups=mesh['x'=2,'z'=4,'y'=2,'c'=2] {'x','z','y','c'}, use_global_device_ids=true, to_apply=%region_19.20 | all-reduce | flops 14336 | bytes 114688 | tf_op jit(solution)/shard_map/psum | solution.py:287
  772.9 5.0 collective-permute-done.73
  780.4 16.5 %collective-permute-done.75 = bf16[4,128,768]{2,1,0:T(8,128)(2,1)S(1)} collective-permute-done((bf16[4,128,768]{2,1,0:T(8,128)(2,1)S(1)}, bf16[4,128,768]{2,1,0:T(8,128)(2,1)S(1)}, u32[]{:S(2)}, u32[]{:S(2)}) %collective-permute-start.75) | collective-permute-done | bytes 786464 | tf_op jit(solution)/shard_map/ppermute | solution.py:20
  (490 shorter events, 283.1 us)
Async XLA Ops:
  7.2 123.8 %all-gather.10.cloned.1.call-start = ((), (), s32[]{:S(2)}) async-start(), calls=%async_computation.5 | async-start | bytes 3932160 | tf_op jit(solution)/shard_map/all_gather | solution.py:121
  24.0 175.2 %all-gather.16.cloned.1.call-start = ((), (), s32[]{:S(2)}) async-start(), calls=%async_computation.13 | async-start | bytes 1310720 | tf_op jit(solution)/shard_map/all_gather | solution.py:121
  24.1 40.9 %collective-permute-start.10 = (s32[256]{0:T(256)}, s32[256]{0:T(256)}, u32[]{:S(2)}, u32[]{:S(2)}) collective-permute-start(s32[256]{0:T(256)} %param.14), channel_id=1, source_target_pairs={{0,16},{1,3},{2,18},{3,1},{16,0},{17,19},{18,2},{19,17},{4,20},{5,... | collective-permute-start | bytes 3080 | tf_op jit(solution)/shard_map/ppermute | solution.py:20
  26.4 43.5 %collective-permute-start.11 = (s32[256]{0:T(256)}, s32[256]{0:T(256)}, u32[]{:S(2)}, u32[]{:S(2)}) collective-permute-start(s32[256]{0:T(256)} %param.14), channel_id=1, source_target_pairs={{0,2},{1,17},{2,0},{3,19},{16,18},{17,1},{18,16},{19,3},{4,6},{5,2... | collective-permute-start | bytes 3080 | tf_op jit(solution)/shard_map/ppermute | solution.py:20
  27.9 43.9 %collective-permute-start.13 = (s32[256]{0:T(256)}, s32[256]{0:T(256)}, u32[]{:S(2)}, u32[]{:S(2)}) collective-permute-start(s32[256]{0:T(256)} %param.14), channel_id=1, source_target_pairs={{0,1},{1,0},{2,3},{3,2},{16,17},{17,16},{18,19},{19,18},{4,5},{5,4... | collective-permute-start | bytes 3080 | tf_op jit(solution)/shard_map/ppermute | solution.py:20
  27.9 49.5 %collective-permute-start = (bf16[256,2048]{1,0:T(8,128)(2,1)S(1)}, bf16[256,2048]{1,0:T(8,128)(2,1)S(1)}, u32[]{:S(2)}, u32[]{:S(2)}) collective-permute-start(bf16[256,2048]{1,0:T(8,128)(2,1)S(1)} %copy-done.4), channel_id=1, source_target_pairs={{0,16},{1,3},{2,18},{3,1},{16,0},{17,19},{18,2},{19,17},{4,20},{5,... | collective-permute-start | bytes 3145736 | tf_op jit(solution)/shard_map/ppermute | solution.py:20
  30.2 297.9 %all-gather.14.cloned.1.call-start = ((), (), s32[]{:S(2)}) async-start(), calls=%async_computation.7 | async-start | bytes 3604480 | tf_op jit(solution)/shard_map/all_gather | solution.py:121
  71.8 25.0 %collective-permute-start.1 = (bf16[256,2048]{1,0:T(8,128)(2,1)S(1)}, bf16[256,2048]{1,0:T(8,128)(2,1)}, u32[]{:S(2)}, u32[]{:S(2)}) collective-permute-start(bf16[256,2048]{1,0:T(8,128)(2,1)S(1)} %copy-done.4), channel_id=1, source_target_pairs={{0,2},{1,17},{2,0},{3,19},{16,18},{17,1},{18,16},{19,3},{4,6},{5,2... | collective-permute-start | bytes 3145736 | tf_op jit(solution)/shard_map/ppermute | solution.py:20
  77.4 28.2 %collective-permute-start.2 = (bf16[256,2048]{1,0:T(8,128)(2,1)S(1)}, bf16[256,2048]{1,0:T(8,128)(2,1)}, u32[]{:S(2)}, u32[]{:S(2)}) collective-permute-start(bf16[256,2048]{1,0:T(8,128)(2,1)S(1)} %collective-permute-done), channel_id=1, source_target_pairs={{0,2},{1,17},{2,0},{3,19},{16,18},{17,1},{18,16},{19,3},{4,6},{5,2... | collective-permute-start | bytes 3145736 | tf_op jit(solution)/shard_map/ppermute | solution.py:20
  96.7 242.6 %all-gather.12.cloned.1.call-start = ((), (), s32[]{:S(2)}) async-start(), calls=%async_computation.6 | async-start | bytes 3604480 | tf_op jit(solution)/shard_map/all_gather | solution.py:121
  217.3 133.1 %all-gather.18.cloned.1.call-start = ((), (), s32[]{:S(2)}) async-start(), calls=%async_computation.14 | async-start | bytes 3604480 | tf_op jit(solution)/shard_map/all_gather | solution.py:121
  217.3 26.5 %collective-permute-start.44 = (bf16[256,2048]{1,0:T(8,128)(2,1)}, bf16[256,2048]{1,0:T(8,128)(2,1)}, u32[]{:S(2)}, u32[]{:S(2)}) collective-permute-start(bf16[256,2048]{1,0:T(8,128)(2,1)} %param.15), channel_id=1, source_target_pairs={{0,16},{1,3},{2,18},{3,1},{16,0},{17,19},{18,2},{19,17},{4,20},{5,... | collective-permute-start | bytes 3145736 | tf_op jit(solution)/shard_map/ppermute | solution.py:20
  217.9 25.9 %collective-permute-start.17 = (bf16[256,2048]{1,0:T(8,128)(2,1)}, bf16[256,2048]{1,0:T(8,128)(2,1)S(1)}, u32[]{:S(2)}, u32[]{:S(2)}) collective-permute-start(bf16[256,2048]{1,0:T(8,128)(2,1)} %get-tuple-element.97), channel_id=1, source_target_pairs={{0,1},{1,0},{2,3},{3,2},{16,17},{17,16},{18,19},{19,18},{4,5},{5,4... | collective-permute-start | bytes 3145736 | tf_op jit(solution)/shard_map/ppermute | solution.py:20
  217.9 39.7 %collective-permute-start.19 = (bf16[256,2048]{1,0:T(8,128)(2,1)S(1)}, bf16[256,2048]{1,0:T(8,128)(2,1)S(1)}, u32[]{:S(2)}, u32[]{:S(2)}) collective-permute-start(bf16[256,2048]{1,0:T(8,128)(2,1)S(1)} %get-tuple-element.101), channel_id=1, source_target_pairs={{0,2},{1,17},{2,0},{3,19},{16,18},{17,1},{18,16},{19,3},{4,6},{5,2... | collective-permute-start | bytes 3145736 | tf_op jit(solution)/shard_map/ppermute | solution.py:20
  237.7 28.5 %collective-permute-start.23 = (bf16[256,2048]{1,0:T(8,128)(2,1)S(1)}, bf16[256,2048]{1,0:T(8,128)(2,1)S(1)}, u32[]{:S(2)}, u32[]{:S(2)}) collective-permute-start(bf16[256,2048]{1,0:T(8,128)(2,1)S(1)} %add_convert_fusion.12), channel_id=1, source_target_pairs={{0,16},{1,3},{2,18},{3,1},{16,0},{17,19},{18,2},{19,17},{4,20},{5,... | collective-permute-start | bytes 3145736 | tf_op jit(solution)/shard_map/ppermute | solution.py:20
  238.2 36.3 %collective-permute-start.45 = (bf16[256,2048]{1,0:T(8,128)(2,1)}, bf16[256,2048]{1,0:T(8,128)(2,1)}, u32[]{:S(2)}, u32[]{:S(2)}) collective-permute-start(bf16[256,2048]{1,0:T(8,128)(2,1)} %param.15), channel_id=1, source_target_pairs={{0,2},{1,17},{2,0},{3,19},{16,18},{17,1},{18,16},{19,3},{4,6},{5,2... | collective-permute-start | bytes 3145736 | tf_op jit(solution)/shard_map/ppermute | solution.py:20
  243.8 51.6 %collective-permute-start.47 = (bf16[256,2048]{1,0:T(8,128)(2,1)}, bf16[256,2048]{1,0:T(8,128)(2,1)}, u32[]{:S(2)}, u32[]{:S(2)}) collective-permute-start(bf16[256,2048]{1,0:T(8,128)(2,1)} %param.15), channel_id=1, source_target_pairs={{0,1},{1,0},{2,3},{3,2},{16,17},{17,16},{18,19},{19,18},{4,5},{5,4... | collective-permute-start | bytes 3145736 | tf_op jit(solution)/shard_map/ppermute | solution.py:20
  243.8 50.3 %collective-permute-start.46 = (bf16[256,2048]{1,0:T(8,128)(2,1)}, bf16[256,2048]{1,0:T(8,128)(2,1)}, u32[]{:S(2)}, u32[]{:S(2)}) collective-permute-start(bf16[256,2048]{1,0:T(8,128)(2,1)} %collective-permute-done.44), channel_id=1, source_target_pairs={{0,2},{1,17},{2,0},{3,19},{16,18},{17,1},{18,16},{19,3},{4,6},{5,2... | collective-permute-start | bytes 3145736 | tf_op jit(solution)/shard_map/ppermute | solution.py:20
  271.6 25.7 %collective-permute-start.24 = (bf16[256,2048]{1,0:T(8,128)(2,1)}, bf16[256,2048]{1,0:T(8,128)(2,1)}, u32[]{:S(2)}, u32[]{:S(2)}) collective-permute-start(bf16[256,2048]{1,0:T(8,128)(2,1)} %get-tuple-element.71), channel_id=1, source_target_pairs={{0,16},{1,3},{2,18},{3,1},{16,0},{17,19},{18,2},{19,17},{4,20},{5,... | collective-permute-start | bytes 3145736 | tf_op jit(solution)/shard_map/ppermute | solution.py:20
  273.1 278.3 %reduce-scatter.12.cloned.1.call-start = ((), (), s32[]{:S(2)}) async-start(), calls=%async_computation.11 | async-start | bytes 3604480 | tf_op jit(solution)/shard_map/reduce_scatter | solution.py:125
  273.1 27.1 %collective-permute-start.48 = (bf16[256,2048]{1,0:T(8,128)(2,1)}, bf16[256,2048]{1,0:T(8,128)(2,1)S(1)}, u32[]{:S(2)}, u32[]{:S(2)}) collective-permute-start(bf16[256,2048]{1,0:T(8,128)(2,1)} %collective-permute-done.44), channel_id=1, source_target_pairs={{0,1},{1,0},{2,3},{3,2},{16,17},{17,16},{18,19},{19,18},{4,5},{5,4... | collective-permute-start | bytes 3145736 | tf_op jit(solution)/shard_map/ppermute | solution.py:20
  274.5 25.9 %collective-permute-start.49 = (bf16[256,2048]{1,0:T(8,128)(2,1)}, bf16[256,2048]{1,0:T(8,128)(2,1)S(1)}, u32[]{:S(2)}, u32[]{:S(2)}) collective-permute-start(bf16[256,2048]{1,0:T(8,128)(2,1)} %collective-permute-done.45), channel_id=1, source_target_pairs={{0,1},{1,0},{2,3},{3,2},{16,17},{17,16},{18,19},{19,18},{4,5},{5,4... | collective-permute-start | bytes 3145736 | tf_op jit(solution)/shard_map/ppermute | solution.py:20
  300.5 24.4 %collective-permute-start.28 = (bf16[256,2048]{1,0:T(8,128)(2,1)}, bf16[256,2048]{1,0:T(8,128)(2,1)S(1)}, u32[]{:S(2)}, u32[]{:S(2)}) collective-permute-start(bf16[256,2048]{1,0:T(8,128)(2,1)} %collective-permute-done.24), channel_id=1, source_target_pairs={{0,1},{1,0},{2,3},{3,2},{16,17},{17,16},{18,19},{19,18},{4,5},{5,4... | collective-permute-start | bytes 3145736 | tf_op jit(solution)/shard_map/ppermute | solution.py:20
  378.3 177.5 %reduce-scatter.10.cloned.1.call-start = ((), (), s32[]{:S(2)}) async-start(), calls=%async_computation.10 | async-start | bytes 3604480 | tf_op jit(solution)/shard_map/reduce_scatter | solution.py:125
  389.9 32.7 %collective-permute-start.38 = (bf16[256,2048]{1,0:T(8,128)(2,1)S(1)}, bf16[256,2048]{1,0:T(8,128)(2,1)S(1)}, u32[]{:S(2)}, u32[]{:S(2)}) collective-permute-start(bf16[256,2048]{1,0:T(8,128)(2,1)S(1)} %get-tuple-element.94), channel_id=1, source_target_pairs={{0,1},{1,0},{2,3},{3,2},{16,17},{17,16},{18,19},{19,18},{4,5},{5,4... | collective-permute-start | bytes 3145736 | tf_op jit(solution)/shard_map/ppermute | solution.py:20
  390.4 32.3 %collective-permute-start.41 = (bf16[256,2048]{1,0:T(8,128)(2,1)S(1)}, bf16[256,2048]{1,0:T(8,128)(2,1)S(1)}, u32[]{:S(2)}, u32[]{:S(2)}) collective-permute-start(bf16[256,2048]{1,0:T(8,128)(2,1)S(1)} %get-tuple-element.92), channel_id=1, source_target_pairs={{0,1},{1,0},{2,3},{3,2},{16,17},{17,16},{18,19},{19,18},{4,5},{5,4... | collective-permute-start | bytes 3145736 | tf_op jit(solution)/shard_map/ppermute | solution.py:20
  431.2 35.0 %collective-permute-start.37 = (bf16[256,2048]{1,0:T(8,128)(2,1)}, bf16[256,2048]{1,0:T(8,128)(2,1)}, u32[]{:S(2)}, u32[]{:S(2)}) collective-permute-start(bf16[256,2048]{1,0:T(8,128)(2,1)} %get-tuple-element.91), channel_id=1, source_target_pairs={{0,1},{1,0},{2,3},{3,2},{16,17},{17,16},{18,19},{19,18},{4,5},{5,4... | collective-permute-start | bytes 3145736 | tf_op jit(solution)/shard_map/ppermute | solution.py:20
  438.4 31.4 %collective-permute-start.39 = (bf16[256,2048]{1,0:T(8,128)(2,1)S(1)}, bf16[256,2048]{1,0:T(8,128)(2,1)}, u32[]{:S(2)}, u32[]{:S(2)}) collective-permute-start(bf16[256,2048]{1,0:T(8,128)(2,1)S(1)} %get-tuple-element.95), channel_id=1, source_target_pairs={{0,2},{1,17},{2,0},{3,19},{16,18},{17,1},{18,16},{19,3},{4,6},{5,2... | collective-permute-start | bytes 3145736 | tf_op jit(solution)/shard_map/ppermute | solution.py:20
  440.4 51.8 %collective-permute-start.53 = (bf16[256,2048]{1,0:T(8,128)(2,1)}, bf16[256,2048]{1,0:T(8,128)(2,1)}, u32[]{:S(2)}, u32[]{:S(2)}) collective-permute-start(bf16[256,2048]{1,0:T(8,128)(2,1)} %get-tuple-element.89), channel_id=1, source_target_pairs={{0,2},{1,17},{2,0},{3,19},{16,18},{17,1},{18,16},{19,3},{4,6},{5,2... | collective-permute-start | bytes 3145736 | tf_op jit(solution)/shard_map/ppermute | solution.py:20
  449.6 42.6 %collective-permute-start.43 = (bf16[256,2048]{1,0:T(8,128)(2,1)}, bf16[256,2048]{1,0:T(8,128)(2,1)}, u32[]{:S(2)}, u32[]{:S(2)}) collective-permute-start(bf16[256,2048]{1,0:T(8,128)(2,1)} %add_convert_fusion.8), channel_id=1, source_target_pairs={{0,16},{1,3},{2,18},{3,1},{16,0},{17,19},{18,2},{19,17},{4,20},{5,... | collective-permute-start | bytes 3145736 | tf_op jit(solution)/shard_map/ppermute | solution.py:20
  453.8 40.3 %collective-permute-start.57 = (bf16[256,2048]{1,0:T(8,128)(2,1)}, bf16[256,2048]{1,0:T(8,128)(2,1)}, u32[]{:S(2)}, u32[]{:S(2)}) collective-permute-start(bf16[256,2048]{1,0:T(8,128)(2,1)} %add_convert_fusion.4), channel_id=1, source_target_pairs={{0,16},{1,3},{2,18},{3,1},{16,0},{17,19},{18,2},{19,17},{4,20},{5,... | collective-permute-start | bytes 3145736 | tf_op jit(solution)/shard_map/ppermute | solution.py:20
  466.2 163.2 %reduce-scatter.14.cloned.1.call-start = ((), (), s32[]{:S(2)}) async-start(), calls=%async_computation.12 | async-start | bytes 3604480 | tf_op jit(solution)/shard_map/reduce_scatter | solution.py:125
  503.7 26.0 %collective-permute-start.58 = (bf16[256,2048]{1,0:T(8,128)(2,1)S(1)}, bf16[256,2048]{1,0:T(8,128)(2,1)S(1)}, u32[]{:S(2)}, u32[]{:S(2)}) collective-permute-start(bf16[256,2048]{1,0:T(8,128)(2,1)S(1)} %get-tuple-element.67), channel_id=1, source_target_pairs={{0,16},{1,3},{2,18},{3,1},{16,0},{17,19},{18,2},{19,17},{4,20},{5,... | collective-permute-start | bytes 3145736 | tf_op jit(solution)/shard_map/ppermute | solution.py:20
  504.3 36.0 %collective-permute-start.59 = (bf16[256,2048]{1,0:T(8,128)(2,1)S(1)}, bf16[256,2048]{1,0:T(8,128)(2,1)}, u32[]{:S(2)}, u32[]{:S(2)}) collective-permute-start(bf16[256,2048]{1,0:T(8,128)(2,1)S(1)} %get-tuple-element.67), channel_id=1, source_target_pairs={{0,2},{1,17},{2,0},{3,19},{16,18},{17,1},{18,16},{19,3},{4,6},{5,2... | collective-permute-start | bytes 3145736 | tf_op jit(solution)/shard_map/ppermute | solution.py:20
  505.8 39.8 %collective-permute-start.61 = (bf16[256,2048]{1,0:T(8,128)(2,1)S(1)}, bf16[256,2048]{1,0:T(8,128)(2,1)}, u32[]{:S(2)}, u32[]{:S(2)}) collective-permute-start(bf16[256,2048]{1,0:T(8,128)(2,1)S(1)} %get-tuple-element.67), channel_id=1, source_target_pairs={{0,1},{1,0},{2,3},{3,2},{16,17},{17,16},{18,19},{19,18},{4,5},{5,4... | collective-permute-start | bytes 3145736 | tf_op jit(solution)/shard_map/ppermute | solution.py:20
  540.2 142.4 %reduce-scatter.8.cloned.1.call-start = ((), (), s32[]{:S(2)}) async-start(), calls=%async_computation.9 | async-start | bytes 1310720 | tf_op jit(solution)/shard_map/reduce_scatter | solution.py:125
  553.7 73.0 %collective-permute-start.81 = (bf16[128,704]{0,1:T(8,128)(2,1)}, bf16[128,704]{0,1:T(8,128)(2,1)}, u32[]{:S(2)}, u32[]{:S(2)}) collective-permute-start(bf16[128,704]{0,1:T(8,128)(2,1)} %get-tuple-element.147), channel_id=1, source_target_pairs={{0,3},{1,2},{2,1},{3,0},{16,19},{17,18},{18,17},{19,16},{4,7},{5,6... | collective-permute-start | bytes 540680 | tf_op jit(solution)/shard_map/ppermute | solution.py:20
  555.5 71.2 %collective-permute-start.82 = (bf16[128,704]{0,1:T(8,128)(2,1)}, bf16[128,704]{0,1:T(8,128)(2,1)}, u32[]{:S(2)}, u32[]{:S(2)}) collective-permute-start(bf16[128,704]{0,1:T(8,128)(2,1)} %get-tuple-element.148), channel_id=1, source_target_pairs={{0,2},{1,3},{2,0},{3,1},{16,18},{17,19},{18,16},{19,17},{4,6},{5,7... | collective-permute-start | bytes 540680 | tf_op jit(solution)/shard_map/ppermute | solution.py:20
  555.8 71.4 %collective-permute-start.83 = (bf16[128,704]{0,1:T(8,128)(2,1)}, bf16[128,704]{0,1:T(8,128)(2,1)}, u32[]{:S(2)}, u32[]{:S(2)}) collective-permute-start(bf16[128,704]{0,1:T(8,128)(2,1)} %get-tuple-element.146), channel_id=1, source_target_pairs={{0,1},{1,0},{2,3},{3,2},{16,17},{17,16},{18,19},{19,18},{4,5},{5,4... | collective-permute-start | bytes 540680 | tf_op jit(solution)/shard_map/ppermute | solution.py:20
  557.9 71.5 %collective-permute-start.77 = (bf16[128,704]{0,1:T(8,128)(2,1)}, bf16[128,704]{0,1:T(8,128)(2,1)}, u32[]{:S(2)}, u32[]{:S(2)}) collective-permute-start(bf16[128,704]{0,1:T(8,128)(2,1)} %get-tuple-element.152), channel_id=1, source_target_pairs={{0,3},{1,2},{2,1},{3,0},{16,19},{17,18},{18,17},{19,16},{4,7},{5,6... | collective-permute-start | bytes 540680 | tf_op jit(solution)/shard_map/ppermute | solution.py:20
  559.7 71.4 %collective-permute-start.78 = (bf16[128,704]{0,1:T(8,128)(2,1)}, bf16[128,704]{0,1:T(8,128)(2,1)}, u32[]{:S(2)}, u32[]{:S(2)}) collective-permute-start(bf16[128,704]{0,1:T(8,128)(2,1)} %get-tuple-element.153), channel_id=1, source_target_pairs={{0,2},{1,3},{2,0},{3,1},{16,18},{17,19},{18,16},{19,17},{4,6},{5,7... | collective-permute-start | bytes 540680 | tf_op jit(solution)/shard_map/ppermute | solution.py:20
  598.6 166.4 %reduce-scatter.6.cloned.1.call-start = ((), (), s32[]{:S(2)}) async-start(), calls=%async_computation.8 | async-start | bytes 3932160 | tf_op jit(solution)/shard_map/reduce_scatter | solution.py:125
  631.1 33.0 %collective-permute-start.84 = (bf16[4,128,704]{1,2,0:T(8,128)(2,1)}, bf16[4,128,704]{1,2,0:T(8,128)(2,1)}, u32[]{:S(2)}, u32[]{:S(2)}) collective-permute-start(bf16[4,128,704]{1,2,0:T(8,128)(2,1)} %pad_maximum_fusion.11), channel_id=1, source_target_pairs={{0,16},{1,17},{2,18},{3,19},{16,0},{17,1},{18,2},{19,3},{4,20},{5,... | collective-permute-start | bytes 2162696 | tf_op jit(solution)/shard_map/ppermute | solution.py:20
  633.5 46.1 %collective-permute-start.80 = (bf16[4,128,704]{1,2,0:T(8,128)(2,1)}, bf16[4,128,704]{1,2,0:T(8,128)(2,1)}, u32[]{:S(2)}, u32[]{:S(2)}) collective-permute-start(bf16[4,128,704]{1,2,0:T(8,128)(2,1)} %pad_maximum_fusion.10), channel_id=1, source_target_pairs={{0,16},{1,17},{2,18},{3,19},{16,0},{17,1},{18,2},{19,3},{4,20},{5,... | collective-permute-start | bytes 2162696 | tf_op jit(solution)/shard_map/ppermute | solution.py:20
  638.4 44.3 %collective-permute-start.68 = (bf16[256,2048]{1,0:T(8,128)(2,1)}, bf16[256,2048]{1,0:T(8,128)(2,1)}, u32[]{:S(2)}, u32[]{:S(2)}) collective-permute-start(bf16[256,2048]{1,0:T(8,128)(2,1)} %get-tuple-element.81), channel_id=1, source_target_pairs={{0,1},{1,0},{2,3},{3,2},{16,17},{17,16},{18,19},{19,18},{4,5},{5,4... | collective-permute-start | bytes 3145736 | tf_op jit(solution)/shard_map/ppermute | solution.py:20
  638.4 61.4 %collective-permute-start.65 = (bf16[256,2048]{1,0:T(8,128)(2,1)}, bf16[256,2048]{1,0:T(8,128)(2,1)}, u32[]{:S(2)}, u32[]{:S(2)}) collective-permute-start(bf16[256,2048]{1,0:T(8,128)(2,1)} %get-tuple-element.79), channel_id=1, source_target_pairs={{0,1},{1,0},{2,3},{3,2},{16,17},{17,16},{18,19},{19,18},{4,5},{5,4... | collective-permute-start | bytes 3145736 | tf_op jit(solution)/shard_map/ppermute | solution.py:20
  648.7 34.1 %collective-permute-start.70 = (bf16[256,2048]{1,0:T(8,128)(2,1)}, bf16[256,2048]{1,0:T(8,128)(2,1)}, u32[]{:S(2)}, u32[]{:S(2)}) collective-permute-start(bf16[256,2048]{1,0:T(8,128)(2,1)} %get-tuple-element.84), channel_id=1, source_target_pairs={{0,2},{1,17},{2,0},{3,19},{16,18},{17,1},{18,16},{19,3},{4,6},{5,2... | collective-permute-start | bytes 3145736 | tf_op jit(solution)/shard_map/ppermute | solution.py:20
  686.2 28.5 %collective-permute-start.71 = (bf16[256,2048]{1,0:T(8,128)(2,1)}, bf16[256,2048]{1,0:T(8,128)(2,1)}, u32[]{:S(2)}, u32[]{:S(2)}) collective-permute-start(bf16[256,2048]{1,0:T(8,128)(2,1)} %add_convert_fusion.1), channel_id=1, source_target_pairs={{0,16},{1,3},{2,18},{3,1},{16,0},{17,19},{18,2},{19,17},{4,20},{5,... | collective-permute-start | bytes 3145736 | tf_op jit(solution)/shard_map/ppermute | solution.py:20
  (117 other events, 1535.5 us)
Sparse Core Ops, SparseCore 0:
  24.1 65.7 all-gather.9
  92.1 26.5 all-gather.15
  120.9 58.6 all-gather.13
  217.4 56.6 all-gather.11
  276.0 57.8 all-gather.17
  378.4 53.7 reduce-scatter.11
  466.3 53.4 reduce-scatter.9
  540.3 54.1 reduce-scatter.13
  598.7 25.1 reduce-scatter.7
  626.2 58.8 reduce-scatter.5

commit v2 on v1

v2 whole, which is shorter than its diff:
```python
import jax
import jax.numpy as jnp
from jax import lax
from jax.experimental import pallas as pl
from jax.experimental.pallas import tpu as pltpu
from jax.sharding import Mesh, PartitionSpec as P

HEAD_DIM = 64
ROT = 16
PLANE = ("x", "y", "c")
EVERY = ("x", "z", "y", "c")
SIBLING = (1, 1)
FIRST = (4, 2)
SECOND = (2, 4)
ACROSS_X = (4, 4)
ACROSS_Y = (2, 2)
ACROSS_YC = (3, 3)
VMEM_BYTES = 48 << 20
COST = pl.CostEstimate(flops=1 << 20, bytes_accessed=1 << 20, transcendentals=0)


def swap(values, masks):
    pairs = [(i, i ^ masks[i & 1]) for i in range(8)]
    return lax.ppermute(values, PLANE, pairs)


def plane_gather(values):
    near = swap(values, FIRST)
    side = swap(values, SECOND)
    return [values, near, side, swap(near, SECOND)]


def plane_sum(own, near, side, far):
    far = swap(far, SECOND)
    side = swap(side, SECOND)
    near = (near + far.astype(jnp.float32)).astype(jnp.bfloat16)

    def finish():
        return own + side.astype(jnp.float32) + swap(near, FIRST).astype(jnp.float32)

    return near, finish


def with_sibling(values):
    return [values, swap(values, SIBLING)]


def by_owner(parts, y_index, c_index):
    first, second, third, fourth = parts
    odd = c_index == 1
    first, second = jnp.where(odd, second, first), jnp.where(odd, first, second)
    third, fourth = jnp.where(odd, fourth, third), jnp.where(odd, third, fourth)
    upper = y_index == 1
    return [
        jnp.where(upper, third, first),
        jnp.where(upper, fourth, second),
        jnp.where(upper, first, third),
        jnp.where(upper, second, fourth),
    ]


def exchange(blocks, y_index, c_index):
    mine = by_owner(blocks, y_index, c_index)
    moved = [
        mine[0],
        swap(mine[1], SIBLING),
        swap(mine[2], ACROSS_Y),
        swap(mine[3], ACROSS_YC),
    ]
    return by_owner(moved, y_index, c_index)


def rounds(planes):
    bits = planes.bit_length() - 1
    return [("c", 1, 2), ("y", 1, 2)] + [("z", 1 << b, planes) for b in range(bits)]


def meet(values, axis, bit, size):
    return lax.ppermute(values, axis, [(i, i ^ bit) for i in range(size)])


def gather_small(vector, planes):
    held = vector[None]
    for axis, bit, size in rounds(planes):
        other = meet(held, axis, bit, size)
        upper = (lax.axis_index(axis) & bit) != 0
        held = jnp.concatenate(
            [jnp.where(upper, other, held), jnp.where(upper, held, other)], 0
        )
    return held


def gather_rows(block, planes):
    length, place = block.shape[0], lax.axis_index("z")
    whole = jnp.zeros((planes * length, block.shape[1]), block.dtype)
    for k in range(planes):
        part = meet(block, "z", k, planes) if k else block
        whole = lax.dynamic_update_slice(whole, part, ((place ^ k) * length, 0))
    return whole


def sum_small(vector, planes):
    for axis, bit, size in [("x", 1, 2)] + rounds(planes):
        vector = vector + meet(vector, axis, bit, size)
    return vector


def layer_norm(values, gain_vec, bias_vec):
    average = jnp.mean(values, -1, keepdims=True)
    centered = values - average
    recip_std = lax.rsqrt(jnp.mean(centered * centered, -1, keepdims=True) + 1e-05)
    unit_vals = centered * recip_std
    return (unit_vals * gain_vec + bias_vec, unit_vals, recip_std)


def norm_back(grad_in, unit_vals, recip_std, gain_vec):
    scaled = grad_in * gain_vec
    return recip_std * (
        scaled
        - jnp.mean(scaled, -1, keepdims=True)
        - unit_vals * jnp.mean(scaled * unit_vals, -1, keepdims=True)
    )


def dot(left, right):
    return jnp.dot(left, right, preferred_element_type=jnp.float32)


def contract_last(left, right):
    return lax.dot_general(
        left, right, (((1,), (1,)), ((), ())), preferred_element_type=jnp.float32
    )


def contract_first(left, right):
    return lax.dot_general(
        left, right, (((0,), (0,)), ((), ())), preferred_element_type=jnp.float32
    )


def spread_rotary(positions):
    half_rot = ROT // 2
    frequency = 10000.0 ** (-(jnp.arange(half_rot, dtype=jnp.float32) * 2.0 / ROT))
    lane = jnp.arange(2 * HEAD_DIM) % HEAD_DIM
    frequency = jnp.where(lane < ROT, jnp.tile(frequency, 2 * HEAD_DIM // half_rot), 0.0)
    angles = positions.astype(jnp.float32)[:, None] * frequency
    sine = jnp.sin(angles)
    from_right = jnp.where(lane < half_rot, -sine, 0.0)
    from_left = jnp.where(lane < half_rot, 0.0, sine)
    return jnp.cos(angles), from_right, from_left


def turn(values, straight, from_right, from_left):
    cols = values.shape[1]
    times = cols // straight.shape[1]
    wide = [jnp.concatenate([t] * times, 1) for t in (straight, from_right, from_left)]
    half_rot = ROT // 2
    return (
        values * wide[0]
        + pltpu.roll(values, cols - half_rot, 1) * wide[1]
        + pltpu.roll(values, half_rot, 1) * wide[2]
    )


def head_mask(head, shape):
    lane = lax.broadcasted_iota(jnp.int32, shape, 1)
    return (lane >= head * HEAD_DIM) & (lane < (head + 1) * HEAD_DIM)


def visible(docs_col, docs_row):
    shape = (docs_col.shape[0], docs_row.shape[1])
    row = lax.broadcasted_iota(jnp.int32, shape, 0)
    col = lax.broadcasted_iota(jnp.int32, shape, 1)
    return (docs_col == docs_row) & (col <= row)


def head_scores(query, key, mask, allowed):
    picked = jnp.where(mask, query, jnp.zeros_like(query)) * 0.125
    return jnp.where(allowed, contract_last(picked.astype(query.dtype), key), -1e30)


def pick_slot(step, slots, place):
    for k, slot in enumerate(slots):

        @pl.when(step == k)
        def _(slot=slot):
            place[...] = slot[...]


def put_slot(step, value, slots):
    for k, slot in enumerate(slots):

        @pl.when(step == k)
        def _(slot=slot):
            slot[...] = value.astype(slot.dtype)


def loader(step, sources, places, sems):
    def copies(which):
        return [
            pltpu.make_async_copy(sources[which][k], places[k].at[which], sems.at[which, k])
            for k in range(len(places))
        ]

    @pl.when(step == 0)
    def _():
        for which in range(2):
            for copy in copies(which):
                copy.start()

    def wait(which):
        @pl.when(step == 0)
        def _():
            for copy in copies(which):
                copy.wait()

    return wait


def forward_kernel(first, *refs):
    slots, refs = refs[:2], refs[2:]
    gain, bias, proj_bias, docs_col, docs_row, straight, right, left = refs[:8]
    weights = [refs[8:10], refs[10:12]]
    outs, (place, weight, weight_out, sems) = refs[-10:-4], refs[-4:]
    normed, proj, lse, attended = outs[:4]
    step = pl.program_id(0)
    wait = loader(step, weights, [weight, weight_out], sems)
    pick_slot(step, slots, place)
    values, _, _ = layer_norm(place[...].astype(jnp.float32), gain[...], bias[...])
    low = values.astype(jnp.bfloat16)
    normed[...] = low
    allowed = visible(docs_col[0], docs_row[0])
    lane = lax.broadcasted_iota(jnp.int32, lse.shape, 1)
    logs = jnp.zeros(lse.shape, jnp.float32)
    partial = 0.0
    cols = weight_out.shape[1]
    heads = cols // HEAD_DIM
    for which in range(2):
        wait(which)
        whole = dot(low, weight[which]) + proj_bias[which : which + 1, :]
        turned = turn(whole[:, : 2 * cols], straight[...], right[...], left[...])
        turned = turned.astype(jnp.bfloat16)
        query, key = turned[:, :cols], turned[:, cols:]
        value = whole[:, 2 * cols :].astype(jnp.bfloat16)
        start = 3 * cols * which
        proj[:, start : start + 2 * cols] = turned
        proj[:, start + 2 * cols : start + 3 * cols] = value
        joined = jnp.zeros(query.shape, jnp.float32)
        for head in range(heads):
            mask = head_mask(head, query.shape)
            scores = head_scores(query, key, mask, allowed)
            highest = jnp.max(scores, -1, keepdims=True)
            powers = jnp.exp(scores - highest)
            total = jnp.sum(powers, -1, keepdims=True)
            probs = (powers * (1.0 / total)).astype(jnp.bfloat16)
            joined = jnp.where(mask, dot(probs, value), joined)
            logs = jnp.where(lane == heads * which + head, highest + jnp.log(total), logs)
        low_joined = joined.astype(jnp.bfloat16)
        attended[:, cols * which : cols * (which + 1)] = low_joined
        partial += dot(low_joined, weight_out[which])
    lse[...] = logs
    put_slot(step, partial, outs[4:])


def backward_kernel(*refs):
    slots, tokens, refs = refs[:2], refs[2:4], refs[4:]
    docs_col, docs_row, straight, right, left, proj, lse, attended, sums_in, out_in = refs[:10]
    weights = [refs[10:12], refs[12:14]]
    outs, (place, inputs, weight, weight_out, sems) = refs[-10:-5], refs[-5:]
    dproj, sums, out_sum = outs[:3]
    step = pl.program_id(0)
    wait = loader(step, weights, [weight, weight_out], sems)
    pick_slot(step, slots, place)
    pick_slot(step, tokens, inputs)

    @pl.when(step == 0)
    def _():
        sums[...] = sums_in[...]
        out_sum[...] = out_in[...]

    grad = place[...]
    out_sum[...] += contract_first(attended[...], grad)
    cols = weight_out.shape[1]
    heads = cols // HEAD_DIM
    allowed = visible(docs_col[0], docs_row[0])
    width = grad.shape[1]
    dnorm = 0.0
    for which in range(2):
        wait(which)
        datt = contract_last(grad, weight_out[which]).astype(jnp.bfloat16)
        start = 3 * cols * which
        query, key, value = (
            proj[:, start + i * cols : start + (i + 1) * cols] for i in range(3)
        )
        dquery = jnp.zeros(query.shape, jnp.float32)
        dkey, dvalue = dquery, dquery
        for head in range(heads):
            mask = head_mask(head, query.shape)
            scores = head_scores(query, key, mask, allowed)
            place_of = heads * which + head
            probs = jnp.exp(scores - lse[:, place_of : place_of + 1])
            dvalue = jnp.where(mask, contract_first(probs.astype(jnp.bfloat16), datt), dvalue)
            dprobs = contract_last(jnp.where(mask, datt, jnp.zeros_like(datt)), value)
            inner = jnp.sum(probs * dprobs, -1, keepdims=True)
            dscores = (0.125 * probs * (dprobs - inner)).astype(jnp.bfloat16)
            dquery = jnp.where(mask, dot(dscores, key), dquery)
            dkey = jnp.where(mask, contract_first(dscores, query), dkey)
        turned = turn(
            jnp.concatenate([dquery, dkey], 1), straight[...], -right[...], -left[...]
        )
        low = jnp.concatenate([turned, dvalue], 1).astype(jnp.bfloat16)
        dproj[:, start : start + 3 * cols] = low
        dnorm += contract_last(low, weight[which])
        start += 2 * width
        sums[:, start : start + 3 * cols] += jnp.sum(low.astype(jnp.float32), 0, keepdims=True)
    put_slot(step, dnorm, outs[3:])
    values = inputs[...].astype(jnp.float32)
    centered = values - jnp.mean(values, -1, keepdims=True)
    unit = centered * lax.rsqrt(jnp.mean(centered * centered, -1, keepdims=True) + 1e-05)
    sums[:, :width] += jnp.sum(dnorm * unit, 0, keepdims=True)
    sums[:, width : 2 * width] += jnp.sum(dnorm, 0, keepdims=True)


def fixed(shape):
    return pl.BlockSpec(shape, lambda i: (0,) * len(shape))


def moving(shape, first):
    return pl.BlockSpec(shape, lambda i: (first + i,) + (0,) * (len(shape) - 1))


def anywhere(count):
    return [pl.BlockSpec(memory_space=pl.ANY)] * count


def run_kernel(
    kernel, name, blocks, inputs, in_specs, shapes, out_specs, scratch, aliases, later=()
):
    given, used = len(later), kernel
    if given:

        def used(*refs):
            kernel(*refs[given:])

    aliases = {k + given: v for k, v in aliases.items()}
    return pl.pallas_call(
        used,
        grid=(blocks,),
        out_shape=shapes,
        in_specs=anywhere(given) + in_specs,
        out_specs=out_specs,
        scratch_shapes=scratch,
        input_output_aliases=aliases,
        compiler_params=pltpu.CompilerParams(vmem_limit_bytes=VMEM_BYTES),
        cost_estimate=COST,
        name=name,
    )(*later, *inputs)


def after(value, *others):
    return pl.pallas_call(
        lambda *refs: None,
        out_shape=jax.ShapeDtypeStruct(value.shape, value.dtype),
        in_specs=anywhere(1 + len(others)),
        out_specs=pl.BlockSpec(memory_space=pl.ANY),
        input_output_aliases={0: 0},
        cost_estimate=COST,
        name="after",
    )(value, *others)


def part_types(first):
    return jnp.bfloat16 if first else jnp.float32


def attention_forward(first, slots, vectors, weights, docs, tables, carried, later=()):
    length, width = slots[0].shape
    cols = weights[0][1].shape[0]
    shape = jax.ShapeDtypeStruct
    shapes = [
        shape((4 * length, width), jnp.bfloat16),
        shape((4 * length, 6 * cols), jnp.bfloat16),
        shape((4 * length, 128), jnp.float32),
        shape((4 * length, 2 * cols), jnp.bfloat16),
    ] + [shape((length, width), part_types(first))] * 2
    inputs = [*slots, *vectors, *docs, *tables, *weights[0], *weights[1], *carried]
    in_specs = (
        [fixed((length, width))] * 2
        + [fixed(v.shape) for v in vectors]
        + [moving((1, length, 1), first), moving((1, 1, length), first)]
        + [moving((length, 128), first)] * 3
        + anywhere(4 + len(carried))
    )
    out_specs = [moving((length, s.shape[1]), first) for s in shapes[:4]]
    out_specs += [fixed((length, width))] * 2
    scratch = [
        pltpu.VMEM((length, width), jnp.bfloat16),
        pltpu.VMEM((2,) + weights[0][0].shape, jnp.bfloat16),
        pltpu.VMEM((2,) + weights[0][1].shape, jnp.bfloat16),
        pltpu.SemaphoreType.DMA((2, 2)),
    ]
    aliases = {len(inputs) - len(carried) + i: i for i in range(len(carried))}

    def kernel(*refs):
        forward_kernel(first, *refs)

    return run_kernel(
        kernel,
        "attention_forward",
        2,
        inputs,
        in_specs,
        shapes,
        out_specs,
        scratch,
        aliases,
        later,
    )


def attention_backward(
    first, slots, tokens, weights, docs, tables, kept, sums, carried, later=()
):
    length, width = slots[0].shape
    cols = weights[0][1].shape[0]
    shape = jax.ShapeDtypeStruct
    shapes = (
        [shape((4 * length, 6 * cols), jnp.bfloat16)]
        + [shape(s.shape, jnp.float32) for s in sums]
        + [shape((length, width), part_types(first))] * 2
    )
    inputs = [*slots, *tokens, *docs, *tables, *kept, *sums, *weights[0], *weights[1], *carried]
    in_specs = (
        [fixed((length, width))] * 4
        + [moving((1, length, 1), first), moving((1, 1, length), first)]
        + [moving((length, 128), first)] * 3
        + [moving((length, k.shape[1]), first) for k in kept]
        + [fixed(s.shape) for s in sums]
        + anywhere(4 + len(carried))
    )
    out_specs = (
        [moving((length, 6 * cols), first)]
        + [fixed(s.shape) for s in sums]
        + [fixed((length, width))] * 2
    )
    scratch = [pltpu.VMEM((length, width), jnp.bfloat16)] * 2 + [
        pltpu.VMEM((2,) + weights[0][0].shape, jnp.bfloat16),
        pltpu.VMEM((2,) + weights[0][1].shape, jnp.bfloat16),
        pltpu.SemaphoreType.DMA((2, 2)),
    ]
    aliases = {len(inputs) - len(carried): 0} if first else {}
    return run_kernel(
        backward_kernel,
        "attention_backward",
        2,
        inputs,
        in_specs,
        shapes,
        out_specs,
        scratch,
        aliases,
        later,
    )


def last_tile(values, start):
    tile = values[:, start:]
    return tile, pltpu.roll(tile, HEAD_DIM, 1)


def hidden_kernel(*refs):
    slots, weights, refs = refs[:4], refs[4:6], refs[6:]
    raw, joined, *mixed, place, weight, sems = refs
    step = pl.program_id(0)
    wait = loader(step, [weights[:1], weights[1:]], [weight], sems)
    pick_slot(step, slots, place)
    joined[...] = place[...]
    cols = weight.shape[2]
    for which in range(2):
        wait(which)
        out = mixed[which]
        hidden = out.shape[1]
        main = hidden // 128 * 128
        both = dot(place[...], weight[which])
        raw[:, which * cols : (which + 1) * cols] = both
        gate, up = both[:, :main], both[:, main : 2 * main]
        out[:, :main] = (gate * jax.nn.sigmoid(gate) * up).astype(jnp.bfloat16)
        if main < hidden:
            gate, up = last_tile(both, 2 * main)
            rest = (gate * jax.nn.sigmoid(gate) * up).astype(jnp.bfloat16)
            out[:, main:] = rest[:, : hidden - main]


def hidden_back_kernel(grad_out, raw, *refs):
    weights = [refs[0:2], refs[2:4]]
    grads, outs, (weight, weight_down, sems) = refs[-7:-5], refs[-5:-3], refs[-3:]
    step = pl.program_id(0)
    wait = loader(step, weights, [weight, weight_down], sems)
    cols, hidden = weight.shape[2], weight_down.shape[1]
    main = hidden // 128 * 128

    def gradients(gate, up, dm):
        sig = jax.nn.sigmoid(gate)
        return dm * up * sig * (1.0 + gate * (1.0 - sig)), dm * gate * sig

    partial = 0.0
    for which in range(2):
        wait(which)
        dmixed = contract_last(grad_out[...], weight_down[which])
        both = raw[:, which * cols : (which + 1) * cols]
        pieces = list(gradients(both[:, :main], both[:, main : 2 * main], dmixed[:, :main]))
        if main < hidden:
            gate, up = last_tile(both, 2 * main)
            rest = dmixed[:, main:]
            dgate, dup = gradients(gate, up, jnp.concatenate([rest, rest], 1))
            lane = lax.broadcasted_iota(jnp.int32, dgate.shape, 1)
            pieces.append(jnp.where(lane < HEAD_DIM, dgate, pltpu.roll(dup, HEAD_DIM, 1)))
        low = jnp.concatenate(pieces, 1).astype(jnp.bfloat16)
        grads[which][...] = low
        partial += contract_last(low, weight[which])
    put_slot(step, partial, outs)


def mlp_forward(slots, weights):
    length, width = slots[0].shape
    both = weights[0].shape[1]
    shape = jax.ShapeDtypeStruct
    shapes = [
        shape((4 * length, 2 * both), jnp.float32),
        shape((4 * length, width), jnp.bfloat16),
    ] + [shape((4 * length, both // 2), jnp.bfloat16)] * 2
    scratch = [
        pltpu.VMEM((length, width), jnp.bfloat16),
        pltpu.VMEM((2,) + weights[0].shape, jnp.bfloat16),
        pltpu.SemaphoreType.DMA((2, 1)),
    ]
    return run_kernel(
        hidden_kernel,
        "mlp_forward",
        4,
        [*slots, *weights],
        [fixed((length, width))] * 4 + anywhere(2),
        shapes,
        [moving((length, s.shape[1]), 0) for s in shapes],
        scratch,
        {},
    )


def mlp_backward(first, grad_out, raw, weights, carried, later=()):
    length, width = grad_out.shape[0] // 4, grad_out.shape[1]
    both = weights[0][0].shape[1]
    shape = jax.ShapeDtypeStruct
    shapes = [shape((4 * length, both), jnp.bfloat16)] * 2
    shapes += [shape((length, width), part_types(first))] * 2
    inputs = [grad_out, raw, *weights[0], *weights[1], *carried]
    scratch = [
        pltpu.VMEM((2,) + weights[0][0].shape, jnp.bfloat16),
        pltpu.VMEM((2,) + weights[0][1].shape, jnp.bfloat16),
        pltpu.SemaphoreType.DMA((2, 2)),
    ]
    return run_kernel(
        hidden_back_kernel,
        "mlp_backward",
        2,
        inputs,
        [moving((length, width), first), moving((length, 2 * both), first)]
        + anywhere(4 + len(carried)),
        shapes,
        [moving((length, both), first)] * 2 + [fixed((length, width))] * 2,
        scratch,
        {6 + i: i for i in range(len(carried))},
        later,
    )


def join_kernel(*refs):
    pick_slot(pl.program_id(0), refs[:-1], refs[-1])


def join(parts):
    length, width = parts[0].shape
    return run_kernel(
        join_kernel,
        "join",
        len(parts),
        parts,
        [fixed((length, width))] * len(parts),
        jax.ShapeDtypeStruct((len(parts) * length, width), parts[0].dtype),
        moving((length, width), 0),
        [],
        {},
    )


def gather_z(values):
    return lax.all_gather(values, "z", axis=0, tiled=True)


def scatter_z(values):
    return lax.psum_scatter(values, "z", scatter_dimension=0, tiled=True)


def per_device(
    tokens,
    doc_ids,
    cotangent,
    ln1_gain,
    ln1_bias,
    w_qkv,
    b_qkv,
    w_out,
    ln2_gain,
    ln2_bias,
    w_gate,
    w_up,
    w_down,
):
    x_index, z_index = lax.axis_index("x"), lax.axis_index("z")
    y_index, c_index = lax.axis_index("y"), lax.axis_index("c")
    yc_index = 2 * y_index + c_index
    planes = lax.axis_size("z")
    shards = 4 * planes
    rows = w_qkv.shape[0]
    width = rows * shards
    hidden_dim = w_gate.shape[1]
    piece = hidden_dim // (2 * shards)
    mlp = piece * planes
    head_cols = width // 8
    spread = rows % (2 * HEAD_DIM) == 0
    groups = planes if spread else 1
    unit = head_cols // groups
    length = tokens.shape[0]

    def pick_x(values, axis):
        return lax.dynamic_index_in_dim(values, x_index, axis, keepdims=False)

    def pick_yc(values, axis):
        return lax.dynamic_index_in_dim(values, yc_index, axis, keepdims=False)

    def columns(weight, outer, size):
        view = pick_x(weight.reshape(rows, outer, 4, 2, size), 3)
        return [view[:, :, t].reshape(rows, outer * size) for t in range(4)]

    def rows_of_plane(blocks):
        return jnp.concatenate(exchange(blocks, y_index, c_index), 0)

    main = mlp // 128 * 128

    def pair(gate, up):
        return jnp.concatenate([gate[:, :main], up[:, :main], gate[:, main:], up[:, main:]], 1)

    def unpair(both):
        rest = both[..., 2 * main :]
        return (
            jnp.concatenate([both[..., :main], rest[..., : mlp - main]], -1),
            jnp.concatenate([both[..., main : 2 * main], rest[..., mlp - main :]], -1),
        )

    vectors = gather_small(
        jnp.concatenate([ln1_gain, ln1_bias, ln2_gain, ln2_bias, b_qkv]), planes
    )
    block_qkv = rows_of_plane(columns(w_qkv, 3 * groups, unit))
    full_qkv = gather_z(after(block_qkv, vectors))
    if spread:
        full_out = gather_rows(pick_x(w_out.reshape(2, rows // 2, width), 0), planes)
    else:
        full_out = lax.all_gather(w_out, ("z", "y", "c"), axis=0, tiled=True)
        full_out = pick_x(pick_yc(full_out.reshape(4, 2, unit, width), 0), 0)
    block_both = rows_of_plane(
        [
            pair(gate, up)
            for gate, up in zip(columns(w_gate, planes, piece), columns(w_up, planes, piece))
        ]
    )
    full_both = gather_z(block_both)
    full_down = gather_z(pick_x(w_down.reshape(2, piece, width), 0))

    vectors = vectors.astype(jnp.float32)
    gain_one, bias_one, gain_two, bias_two = (
        vectors[:, i * rows : (i + 1) * rows].reshape(width) for i in range(4)
    )
    bias_qkv = vectors[:, 4 * rows :].reshape(3 * groups, 4, 2, unit)
    bias_qkv = pick_x(bias_qkv, 2)
    bias_qkv = jnp.stack(
        [
            lax.dynamic_index_in_dim(bias_qkv, yc_index ^ k, 1, keepdims=False).reshape(-1)
            for k in range(2)
        ]
    )

    docs = jnp.stack(plane_gather(doc_ids))
    token_slots = plane_gather(after(tokens, block_qkv))
    all_cot = join(plane_gather(after(cotangent, token_slots[3])))

    indices = jnp.arange(length, dtype=jnp.int32)
    same_doc = docs[:, :, None] == docs[:, None, :]
    first_row = jnp.min(jnp.where(same_doc, indices[None, None, :], length), axis=2)
    tables = spread_rotary((indices[None] - first_row).reshape(-1))
    docs = (docs[:, :, None], docs[:, None, :])

    norm_vectors = (gain_one[None], bias_one[None], bias_qkv)
    full_qkv = after(
        full_qkv, full_out, block_both, token_slots[3], *tables, *docs, *norm_vectors
    )
    weights = list(zip(with_sibling(full_qkv), with_sibling(full_out)))
    *carried, side_part, far_part = attention_forward(
        2, token_slots[2:], norm_vectors, weights, docs, tables, ()
    )
    normed_low, proj, lse, attended_low, own_part, near_part = attention_forward(
        0, token_slots[:2], norm_vectors, weights, docs, tables, carried, (all_cot,)
    )
    inputs = tokens.astype(jnp.float32)
    hidden = inputs + plane_sum(own_part, near_part, side_part, far_part)[1]()
    normed_two, unit_two, scale_two = layer_norm(hidden, gain_two, bias_two)
    two_slots = plane_gather(normed_two.astype(jnp.bfloat16))
    both_weights = with_sibling(after(full_both, two_slots[1]))
    raw, two_low, *mixed = mlp_forward(two_slots, both_weights)
    down_weights = with_sibling(after(full_down, raw))
    mlp_weights = list(zip(both_weights, down_weights))

    def chip_grad(left, right):
        there = swap(contract_first(left[1], right[1]).astype(jnp.bfloat16), SIBLING)
        here = contract_first(left[0], right[0])
        return (here + there.astype(jnp.float32)).astype(jnp.bfloat16)

    down_grad = chip_grad(mixed, [all_cot] * 2)
    down_sum = scatter_z(down_grad)
    *carried, side_part, far_part = mlp_backward(2, all_cot, raw, mlp_weights, (), (down_grad,))
    *both_grads, own_part, near_part = mlp_backward(0, all_cot, raw, mlp_weights, carried)
    near_low, finish = plane_sum(own_part, near_part, side_part, far_part)
    grad_norm_two = finish()
    two_late = after(two_low, near_low)
    there = swap(contract_first(two_late, both_grads[1]).astype(jnp.bfloat16), SIBLING)
    mixed = [after(m, near_low) for m in mixed]
    down_part = dot(mixed[0], down_weights[0]) + dot(mixed[1], down_weights[1])
    down_part = down_part.reshape(4, length, width)
    down_low = down_part[2:].astype(jnp.bfloat16)
    _, finish = plane_sum(down_part[0], down_part[1], down_low[0], down_low[1])
    activations = (hidden + finish()).astype(jnp.bfloat16)
    grad_gain_two = jnp.sum(grad_norm_two * unit_two, 0)
    grad_bias_two = jnp.sum(grad_norm_two, 0)
    grad_hidden = cotangent.astype(jnp.float32) + norm_back(
        grad_norm_two, unit_two, scale_two, gain_two
    )
    hidden_low = after(grad_hidden.astype(jnp.bfloat16), down_sum)
    here = contract_first(after(two_late, hidden_low), both_grads[0])
    both_grad = (here + there.astype(jnp.float32)).astype(jnp.bfloat16)
    both_sum = scatter_z(both_grad)
    hidden_slots = plane_gather(hidden_low)
    kept = (proj, lse, attended_low)
    sums = [
        jnp.zeros((1, 2 * width + 6 * head_cols), jnp.float32),
        jnp.zeros((2 * head_cols, width), jnp.float32),
    ]
    grad_proj_low, *sums, own_part, near_part = attention_backward(
        0, hidden_slots[:2], token_slots[:2], weights, docs, tables, kept, sums, (), (both_grad,)
    )
    grad_proj_low, vector_sums, out_sum, side_part, far_part = attention_backward(
        2, hidden_slots[2:], token_slots[2:], weights, docs, tables, kept, sums, (grad_proj_low,)
    )
    qkv_grad = chip_grad(
        [normed_low] * 2,
        [grad_proj_low[:, : 3 * head_cols], grad_proj_low[:, 3 * head_cols :]],
    )
    qkv_sum = scatter_z(after(qkv_grad, both_sum))
    out_there = swap(out_sum[head_cols:].astype(jnp.bfloat16), SIBLING)
    out_part = (out_sum[:head_cols] + out_there.astype(jnp.float32)).astype(jnp.bfloat16)
    placed = jnp.zeros((3 * groups, 4, 2, unit), jnp.float32)
    for k in range(2):
        piece_sum = vector_sums[0, 2 * width + 3 * head_cols * k :][: 3 * head_cols]
        placed = lax.dynamic_update_slice(
            placed,
            piece_sum.reshape(3 * groups, 1, 1, unit),
            (0, yc_index ^ k, x_index, 0),
        )
    grad_norm_one = plane_sum(own_part, near_part, side_part, far_part)[1]()
    _, unit_one, scale_one = layer_norm(inputs, gain_one, bias_one)
    grad_gain_one, grad_bias_one = vector_sums[0, :width], vector_sums[0, width : 2 * width]
    d_tokens = grad_hidden + norm_back(grad_norm_one, unit_one, scale_one, gain_one)

    sums = sum_small(
        jnp.concatenate(
            [
                grad_gain_one,
                grad_bias_one,
                grad_gain_two,
                grad_bias_two,
                placed.reshape(3 * width),
            ]
        ),
        planes,
    )
    shard_index = 4 * z_index + yc_index
    small = [
        lax.dynamic_slice_in_dim(sums[i * width : (i + 1) * width], shard_index * rows, rows)
        for i in range(4)
    ]
    owned_bqkv = lax.dynamic_slice_in_dim(sums[4 * width :], shard_index * 3 * rows, 3 * rows)

    def whole_rows(half):
        other = swap(half, ACROSS_X)
        odd = x_index == 1
        return jnp.concatenate(
            [jnp.where(odd, other, half), jnp.where(odd, half, other)], 0
        ).astype(jnp.float32)

    if spread:
        owned_out = whole_rows(scatter_z(after(out_part, qkv_sum)))
    else:
        placed_out = lax.dynamic_update_slice(
            jnp.zeros((4, 2, unit, width), jnp.bfloat16),
            out_part[None, None],
            (yc_index, x_index, 0, 0),
        )
        owned_out = lax.psum_scatter(
            placed_out.reshape(width, width), ("z", "y", "c"), scatter_dimension=0, tiled=True
        )
        owned_out = lax.psum(owned_out, "x").astype(jnp.float32)

    def whole_columns(summed):
        blocks = summed.reshape(4, rows, summed.shape[1])
        half = jnp.stack(exchange([blocks[t] for t in range(4)], y_index, c_index))
        other = swap(half, ACROSS_X)
        odd = x_index == 1
        return jnp.stack([jnp.where(odd, other, half), jnp.where(odd, half, other)])

    def in_order(both, outer, size):
        both = both.reshape(2, 4, rows, outer, size)
        return both.transpose(2, 3, 1, 0, 4).reshape(rows, -1).astype(jnp.float32)

    owned_qkv = in_order(whole_columns(qkv_sum), 3 * groups, unit)
    owned_gate, owned_up = (
        in_order(half, planes, piece) for half in unpair(whole_columns(both_sum))
    )

    return (
        activations,
        d_tokens,
        small[0],
        small[1],
        owned_qkv,
        owned_bqkv,
        owned_out,
        small[2],
        small[3],
        owned_gate,
        owned_up,
        whole_rows(down_sum),
    )


def solution(mesh):
    reps, shards = mesh.shape["rep"], mesh.shape["shard"]
    grid = Mesh(mesh.devices.reshape(reps, shards // 4, 2, 2), EVERY)
    tokens, rows, vector = P(EVERY, None), P(("z", "y", "c"), None), P(("z", "y", "c"))
    return jax.shard_map(
        per_device,
        mesh=grid,
        in_specs=(
            tokens,
            P(EVERY),
            tokens,
            vector,
            vector,
            rows,
            vector,
            rows,
            vector,
            vector,
            rows,
            rows,
            rows,
        ),
        out_specs=(
            tokens,
            tokens,
            vector,
            vector,
            rows,
            vector,
            rows,
            vector,
            vector,
            rows,
            rows,
            rows,
        ),
        check_vma=False,
    )
```

time: 821 us -> 726 us (0.88)
  Pallas kernels: 0 us -> 155 us
  matrix products: 176 us -> 57.7 us
  local copies, waits for them, and re-layouts: 153 us -> 85.8 us
  blocking collectives: 63.2 us -> 0 us
  other arithmetic: 95.5 us -> 56.8 us
  waiting for transfers between devices: 251 us -> 281 us
    pallas_call x0 -> x21, Pallas kernels: none -> 155 us  [the longest x8 155 us: run_kernel(): pl.pallas_call(used, grid=(blocks,), out_shape=shapes, in_specs=anywhere(...]
    dot_general x10 -> x0, matrix products: 73 us -> none  [the longest x5 56.1 us: contract_last(): lax.dot_general(left, right, (((1,), (1,)), ((), ())), preferred_element_...]
    unnamed x189 -> x183, local copies, waits for them, and re-layouts: 86.4 us -> 36.7 us
    ppermute x86 -> x51, waiting for transfers between devices: 251 us -> 203 us  [swap(): return lax.ppermute(values, PLANE, pairs)]
    ppermute x0 -> x12, waiting for transfers between devices: none -> 45.7 us  [meet(): return lax.ppermute(values, axis, [(i, i ^ bit) for i in range(size)])]
    psum x1 -> x0, blocking collectives: 41.8 us -> none  [per_device(): lax.psum(jnp.concatenate([grad_gain_one, grad_bias_one, grad_gain_two, gr...]
    dot_general x5 -> x2, matrix products: 47.5 us -> 9.27 us  [dot(): return jnp.dot(left, right, preferred_element_type=jnp.float32)]
    all_gather x5 -> x3, waiting for transfers between devices: 0.03 us -> 31.4 us  [gather_z(): return lax.all_gather(values, 'z', axis=0, tiled=True)]
  transfers between devices with their start and end apart: 96 -> 70, of which waited for: 31 -> 32; matrix products, arithmetic and copies ran while one was open for 46% -> 24% of each run, Pallas kernels for 0% -> 19%
where the time goes in v2:
time: 726 us; the launch traced here: 713 us
  waiting for transfers between devices  281 us (39%)
  Pallas kernels  155 us (21%)
  local copies, waits for them, and re-layouts  85.8 us (12%)
  starting transfers between devices  61.4 us (8%)
  matrix products  57.7 us (8%)
  other arithmetic  56.8 us (8%)
  between operations  15.7 us (2%)
    ppermute x51, waiting for transfers between devices, swap(): return lax.ppermute(values, PLANE, pairs)  203 us
    pallas_call x8, Pallas kernels, run_kernel(): pl.pallas_call(used, grid=(blocks,), out_shape=shapes, in_specs=anywhere(...  155 us
    dot_general x6, matrix products, contract_first(): lax.dot_general(left, right, (((0,), (0,)), ((), ())), preferred_element_...  48.5 us
    ppermute x12, waiting for transfers between devices, meet(): return lax.ppermute(values, axis, [(i, i ^ bit) for i in range(size)])  45.7 us
    ppermute x51, starting transfers between devices, swap(): return lax.ppermute(values, PLANE, pairs)  43.3 us
    unnamed x183, local copies, waits for them, and re-layouts  36.7 us
    all_gather x3, waiting for transfers between devices, gather_z(): return lax.all_gather(values, 'z', axis=0, tiled=True)  31.4 us
    ppermute x12, starting transfers between devices, meet(): return lax.ppermute(values, axis, [(i, i ^ bit) for i in range(size)])  17.2 us
  transfers between devices with their start and end apart: 70, of which 32 were waited for; matrix products, arithmetic and copies ran while one was open for 24% of the time, Pallas kernels for 19%

profile of v2, /device:TPU:0, one launch (start us, length us, event | category | flops | bytes accessed | tf_op | source)
XLA Modules:
  0.0 713.2 jit_solution(1729426773864859851)
XLA Ops:
  36.1 4.3 collective-permute-done.1
  65.5 7.9 %collective-permute-done.14 = s32[256]{0:T(256)S(1)} collective-permute-done((s32[256]{0:T(256)S(1)}, s32[256]{0:T(256)S(1)}, u32[]{:S(2)}, u32[]{:S(2)}) %collective-permute-start.14) | collective-permute-done | bytes 1056 | tf_op jit(solution)/shard_map/ppermute | solution.py:24
  97.3 7.3 %collective-permute-done.17 = bf16[64,2048]{1,0:T(8,128)(2,1)} collective-permute-done((bf16[64,2048]{1,0:T(8,128)(2,1)}, bf16[64,2048]{1,0:T(8,128)(2,1)}, u32[]{:S(2)}, u32[]{:S(2)}) %collective-permute-start.17) | collective-permute-done | bytes 262176 | tf_op jit(solution)/shard_map/ppermute | solution.py:79
  106.8 17.1 %all-gather.5.cloned.1.call-done.refs_0_ = bf16[2048,768]{1,0:T(8,128)(2,1)} async-done(((bf16[512,768]{1,0:T(8,128)(2,1)}), bf16[2048,768]{1,0:T(8,128)(2,1)}) %all-gather.5.cloned.1.call-update) | async-done | bytes 3145744 | tf_op jit(solution)/shard_map/all_gather | solution.py:597
  128.8 23.6 %collective-permute-done.5.refs_1_ = bf16[256,2048]{1,0:T(8,128)(2,1)S(1)} collective-permute-done((bf16[256,2048]{1,0:T(8,128)(2,1)}, bf16[256,2048]{1,0:T(8,128)(2,1)S(1)}, u32[]{:S(2)}, u32[]{:S(2)}) %collective-permute-start.5) | collective-permute-done | bytes 1048608 | tf_op jit(solution)/shard_map/ppermute | solution.py:24
  155.3 18.2 %attention_forward.2 = (bf16[1024,2048]{1,0:T(8,128)(2,1)}, bf16[1024,1536]{1,0:T(8,128)(2,1)}, f32[1024,128]{1,0:T(8,128)S(1)}, bf16[1024,512]{1,0:T(8,128)(2,1...) custom-call(bf16[256,2048]{1,0:T(8,128)(2,1)} %copy-done.38, bf16[256,2048]{1,0:T(8,128)(2,1)} %copy-done.35, ...), custom_call_target="tpu_custom_call" | custom-call | flops 1048576 | bytes 1048576 | tf_op jit(solution)/shard_map/attention_forward/pallas_call | solution.py:346
  178.2 18.3 %attention_forward.3 = (bf16[1024,2048]{1,0:T(8,128)(2,1)}, bf16[1024,1536]{1,0:T(8,128)(2,1)}, f32[1024,128]{1,0:T(8,128)S(1)}, bf16[1024,512]{1,0:T(8,128)(2,1...) custom-call(bf16[1024,2048]{1,0:T(8,128)(2,1)} %join.1.refs_0_.refs_, ...), custom_call_target="tpu_custom_call", output_to_operand_aliasing={{0}: (15, {}), {1}: (16, {}), {2}: (17, {}), {3}: (18, {})} | custom-call | flops 1048576 | bytes 1048576 | tf_op jit(solution)/shard_map/attention_forward/pallas_call | solution.py:346
  199.9 13.9 %collective-permute-done.26 = bf16[256,2048]{1,0:T(8,128)(2,1)S(1)} collective-permute-done((bf16[256,2048]{1,0:T(8,128)(2,1)S(1)}, bf16[256,2048]{1,0:T(8,128)(2,1)S(1)}, u32[]{:S(2)}, u32[]{:S(2)}) %collective-permute-start.26) | collective-permute-done | bytes 1048608 | tf_op jit(solution)/shard_map/ppermute | solution.py:24
  218.1 11.4 %all-gather.7.cloned.1.call-done.refs_0_ = bf16[2048,1408]{1,0:T(8,128)(2,1)} async-done(((bf16[512,1408]{1,0:T(8,128)(2,1)}), bf16[2048,1408]{1,0:T(8,128)(2,1)}) %all-gather.7.cloned.1.call-update) | async-done | bytes 5767184 | tf_op jit(solution)/shard_map/all_gather | solution.py:597
  235.8 13.0 %collective-permute-done.28.refs_2_ = bf16[256,2048]{1,0:T(8,128)(2,1)S(1)} collective-permute-done((bf16[256,2048]{1,0:T(8,128)(2,1)}, bf16[256,2048]{1,0:T(8,128)(2,1)S(1)}, u32[]{:S(2)}, u32[]{:S(2)}) %collective-permute-start.28) | collective-permute-done | bytes 1048608 | tf_op jit(solution)/shard_map/ppermute | solution.py:24
  248.8 11.2 %collective-permute-done.29.refs_3_ = bf16[256,2048]{1,0:T(8,128)(2,1)S(1)} collective-permute-done((bf16[256,2048]{1,0:T(8,128)(2,1)}, bf16[256,2048]{1,0:T(8,128)(2,1)S(1)}, u32[]{:S(2)}, u32[]{:S(2)}) %collective-permute-start.29) | collective-permute-done | bytes 1048608 | tf_op jit(solution)/shard_map/ppermute | solution.py:24
  260.0 21.4 %mlp_forward.1 = (f32[1024,2816]{1,0:T(8,128)}, bf16[1024,2048]{1,0:T(8,128)(2,1)}, bf16[1024,704]{1,0:T(8,128)(2,1)S(1)}, bf16[1024,704]{1,0:T(8,128)(2,1)}) custom-call(bf16[256,2048]{1,0:T(8,128)(2,1)} %add_convert_fusion.6.refs_0_, bf16[256,2048]{1,0:T(8,128)(2,1)} %collective-permute-done.27.refs_1_, ...), custom_call_target="tpu_custom_call" | custom-call | flops 1048576 | bytes 1048576 | tf_op jit(solution)/shard_map/mlp_forward/pallas_call | solution.py:346
  281.4 6.5 convolution_convert_fusion.2
  293.5 8.3 %add_convert_fusion.2.refs_0_ = bf16[704,2048]{1,0:T(8,128)(2,1)} fusion(bf16[704,2048]{1,0:T(8,128)(2,1)} %collective-permute-done.32, bf16[1024,704]{1,0:T(8,128)(2,1)} %copy-done.10, bf16[1024,2048]{1,0:T(8,128)(2,1)} %join.1.refs_0_.refs_1_.grad_out), kind=kOutput, calls=%fused_computation.3 | convolution fusion | flops 2957115392 | bytes 11403264 | tf_op jit(solution)/shard_map/dot_general | solution.py:136
  301.8 21.3 %mlp_backward.2 = (bf16[1024,1408]{1,0:T(8,128)(2,1)S(1)}, bf16[1024,1408]{1,0:T(8,128)(2,1)}, bf16[256,2048]{1,0:T(8,128)(2,1)S(1)}, bf16[256,2048]{1,0:T(8,128)(2,1)}) custom-call(bf16[704,2048]{1,0:T(8,128)(2,1)} %add_convert_fusion.2.refs_0_, bf16[1024,2048]{1,0:T(8,128)(2,1)} %join.1.refs_0_.refs_1_.grad_out, ...), custom_call_target="tpu_custom_call" | custom-call | flops 1048576 | bytes 1048576 | tf_op jit(solution)/shard_map/mlp_backward/pallas_call | solution.py:346
  326.7 21.5 %mlp_backward.3 = (bf16[1024,1408]{1,0:T(8,128)(2,1)}, bf16[1024,1408]{1,0:T(8,128)(2,1)}, f32[256,2048]{1,0:T(8,128)S(1)}, f32[256,2048]{1,0:T(8,128)S(1)}) custom-call(bf16[1024,2048]{1,0:T(8,128)(2,1)} %join.1.refs_0_.refs_1_.grad_out, f32[1024,2816]{1,0:T(8,128)} %get-tuple-element.55.refs_1_.refs_2_.raw, ...), custom_call_target="tpu_custom_call", output_to_operand_aliasing={{0}: (6, {}), {1}: (7, {})} | custom-call | flops 1048576 | bytes 1048576 | tf_op jit(solution)/shard_map/mlp_backward/pallas_call | solution.py:346
  351.5 11.1 %convolution_convert_fusion = bf16[2048,1408]{1,0:T(8,128)(2,1)} fusion(bf16[1024,2048]{1,0:T(8,128)(2,1)} %after.21.refs_0_, bf16[1024,1408]{1,0:T(8,128)(2,1)} %get-tuple-element.65), kind=kOutput, calls=%fused_computation.1 | convolution fusion | flops 5908463616 | bytes 12845056 | tf_op jit(solution)/shard_map/dot_general | solution.py:136
  362.7 5.9 fusion.37
  368.6 3.4 fusion.36
  376.3 21.1 %collective-permute-done.35 = bf16[256,2048]{1,0:T(8,128)(2,1)S(1)} collective-permute-done((bf16[256,2048]{1,0:T(8,128)(2,1)S(1)}, bf16[256,2048]{1,0:T(8,128)(2,1)S(1)}, u32[]{:S(2)}, u32[]{:S(2)}) %collective-permute-start.35) | collective-permute-done | bytes 1048608 | tf_op jit(solution)/shard_map/ppermute | solution.py:24
  398.5 21.4 %collective-permute-done.37 = bf16[256,2048]{1,0:T(8,128)(2,1)S(1)} collective-permute-done((bf16[256,2048]{1,0:T(8,128)(2,1)S(1)}, bf16[256,2048]{1,0:T(8,128)(2,1)S(1)}, u32[]{:S(2)}, u32[]{:S(2)}) %collective-permute-start.37) | collective-permute-done | bytes 1048608 | tf_op jit(solution)/shard_map/ppermute | solution.py:24
  421.3 10.9 %collective-permute-done.34 = bf16[256,2048]{1,0:T(8,128)(2,1)S(1)} collective-permute-done((bf16[256,2048]{1,0:T(8,128)(2,1)S(1)}, bf16[256,2048]{1,0:T(8,128)(2,1)S(1)}, u32[]{:S(2)}, u32[]{:S(2)}) %collective-permute-start.34) | collective-permute-done | bytes 1048608 | tf_op jit(solution)/shard_map/ppermute | solution.py:24
  432.1 3.3 fusion.29
  435.5 11.8 %add_convert_fusion.refs_0_ = bf16[2048,1408]{1,0:T(8,128)(2,1)} fusion(bf16[2048,1408]{1,0:T(8,128)(2,1)} %collective-permute-done.39, bf16[1024,2048]{1,0:T(8,128)(2,1)} %after.23, bf16[1024,1408]{1,0:T(8,128)(2,1)} %get-tuple-element.64), kind=kOutput, calls=%fused_computation | convolution fusion | flops 5914230784 | bytes 18612224 | tf_op jit(solution)/shard_map/dot_general | solution.py:136
  450.5 22.8 %collective-permute-done.40.refs_2_ = bf16[256,2048]{1,0:T(8,128)(2,1)S(1)} collective-permute-done((bf16[256,2048]{1,0:T(8,128)(2,1)S(1)}, bf16[256,2048]{1,0:T(8,128)(2,1)S(1)}, u32[]{:S(2)}, u32[]{:S(2)}) %collective-permute-start.40) | collective-permute-done | bytes 1048608 | tf_op jit(solution)/shard_map/ppermute | solution.py:24
  477.6 25.9 %attention_backward.2 = (bf16[1024,1536]{1,0:T(8,128)(2,1)}, f32[1,5632]{1,0:T(1,128)S(1)}, f32[512,2048]{1,0:T(8,128)}, f32[256,2048]{1,0:T(8,128)}, f32[256,2048]{1,0:T(8,128)}) custom-call(bf16[2048,1408]{1,0:T(8,128)(2,1)} %add_convert_fusion.refs_0_, bf16[256,2048]{1,0:T(8,128)(2,1)S(1)} %copy-done.9, ...), custom_call_target="tpu_custom_call" | custom-call | flops 1048576 | bytes 1048576 | tf_op jit(solution)/shard_map/attention_backward/pallas_call | solution.py:346
  504.5 25.8 %attention_backward.3 = (bf16[1024,1536]{1,0:T(8,128)(2,1)}, f32[1,5632]{1,0:T(1,128)S(1)}, f32[512,2048]{1,0:T(8,128)}, bf16[256,2048]{1,0:T(8,128)(2,1)S(1)}, bf16[256,2048]{1,0:T(8,128)(2,1)S(1)}) custom-call(bf16[256,2048]{1,0:T(8,128)(2,1)S(1)} %collective-permute-done.41.refs_0_, ...), custom_call_target="tpu_custom_call", output_to_operand_aliasing={{0}: (18, {})} | custom-call | flops 1048576 | bytes 1048576 | tf_op jit(solution)/shard_map/attention_backward/pallas_call | solution.py:346
  530.3 5.6 convolution_convert_fusion.1
  536.0 5.6 collective-permute-done.51
  541.6 5.0 add_convert_fusion.1.refs_0_
  550.5 16.7 %collective-permute-done.46 = f32[14336]{0:T(1024)S(1)} collective-permute-done((f32[14336]{0:T(1024)S(1)}, f32[14336]{0:T(1024)S(1)}, u32[]{:S(2)}, u32[]{:S(2)}) %collective-permute-start.46) | collective-permute-done | bytes 57376 | tf_op jit(solution)/shard_map/ppermute | solution.py:79
  570.0 13.4 %collective-permute-done.48 = f32[14336]{0:T(1024)S(1)} collective-permute-done((f32[14336]{0:T(1024)S(1)}, f32[14336]{0:T(1024)S(1)}, u32[]{:S(2)}, u32[]{:S(2)}) %collective-permute-start.48) | collective-permute-done | bytes 57376 | tf_op jit(solution)/shard_map/ppermute | solution.py:79
  595.4 4.3 collective-permute-done.50
  608.4 4.0 collective-permute-done.43
  612.4 5.5 collective-permute-done.45
  620.1 11.5 %collective-permute-done.58 = bf16[128,1408]{1,0:T(8,128)(2,1)S(1)} collective-permute-done((bf16[128,1408]{1,0:T(8,128)(2,1)S(1)}, bf16[128,1408]{1,0:T(8,128)(2,1)S(1)}, u32[]{:S(2)}, u32[]{:S(2)}) %collective-permute-start.58) | collective-permute-done | bytes 360480 | tf_op jit(solution)/shard_map/ppermute | solution.py:24
  636.7 4.6 collective-permute-start.52
  641.9 4.2 fusion.9
  647.0 4.2 collective-permute-done.53
  652.9 12.3 %collective-permute-done.61 = bf16[4,128,1408]{2,1,0:T(8,128)(2,1)} collective-permute-done((bf16[4,128,1408]{2,1,0:T(8,128)(2,1)}, bf16[4,128,1408]{2,1,0:T(8,128)(2,1)}, u32[]{:S(2)}, u32[]{:S(2)}) %collective-permute-start.61) | collective-permute-done | bytes 1441824 | tf_op jit(solution)/shard_map/ppermute | solution.py:24
  670.4 3.5 copy.223
  673.8 3.7 copy.224
  677.5 3.4 copy.228
  680.9 3.3 fusion.17
  684.2 3.5 copy.225
  687.6 3.7 copy.226
  691.3 3.4 copy.229
  700.4 3.7 copy.227
  (451 shorter events, 184.0 us)
Async XLA Ops:
  15.8 47.6 %collective-permute-start.12 = (s32[256]{0:T(256)}, s32[256]{0:T(256)S(1)}, u32[]{:S(2)}, u32[]{:S(2)}) collective-permute-start(s32[256]{0:T(256)} %param.14), channel_id=1, source_target_pairs={{0,16},{1,3},{2,18},{3,1},{16,0},{17,19},{18,2},{19,17},{4,20},{5,... | collective-permute-start | bytes 3080 | tf_op jit(solution)/shard_map/ppermute | solution.py:24
  17.3 47.1 %collective-permute-start.13 = (s32[256]{0:T(256)}, s32[256]{0:T(256)S(1)}, u32[]{:S(2)}, u32[]{:S(2)}) collective-permute-start(s32[256]{0:T(256)} %param.14), channel_id=1, source_target_pairs={{0,2},{1,17},{2,0},{3,19},{16,18},{17,1},{18,16},{19,3},{4,6},{5,2... | collective-permute-start | bytes 3080 | tf_op jit(solution)/shard_map/ppermute | solution.py:24
  42.4 81.5 %all-gather.5.cloned.1.call-start = ((), (), s32[]{:S(2)}) async-start(), calls=%async_computation.4 | async-start | bytes 3932160 | tf_op jit(solution)/shard_map/all_gather | solution.py:597
  43.1 186.4 %all-gather.7.cloned.1.call-start = ((), (), s32[]{:S(2)}) async-start(), calls=%async_computation.5 | async-start | bytes 7208960 | tf_op jit(solution)/shard_map/all_gather | solution.py:597
  45.2 41.0 %collective-permute-start.15 = (bf16[64,2048]{1,0:T(8,128)(2,1)}, bf16[64,2048]{1,0:T(8,128)(2,1)}, u32[]{:S(2)}, u32[]{:S(2)}) collective-permute-start(bf16[64,2048]{1,0:T(8,128)(2,1)} %get-tuple-element.155), channel_id=1, source_target_pairs={{0,4},{4,0},{8,12},{12,8},{1,5},{5,1},{9,13},{13,9},{2,6},{6,2},{1... | collective-permute-start | bytes 786440 | tf_op jit(solution)/shard_map/ppermute | solution.py:79
  46.7 41.1 %collective-permute-start.16 = (bf16[64,2048]{1,0:T(8,128)(2,1)}, bf16[64,2048]{1,0:T(8,128)(2,1)}, u32[]{:S(2)}, u32[]{:S(2)}) collective-permute-start(bf16[64,2048]{1,0:T(8,128)(2,1)} %get-tuple-element.155), channel_id=1, source_target_pairs={{0,8},{4,12},{8,0},{12,4},{1,9},{5,13},{9,1},{13,5},{2,10},{6,14},... | collective-permute-start | bytes 786440 | tf_op jit(solution)/shard_map/ppermute | solution.py:79
  63.2 30.0 %collective-permute-start.18 = (bf16[128,1408]{1,0:T(8,128)(2,1)}, bf16[128,1408]{1,0:T(8,128)(2,1)}, u32[]{:S(2)}, u32[]{:S(2)}) collective-permute-start(bf16[128,1408]{1,0:T(8,128)(2,1)} %get-tuple-element.180), channel_id=1, source_target_pairs={{0,3},{1,2},{2,1},{3,0},{16,19},{17,18},{18,17},{19,16},{4,7},{5,6... | collective-permute-start | bytes 1081352 | tf_op jit(solution)/shard_map/ppermute | solution.py:24
  64.4 28.8 %collective-permute-start.19 = (bf16[128,1408]{1,0:T(8,128)(2,1)}, bf16[128,1408]{1,0:T(8,128)(2,1)}, u32[]{:S(2)}, u32[]{:S(2)}) collective-permute-start(bf16[128,1408]{1,0:T(8,128)(2,1)} %get-tuple-element.179), channel_id=1, source_target_pairs={{0,2},{1,3},{2,0},{3,1},{16,18},{17,19},{18,16},{19,17},{4,6},{5,7... | collective-permute-start | bytes 1081352 | tf_op jit(solution)/shard_map/ppermute | solution.py:24
  75.4 16.6 %collective-permute-start.3 = (bf16[256,2048]{1,0:T(8,128)(2,1)S(1)}, bf16[256,2048]{1,0:T(8,128)(2,1)S(1)}, u32[]{:S(2)}, u32[]{:S(2)}) collective-permute-start(bf16[256,2048]{1,0:T(8,128)(2,1)S(1)} %copy-done.6), channel_id=1, source_target_pairs={{0,16},{1,3},{2,18},{3,1},{16,0},{17,19},{18,2},{19,17},{4,20},{5,... | collective-permute-start | bytes 3145736 | tf_op jit(solution)/shard_map/ppermute | solution.py:24
  87.8 16.7 %collective-permute-start.17 = (bf16[64,2048]{1,0:T(8,128)(2,1)}, bf16[64,2048]{1,0:T(8,128)(2,1)}, u32[]{:S(2)}, u32[]{:S(2)}) collective-permute-start(bf16[64,2048]{1,0:T(8,128)(2,1)} %get-tuple-element.155), channel_id=1, source_target_pairs={{0,12},{4,8},{8,4},{12,0},{1,13},{5,9},{9,5},{13,1},{2,14},{6,10},... | collective-permute-start | bytes 786440 | tf_op jit(solution)/shard_map/ppermute | solution.py:79
  97.2 193.6 %all-gather.9.cloned.1.call-start = ((), (), s32[]{:S(2)}) async-start(), calls=%async_computation.10 | async-start | bytes 3604480 | tf_op jit(solution)/shard_map/all_gather | solution.py:597
  123.9 28.6 %collective-permute-start.21 = (bf16[2048,768]{1,0:T(8,128)(2,1)}, bf16[2048,768]{1,0:T(8,128)(2,1)}, u32[]{:S(2)}, u32[]{:S(2)}) collective-permute-start(bf16[2048,768]{1,0:T(8,128)(2,1)} %after.16.refs_10_.refs_11_.refs_15_.refs_14_), channel_id=1, source_target_pairs={{0,1},{1,0},{2,3},{3,2},{16,17},{17,16},{18,19},{19,18},{4,5},{5,4... | collective-permute-start | bytes 9437192 | tf_op jit(solution)/shard_map/ppermute | solution.py:24
  126.1 26.3 %collective-permute-start.5 = (bf16[256,2048]{1,0:T(8,128)(2,1)}, bf16[256,2048]{1,0:T(8,128)(2,1)S(1)}, u32[]{:S(2)}, u32[]{:S(2)}) collective-permute-start(bf16[256,2048]{1,0:T(8,128)(2,1)} %after.14.refs_0_), channel_id=1, source_target_pairs={{0,16},{1,3},{2,18},{3,1},{16,0},{17,19},{18,2},{19,17},{4,20},{5,... | collective-permute-start | bytes 3145736 | tf_op jit(solution)/shard_map/ppermute | solution.py:24
  126.8 25.8 %collective-permute-start.23 = (bf16[256,2048]{1,0:T(8,128)(2,1)}, bf16[256,2048]{1,0:T(8,128)(2,1)S(1)}, u32[]{:S(2)}, u32[]{:S(2)}) collective-permute-start(bf16[256,2048]{1,0:T(8,128)(2,1)} %after.13.refs_1_.refs_3_), channel_id=1, source_target_pairs={{0,2},{1,17},{2,0},{3,19},{16,18},{17,1},{18,16},{19,3},{4,6},{5,2... | collective-permute-start | bytes 3145736 | tf_op jit(solution)/shard_map/ppermute | solution.py:24
  127.2 25.3 %collective-permute-start.22 = (bf16[256,2048]{1,0:T(8,128)(2,1)}, bf16[256,2048]{1,0:T(8,128)(2,1)S(1)}, u32[]{:S(2)}, u32[]{:S(2)}) collective-permute-start(bf16[256,2048]{1,0:T(8,128)(2,1)} %constant_dynamic-update-slice_fusion.4.refs_1_.refs_11_.refs_12_.refs_16_.refs_15_), channel_id=1, source_target_pairs={{0,1},{1,0},{2,3},{3,2},{16,17},{17,16},{18,19},{19,18},{4,5},{5,4... | collective-permute-start | bytes 3145736 | tf_op jit(solution)/shard_map/ppermute | solution.py:24
  127.2 48.3 %collective-permute-start.6 = (bf16[256,2048]{1,0:T(8,128)(2,1)}, bf16[256,2048]{1,0:T(8,128)(2,1)S(1)}, u32[]{:S(2)}, u32[]{:S(2)}) collective-permute-start(bf16[256,2048]{1,0:T(8,128)(2,1)} %after.14.refs_0_), channel_id=1, source_target_pairs={{0,2},{1,17},{2,0},{3,19},{16,18},{17,1},{18,16},{19,3},{4,6},{5,2... | collective-permute-start | bytes 3145736 | tf_op jit(solution)/shard_map/ppermute | solution.py:24
  152.4 23.1 %collective-permute-start.7 = (bf16[256,2048]{1,0:T(8,128)(2,1)S(1)}, bf16[256,2048]{1,0:T(8,128)(2,1)S(1)}, u32[]{:S(2)}, u32[]{:S(2)}) collective-permute-start(bf16[256,2048]{1,0:T(8,128)(2,1)S(1)} %collective-permute-done.5.refs_1_), channel_id=1, source_target_pairs={{0,2},{1,17},{2,0},{3,19},{16,18},{17,1},{18,16},{19,3},{4,6},{5,2... | collective-permute-start | bytes 3145736 | tf_op jit(solution)/shard_map/ppermute | solution.py:24
  173.5 23.0 %collective-permute-start.25 = (bf16[256,2048]{1,0:T(8,128)(2,1)S(1)}, bf16[256,2048]{1,0:T(8,128)(2,1)S(1)}, u32[]{:S(2)}, u32[]{:S(2)}) collective-permute-start(bf16[256,2048]{1,0:T(8,128)(2,1)S(1)} %get-tuple-element.53), channel_id=1, source_target_pairs={{0,2},{1,17},{2,0},{3,19},{16,18},{17,1},{18,16},{19,3},{4,6},{5,2... | collective-permute-start | bytes 3145736 | tf_op jit(solution)/shard_map/ppermute | solution.py:24
  178.1 21.8 %collective-permute-start.24 = (bf16[256,2048]{1,0:T(8,128)(2,1)S(1)}, bf16[256,2048]{1,0:T(8,128)(2,1)S(1)}, u32[]{:S(2)}, u32[]{:S(2)}) collective-permute-start(bf16[256,2048]{1,0:T(8,128)(2,1)S(1)} %get-tuple-element.51), channel_id=1, source_target_pairs={{0,2},{1,17},{2,0},{3,19},{16,18},{17,1},{18,16},{19,3},{4,6},{5,2... | collective-permute-start | bytes 3145736 | tf_op jit(solution)/shard_map/ppermute | solution.py:24
  217.5 15.1 %collective-permute-start.27 = (bf16[256,2048]{1,0:T(8,128)(2,1)}, bf16[256,2048]{1,0:T(8,128)(2,1)}, u32[]{:S(2)}, u32[]{:S(2)}) collective-permute-start(bf16[256,2048]{1,0:T(8,128)(2,1)} %add_convert_fusion.6.refs_0_), channel_id=1, source_target_pairs={{0,16},{1,3},{2,18},{3,1},{16,0},{17,19},{18,2},{19,17},{4,20},{5,... | collective-permute-start | bytes 3145736 | tf_op jit(solution)/shard_map/ppermute | solution.py:24
  232.7 27.3 %collective-permute-start.30 = (bf16[2048,1408]{1,0:T(8,128)(2,1)}, bf16[2048,1408]{1,0:T(8,128)(2,1)}, u32[]{:S(2)}, u32[]{:S(2)}) collective-permute-start(bf16[2048,1408]{1,0:T(8,128)(2,1)} %after.17.refs_4_.refs_3_.refs_0_), channel_id=1, source_target_pairs={{0,1},{1,0},{2,3},{3,2},{16,17},{17,16},{18,19},{19,18},{4,5},{5,4... | collective-permute-start | bytes 17301512 | tf_op jit(solution)/shard_map/ppermute | solution.py:24
  233.6 201.8 %reduce-scatter.5.cloned.1.call-start = ((), (), s32[]{:S(2)}) async-start(), calls=%async_computation.6 | async-start | bytes 3604480 | tf_op jit(solution)/shard_map/reduce_scatter | solution.py:601
  233.7 15.1 %collective-permute-start.28 = (bf16[256,2048]{1,0:T(8,128)(2,1)}, bf16[256,2048]{1,0:T(8,128)(2,1)S(1)}, u32[]{:S(2)}, u32[]{:S(2)}) collective-permute-start(bf16[256,2048]{1,0:T(8,128)(2,1)} %add_convert_fusion.6.refs_0_), channel_id=1, source_target_pairs={{0,2},{1,17},{2,0},{3,19},{16,18},{17,1},{18,16},{19,3},{4,6},{5,2... | collective-permute-start | bytes 3145736 | tf_op jit(solution)/shard_map/ppermute | solution.py:24
  235.6 24.3 %collective-permute-start.29 = (bf16[256,2048]{1,0:T(8,128)(2,1)}, bf16[256,2048]{1,0:T(8,128)(2,1)S(1)}, u32[]{:S(2)}, u32[]{:S(2)}) collective-permute-start(bf16[256,2048]{1,0:T(8,128)(2,1)} %collective-permute-done.27.refs_1_), channel_id=1, source_target_pairs={{0,2},{1,17},{2,0},{3,19},{16,18},{17,1},{18,16},{19,3},{4,6},{5,2... | collective-permute-start | bytes 3145736 | tf_op jit(solution)/shard_map/ppermute | solution.py:24
  324.7 23.5 %collective-permute-start.33 = (bf16[256,2048]{1,0:T(8,128)(2,1)}, bf16[256,2048]{1,0:T(8,128)(2,1)}, u32[]{:S(2)}, u32[]{:S(2)}) collective-permute-start(bf16[256,2048]{1,0:T(8,128)(2,1)} %get-tuple-element.60), channel_id=1, source_target_pairs={{0,2},{1,17},{2,0},{3,19},{16,18},{17,1},{18,16},{19,3},{4,6},{5,2... | collective-permute-start | bytes 3145736 | tf_op jit(solution)/shard_map/ppermute | solution.py:24
  326.6 220.2 %reduce-scatter.7.cloned.1.call-start = ((), (), s32[]{:S(2)}) async-start(), calls=%async_computation.7 | async-start | bytes 7208960 | tf_op jit(solution)/shard_map/reduce_scatter | solution.py:601
  362.6 72.8 %collective-permute-start.39 = (bf16[2048,1408]{1,0:T(8,128)(2,1)}, bf16[2048,1408]{1,0:T(8,128)(2,1)}, u32[]{:S(2)}, u32[]{:S(2)}) collective-permute-start(bf16[2048,1408]{1,0:T(8,128)(2,1)} %convolution_convert_fusion), channel_id=1, source_target_pairs={{0,1},{1,0},{2,3},{3,2},{16,17},{17,16},{18,19},{19,18},{4,5},{5,4... | collective-permute-start | bytes 17301512 | tf_op jit(solution)/shard_map/ppermute | solution.py:24
  372.3 25.1 %collective-permute-start.35 = (bf16[256,2048]{1,0:T(8,128)(2,1)S(1)}, bf16[256,2048]{1,0:T(8,128)(2,1)S(1)}, u32[]{:S(2)}, u32[]{:S(2)}) collective-permute-start(bf16[256,2048]{1,0:T(8,128)(2,1)S(1)} %get-tuple-element.157), channel_id=1, source_target_pairs={{0,2},{1,17},{2,0},{3,19},{16,18},{17,1},{18,16},{19,3},{4,6},{5,2... | collective-permute-start | bytes 3145736 | tf_op jit(solution)/shard_map/ppermute | solution.py:24
  372.9 47.1 %collective-permute-start.37 = (bf16[256,2048]{1,0:T(8,128)(2,1)S(1)}, bf16[256,2048]{1,0:T(8,128)(2,1)S(1)}, u32[]{:S(2)}, u32[]{:S(2)}) collective-permute-start(bf16[256,2048]{1,0:T(8,128)(2,1)S(1)} %get-tuple-element.62), channel_id=1, source_target_pairs={{0,2},{1,17},{2,0},{3,19},{16,18},{17,1},{18,16},{19,3},{4,6},{5,2... | collective-permute-start | bytes 3145736 | tf_op jit(solution)/shard_map/ppermute | solution.py:24
  374.4 45.5 %collective-permute-start.38 = (bf16[256,2048]{1,0:T(8,128)(2,1)S(1)}, bf16[256,2048]{1,0:T(8,128)(2,1)S(1)}, u32[]{:S(2)}, u32[]{:S(2)}) collective-permute-start(bf16[256,2048]{1,0:T(8,128)(2,1)S(1)} %copy-done.36), channel_id=1, source_target_pairs={{0,16},{1,3},{2,18},{3,1},{16,0},{17,19},{18,2},{19,17},{4,20},{5,... | collective-permute-start | bytes 3145736 | tf_op jit(solution)/shard_map/ppermute | solution.py:24
  375.1 57.0 %collective-permute-start.34 = (bf16[256,2048]{1,0:T(8,128)(2,1)S(1)}, bf16[256,2048]{1,0:T(8,128)(2,1)S(1)}, u32[]{:S(2)}, u32[]{:S(2)}) collective-permute-start(bf16[256,2048]{1,0:T(8,128)(2,1)S(1)} %get-tuple-element.156), channel_id=1, source_target_pairs={{0,2},{1,17},{2,0},{3,19},{16,18},{17,1},{18,16},{19,3},{4,6},{5,2... | collective-permute-start | bytes 3145736 | tf_op jit(solution)/shard_map/ppermute | solution.py:24
  397.8 34.3 %collective-permute-start.36 = (bf16[256,2048]{1,0:T(8,128)(2,1)S(1)}, bf16[256,2048]{1,0:T(8,128)(2,1)S(1)}, u32[]{:S(2)}, u32[]{:S(2)}) collective-permute-start(bf16[256,2048]{1,0:T(8,128)(2,1)S(1)} %fusion.11), channel_id=1, source_target_pairs={{0,16},{1,3},{2,18},{3,1},{16,0},{17,19},{18,2},{19,17},{4,20},{5,... | collective-permute-start | bytes 3145736 | tf_op jit(solution)/shard_map/ppermute | solution.py:24
  447.3 187.3 %reduce-scatter.9.cloned.1.call-start = ((), (), s32[]{:S(2)}) async-start(), calls=%async_computation.8 | async-start | bytes 3932160 | tf_op jit(solution)/shard_map/reduce_scatter | solution.py:601
  448.5 24.7 %collective-permute-start.40 = (bf16[256,2048]{1,0:T(8,128)(2,1)S(1)}, bf16[256,2048]{1,0:T(8,128)(2,1)S(1)}, u32[]{:S(2)}, u32[]{:S(2)}) collective-permute-start(bf16[256,2048]{1,0:T(8,128)(2,1)S(1)} %copy-done.9), channel_id=1, source_target_pairs={{0,16},{1,3},{2,18},{3,1},{16,0},{17,19},{18,2},{19,17},{4,20},{5,... | collective-permute-start | bytes 3145736 | tf_op jit(solution)/shard_map/ppermute | solution.py:24
  449.2 54.3 %collective-permute-start.41 = (bf16[256,2048]{1,0:T(8,128)(2,1)S(1)}, bf16[256,2048]{1,0:T(8,128)(2,1)S(1)}, u32[]{:S(2)}, u32[]{:S(2)}) collective-permute-start(bf16[256,2048]{1,0:T(8,128)(2,1)S(1)} %copy-done.9), channel_id=1, source_target_pairs={{0,2},{1,17},{2,0},{3,19},{16,18},{17,1},{18,16},{19,3},{4,6},{5,2... | collective-permute-start | bytes 3145736 | tf_op jit(solution)/shard_map/ppermute | solution.py:24
  473.2 30.3 %collective-permute-start.42 = (bf16[256,2048]{1,0:T(8,128)(2,1)S(1)}, bf16[256,2048]{1,0:T(8,128)(2,1)S(1)}, u32[]{:S(2)}, u32[]{:S(2)}) collective-permute-start(bf16[256,2048]{1,0:T(8,128)(2,1)S(1)} %collective-permute-done.40.refs_2_), channel_id=1, source_target_pairs={{0,2},{1,17},{2,0},{3,19},{16,18},{17,1},{18,16},{19,3},{4,6},{5,2... | collective-permute-start | bytes 3145736 | tf_op jit(solution)/shard_map/ppermute | solution.py:24
  546.9 147.9 %reduce-scatter.11.cloned.1.call-start = ((), (), s32[]{:S(2)}) async-start(), calls=%async_computation.9 | async-start | bytes 1310720 | tf_op jit(solution)/shard_map/reduce_scatter | solution.py:601
  548.0 36.9 %collective-permute-start.62 = (bf16[176,2048]{1,0:T(8,128)(2,1)S(1)}, bf16[176,2048]{1,0:T(8,128)(2,1)}, u32[]{:S(2)}, u32[]{:S(2)}) collective-permute-start(bf16[176,2048]{1,0:T(8,128)(2,1)S(1)} %copy-done.51), channel_id=1, source_target_pairs={{0,16},{1,17},{2,18},{3,19},{16,0},{17,1},{18,2},{19,3},{4,20},{5,... | collective-permute-start | bytes 2162696 | tf_op jit(solution)/shard_map/ppermute | solution.py:24
  549.9 17.3 %collective-permute-start.46 = (f32[14336]{0:T(1024)S(1)}, f32[14336]{0:T(1024)S(1)}, u32[]{:S(2)}, u32[]{:S(2)}) collective-permute-start(f32[14336]{0:T(1024)S(1)} %constant_dynamic-update-slice_fusion), channel_id=1, source_target_pairs={{0,16},{16,0},{1,17},{17,1},{2,18},{18,2},{3,19},{19,3},{4,20},{20... | collective-permute-start | bytes 172040 | tf_op jit(solution)/shard_map/ppermute | solution.py:79
  567.3 35.4 %collective-permute-start.44 = (bf16[256,2048]{1,0:T(8,128)(2,1)S(1)}, bf16[256,2048]{1,0:T(8,128)(2,1)S(1)}, u32[]{:S(2)}, u32[]{:S(2)}) collective-permute-start(bf16[256,2048]{1,0:T(8,128)(2,1)S(1)} %copy-done.26), channel_id=1, source_target_pairs={{0,2},{1,17},{2,0},{3,19},{16,18},{17,1},{18,16},{19,3},{4,6},{5,2... | collective-permute-start | bytes 3145736 | tf_op jit(solution)/shard_map/ppermute | solution.py:24
  587.9 16.7 %collective-permute-start.56 = (bf16[256,2048]{1,0:T(8,128)(2,1)S(1)}, bf16[256,2048]{1,0:T(8,128)(2,1)S(1)}, u32[]{:S(2)}, u32[]{:S(2)}) collective-permute-start(bf16[256,2048]{1,0:T(8,128)(2,1)S(1)} %slice.456), channel_id=1, source_target_pairs={{0,1},{1,0},{2,3},{3,2},{16,17},{17,16},{18,19},{19,18},{4,5},{5,4... | collective-permute-start | bytes 3145736 | tf_op jit(solution)/shard_map/ppermute | solution.py:24
  593.9 18.5 %collective-permute-start.43 = (bf16[256,2048]{1,0:T(8,128)(2,1)S(1)}, bf16[256,2048]{1,0:T(8,128)(2,1)S(1)}, u32[]{:S(2)}, u32[]{:S(2)}) collective-permute-start(bf16[256,2048]{1,0:T(8,128)(2,1)S(1)} %get-tuple-element.73), channel_id=1, source_target_pairs={{0,2},{1,17},{2,0},{3,19},{16,18},{17,1},{18,16},{19,3},{4,6},{5,2... | collective-permute-start | bytes 3145736 | tf_op jit(solution)/shard_map/ppermute | solution.py:24
  603.0 14.9 %collective-permute-start.45 = (bf16[256,2048]{1,0:T(8,128)(2,1)S(1)}, bf16[256,2048]{1,0:T(8,128)(2,1)S(1)}, u32[]{:S(2)}, u32[]{:S(2)}) collective-permute-start(bf16[256,2048]{1,0:T(8,128)(2,1)S(1)} %add_convert_fusion.4), channel_id=1, source_target_pairs={{0,16},{1,3},{2,18},{3,1},{16,0},{17,19},{18,2},{19,17},{4,20},{5,... | collective-permute-start | bytes 3145736 | tf_op jit(solution)/shard_map/ppermute | solution.py:24
  606.5 25.1 %collective-permute-start.58 = (bf16[128,1408]{1,0:T(8,128)(2,1)S(1)}, bf16[128,1408]{1,0:T(8,128)(2,1)S(1)}, u32[]{:S(2)}, u32[]{:S(2)}) collective-permute-start(bf16[128,1408]{1,0:T(8,128)(2,1)S(1)} %get-tuple-element.174), channel_id=1, source_target_pairs={{0,3},{1,2},{2,1},{3,0},{16,19},{17,18},{18,17},{19,16},{4,7},{5,6... | collective-permute-start | bytes 1081352 | tf_op jit(solution)/shard_map/ppermute | solution.py:24
  606.9 24.7 %collective-permute-start.59 = (bf16[128,1408]{1,0:T(8,128)(2,1)S(1)}, bf16[128,1408]{1,0:T(8,128)(2,1)S(1)}, u32[]{:S(2)}, u32[]{:S(2)}) collective-permute-start(bf16[128,1408]{1,0:T(8,128)(2,1)S(1)} %get-tuple-element.175), channel_id=1, source_target_pairs={{0,2},{1,3},{2,0},{3,1},{16,18},{17,19},{18,16},{19,17},{4,6},{5,7... | collective-permute-start | bytes 1081352 | tf_op jit(solution)/shard_map/ppermute | solution.py:24
  608.1 23.4 %collective-permute-start.60 = (bf16[128,1408]{1,0:T(8,128)(2,1)S(1)}, bf16[128,1408]{1,0:T(8,128)(2,1)S(1)}, u32[]{:S(2)}, u32[]{:S(2)}) collective-permute-start(bf16[128,1408]{1,0:T(8,128)(2,1)S(1)} %get-tuple-element.173), channel_id=1, source_target_pairs={{0,1},{1,0},{2,3},{3,2},{16,17},{17,16},{18,19},{19,18},{4,5},{5,4... | collective-permute-start | bytes 1081352 | tf_op jit(solution)/shard_map/ppermute | solution.py:24
  633.2 32.0 %collective-permute-start.61 = (bf16[4,128,1408]{2,1,0:T(8,128)(2,1)}, bf16[4,128,1408]{2,1,0:T(8,128)(2,1)}, u32[]{:S(2)}, u32[]{:S(2)}) collective-permute-start(bf16[4,128,1408]{2,1,0:T(8,128)(2,1)} %pad_maximum_fusion.1), channel_id=1, source_target_pairs={{0,16},{1,17},{2,18},{3,19},{16,0},{17,1},{18,2},{19,3},{4,20},{5,... | collective-permute-start | bytes 4325384 | tf_op jit(solution)/shard_map/ppermute | solution.py:24
  652.3 43.9 %collective-permute-start.55 = (bf16[4,128,768]{2,1,0:T(8,128)(2,1)}, bf16[4,128,768]{2,1,0:T(8,128)(2,1)}, u32[]{:S(2)}, u32[]{:S(2)}) collective-permute-start(bf16[4,128,768]{2,1,0:T(8,128)(2,1)} %pad_maximum_fusion.3), channel_id=1, source_target_pairs={{0,16},{1,17},{2,18},{3,19},{16,0},{17,1},{18,2},{19,3},{4,20},{5,... | collective-permute-start | bytes 2359304 | tf_op jit(solution)/shard_map/ppermute | solution.py:24
  (97 other events, 1192.7 us)
Sparse Core Ops, SparseCore 0:
  45.4 78.4 all-gather.4
  126.0 103.4 all-gather.6
  233.7 56.9 all-gather.8
  326.7 52.9 reduce-scatter.4
  447.5 99.3 reduce-scatter.6
  549.6 63.1 reduce-scatter.8
  642.0 25.5 reduce-scatter.10

commit v3 on v2

v3 whole, which is shorter than its diff:
```python
import jax
import jax.numpy as jnp
from jax import lax
from jax.experimental import pallas as pl
from jax.experimental.pallas import tpu as pltpu
from jax.sharding import Mesh, PartitionSpec as P

HEAD_DIM = 64
ROT = 16
PLANE = ("x", "y", "c")
EVERY = ("x", "z", "y", "c")
SIBLING = (1, 1)
FIRST = (4, 2)
SECOND = (2, 4)
ACROSS_X = (4, 4)
ACROSS_Y = (2, 2)
ACROSS_YC = (3, 3)
VMEM_BYTES = 48 << 20
EXTRA_ROWS = 16
MICROSECONDS = {
    "attention_forward": 15,
    "attention_backward": 18,
    "mlp_forward": 21,
    "mlp_backward": 21,
    "mlp_output": 13,
    "token_product": 14,
    "norm_forward": 5,
    "norm_backward": 5,
    "spread_columns": 4,
    "pick_columns": 3,
    "place_blocks": 1,
    "split_blocks": 1,
    "unpack_vectors": 1,
    "after": 0,
}


def cost(name):
    return cost_of(MICROSECONDS[name])


def cost_of(us):
    flops = us * 1_150_000_000 + 1_000_000
    return pl.CostEstimate(flops=flops, bytes_accessed=1 << 10, transcendentals=0)


def swap(values, masks):
    pairs = [(i, i ^ masks[i & 1]) for i in range(8)]
    return lax.ppermute(values, PLANE, pairs)


def plane_gather(values):
    side = swap(values, SECOND)
    near = after(swap(values, FIRST), side)
    return [values, near, side, swap(near, SECOND)]


def plane_sum(own, near, side, far, later=()):
    far = swap(far, SECOND)
    side = swap(side, SECOND)
    near = after((near + far.astype(jnp.float32)).astype(jnp.bfloat16), side, *later)

    return near, (own, side, swap(near, FIRST))


def with_sibling(values):
    return [values, swap(values, SIBLING)]


def exchange(blocks, later=()):
    if later:
        blocks = [blocks[0]] + [after(block, *later) for block in blocks[1:]]
    blocks, masks = list(blocks), (None, SIBLING, ACROSS_Y, ACROSS_YC)
    return blocks[:1] + [swap(blocks[k], masks[k]) for k in range(1, 4)]


def meet(values, axis, bit, size):
    return lax.ppermute(values, axis, [(i, i ^ bit) for i in range(size)])


def gather_direct(block, axis, size):
    parts = [block] + [meet(block, axis, k, size) for k in range(1, size)]
    return place_blocks(parts, lax.axis_index(axis))


def layer_norm(values, gain_vec, bias_vec):
    average = jnp.mean(values, -1, keepdims=True)
    centered = values - average
    recip_std = lax.rsqrt(jnp.mean(centered * centered, -1, keepdims=True) + 1e-05)
    unit_vals = centered * recip_std
    return (unit_vals * gain_vec + bias_vec, unit_vals, recip_std)


def norm_back(grad_in, unit_vals, recip_std, gain_vec):
    scaled = grad_in * gain_vec
    return recip_std * (
        scaled
        - jnp.mean(scaled, -1, keepdims=True)
        - unit_vals * jnp.mean(scaled * unit_vals, -1, keepdims=True)
    )


def dot(left, right):
    return jnp.dot(left, right, preferred_element_type=jnp.float32)


def contract_last(left, right):
    return lax.dot_general(
        left, right, (((1,), (1,)), ((), ())), preferred_element_type=jnp.float32
    )


def contract_first(left, right):
    return lax.dot_general(
        left, right, (((0,), (0,)), ((), ())), preferred_element_type=jnp.float32
    )


def spread_rotary(positions):
    half_rot = ROT // 2
    frequency = 10000.0 ** (-(jnp.arange(half_rot, dtype=jnp.float32) * 2.0 / ROT))
    lane = jnp.arange(2 * HEAD_DIM) % HEAD_DIM
    frequency = jnp.where(lane < ROT, jnp.tile(frequency, 2 * HEAD_DIM // half_rot), 0.0)
    angles = positions.astype(jnp.float32)[:, None] * frequency
    sine = jnp.sin(angles)
    from_right = jnp.where(lane < half_rot, -sine, 0.0)
    from_left = jnp.where(lane < half_rot, 0.0, sine)
    return jnp.concatenate([jnp.cos(angles), from_right, from_left], 1)


def turn(values, table, direction):
    cols, lanes = values.shape[1], 2 * HEAD_DIM
    times = cols // lanes
    wide = [jnp.concatenate([table[:, k * lanes : (k + 1) * lanes]] * times, 1) for k in range(3)]
    half_rot = ROT // 2
    from_right = pltpu.roll(values, cols - half_rot, 1) * wide[1]
    from_left = pltpu.roll(values, half_rot, 1) * wide[2]
    return values * wide[0] + direction * (from_right + from_left)


def head_mask(head, shape):
    lane = lax.broadcasted_iota(jnp.int32, shape, 1)
    return (lane >= head * HEAD_DIM) & (lane < (head + 1) * HEAD_DIM)


def visible(docs_col, docs_row):
    shape = (docs_col.shape[0], docs_row.shape[1])
    row = lax.broadcasted_iota(jnp.int32, shape, 0)
    col = lax.broadcasted_iota(jnp.int32, shape, 1)
    return (docs_col == docs_row) & (col <= row)


def by_head(values):
    heads = values.shape[1] // HEAD_DIM
    zero = jnp.zeros_like(values)
    return jnp.concatenate(
        [jnp.where(head_mask(head, values.shape), values, zero) for head in range(heads)], 0
    )


def join_heads(stacked):
    heads = stacked.shape[1] // HEAD_DIM
    rows = stacked.shape[0] // heads
    joined = stacked[:rows]
    for head in range(1, heads):
        part = stacked[head * rows : (head + 1) * rows]
        joined = jnp.where(head_mask(head, part.shape), part, joined)
    return joined


def head_scores(query_heads, key, allowed):
    return jnp.where(allowed, contract_last(query_heads, key) * 0.125, -1e30)


def pick_slot(step, slots, place):
    for k, slot in enumerate(slots):

        @pl.when(step == k)
        def _(slot=slot):
            place[...] = slot[...]


def put_slot(step, value, slots):
    for k, slot in enumerate(slots):

        @pl.when(step == k)
        def _(slot=slot):
            slot[...] = value.astype(slot.dtype)


def loader(step, sources, places, sems):
    def copies(which):
        return [
            pltpu.make_async_copy(sources[which][k], places[k].at[which], sems.at[which, k])
            for k in range(len(places))
        ]

    @pl.when(step == 0)
    def _():
        for which in range(2):
            for copy in copies(which):
                copy.start()

    def wait(which):
        @pl.when(step == 0)
        def _():
            for copy in copies(which):
                copy.wait()

    return wait


def forward_kernel(first, *refs):
    slots, refs = refs[:2], refs[2:]
    vectors, docs_col, docs_row, table = refs[:4]
    weights = [refs[4:6], refs[6:8]]
    outs, (place, weight, weight_out, sems) = refs[-10:-4], refs[-4:]
    normed, proj, lse, attended = outs[:4]
    step = pl.program_id(0)
    wait = loader(step, weights, [weight, weight_out], sems)
    pick_slot(step, slots, place)
    width = normed.shape[1]
    gain, bias = vectors[:1, :width], vectors[:1, width : 2 * width]
    values, _, _ = layer_norm(place[...].astype(jnp.float32), gain, bias)
    low = values.astype(jnp.bfloat16)
    normed[...] = low
    allowed = visible(docs_col[0], docs_row[0])
    allowed = jnp.concatenate([allowed] * (weight_out.shape[1] // HEAD_DIM), 0)
    lane = lax.broadcasted_iota(jnp.int32, lse.shape, 1)
    logs = jnp.zeros(lse.shape, jnp.float32)
    partial = 0.0
    cols = weight_out.shape[1]
    heads = cols // HEAD_DIM
    for which in range(2):
        wait(which)
        start = 4 * width + 3 * cols * which
        whole = dot(low, weight[which]) + vectors[:1, start : start + 3 * cols]
        turned = turn(whole[:, : 2 * cols], table[...], 1.0)
        turned = turned.astype(jnp.bfloat16)
        query, key = turned[:, :cols], turned[:, cols:]
        value = whole[:, 2 * cols :].astype(jnp.bfloat16)
        start = 3 * cols * which
        proj[:, start : start + 2 * cols] = turned
        proj[:, start + 2 * cols : start + 3 * cols] = value
        scores = head_scores(by_head(query), key, allowed)
        highest = jnp.max(scores, -1, keepdims=True)
        powers = jnp.exp(scores - highest)
        total = jnp.sum(powers, -1, keepdims=True)
        probs = (powers * (1.0 / total)).astype(jnp.bfloat16)
        joined = join_heads(dot(probs, value))
        log_total = highest + jnp.log(total)
        rows = query.shape[0]
        for head in range(heads):
            part = log_total[head * rows : (head + 1) * rows]
            logs = jnp.where(lane == heads * which + head, part, logs)
        low_joined = joined.astype(jnp.bfloat16)
        attended[:, cols * which : cols * (which + 1)] = low_joined
        partial += dot(low_joined, weight_out[which])
    lse[...] = logs
    put_slot(step, partial, outs[4:])


def backward_kernel(count, *refs):
    slots, tokens, refs = refs[:count], refs[count : 2 * count], refs[2 * count :]
    docs_col, docs_row, table, proj, lse, sums_in = refs[:6]
    weights = [refs[6:8], refs[8:10]]
    outs, (place, inputs, weight, weight_out, sems) = refs[-7 - 2 * count : -5], refs[-5:]
    dproj, sums, dproj_there = outs[0], outs[1], outs[2 : 2 + count]
    step = pl.program_id(0)
    wait = loader(step, weights, [weight, weight_out], sems)
    pick_slot(step, slots, place)
    pick_slot(step, tokens, inputs)

    @pl.when(step == 0)
    def _():
        sums[...] = sums_in[...]

    grad = place[...]
    cols = weight_out.shape[1]
    heads = cols // HEAD_DIM
    allowed = visible(docs_col[0], docs_row[0])
    allowed = jnp.concatenate([allowed] * heads, 0)
    width = grad.shape[1]
    dnorm = 0.0
    for which in range(2):
        wait(which)
        datt = contract_last(grad, weight_out[which]).astype(jnp.bfloat16)
        start = 3 * cols * which
        query, key, value = (
            proj[:, start + i * cols : start + (i + 1) * cols] for i in range(3)
        )
        query_heads, datt_heads = by_head(query), by_head(datt)
        scores = head_scores(query_heads, key, allowed)
        log_total = jnp.concatenate(
            [lse[:, heads * which + head : heads * which + head + 1] for head in range(heads)], 0
        )
        probs = jnp.exp(scores - log_total)
        dvalue = contract_first(probs.astype(jnp.bfloat16), datt_heads)
        dprobs = contract_last(datt_heads, value)
        inner = jnp.sum(probs * dprobs, -1, keepdims=True)
        dscores = (0.125 * probs * (dprobs - inner)).astype(jnp.bfloat16)
        dquery = join_heads(dot(dscores, key))
        dkey = contract_first(dscores, query_heads)
        turned = turn(jnp.concatenate([dquery, dkey], 1), table[...], -1.0)
        low = jnp.concatenate([turned, dvalue], 1).astype(jnp.bfloat16)
        if which == 0:
            dproj[...] = low
        else:
            put_slot(step, low, dproj_there)
        dnorm += contract_last(low, weight[which])
        start += 2 * width
        sums[:, start : start + 3 * cols] += jnp.sum(low.astype(jnp.float32), 0, keepdims=True)
    put_slot(step, dnorm, outs[2 + count :])
    values = inputs[...].astype(jnp.float32)
    centered = values - jnp.mean(values, -1, keepdims=True)
    unit = centered * lax.rsqrt(jnp.mean(centered * centered, -1, keepdims=True) + 1e-05)
    sums[:, :width] += jnp.sum(dnorm * unit, 0, keepdims=True)
    sums[:, width : 2 * width] += jnp.sum(dnorm, 0, keepdims=True)


def standardized(values):
    centered = values - jnp.mean(values, -1, keepdims=True)
    recip_std = lax.rsqrt(jnp.mean(centered * centered, -1, keepdims=True) + 1e-05)
    return centered * recip_std, recip_std


def norm_forward(tokens, parts, vectors):
    length, width = tokens.shape
    step = length // 4

    def kernel(token_ref, own, side, near, vec, hidden, low):
        total = own[...] + side[...].astype(jnp.float32) + near[...].astype(jnp.float32)
        total += token_ref[...].astype(jnp.float32)
        hidden[...] = total
        unit, _ = standardized(total)
        gain, bias = vec[:1, 2 * width : 3 * width], vec[:1, 3 * width : 4 * width]
        low[...] = (unit * gain + bias).astype(jnp.bfloat16)

    block = moving((step, width), 0)
    return run_kernel(
        kernel,
        "norm_forward",
        4,
        [tokens, *parts, vectors],
        [block] * 4 + [fixed(vectors.shape)],
        [jax.ShapeDtypeStruct((length, width), d) for d in (jnp.float32, jnp.bfloat16)],
        [block] * 2,
        [],
        {},
    )


def norm_backward(values, straight, parts, vectors, which, with_sums, later=()):
    length, width = values.shape
    step = length // 4

    def kernel(value_ref, straight_ref, own, side, near, vec, total, *more):
        grad = own[...] + side[...].astype(jnp.float32) + near[...].astype(jnp.float32)
        unit, recip_std = standardized(value_ref[...].astype(jnp.float32))
        gain = vec[:1, 2 * which * width : (2 * which + 1) * width]
        back = norm_back(grad, unit, recip_std, gain)
        back += straight_ref[...].astype(jnp.float32)
        total[...] = back
        if with_sums:
            low, sums = more
            low[...] = back.astype(jnp.bfloat16)

            @pl.when(pl.program_id(0) == 0)
            def _():
                sums[...] = jnp.zeros_like(sums)

            sums[:, :width] += jnp.sum(grad * unit, 0, keepdims=True)
            sums[:, width:] += jnp.sum(grad, 0, keepdims=True)

    block = moving((step, width), 0)
    shape = jax.ShapeDtypeStruct
    shapes, specs = [shape((length, width), jnp.float32)], [block]
    if with_sums:
        shapes += [shape((length, width), jnp.bfloat16), shape((1, 2 * width), jnp.float32)]
        specs += [block, fixed((1, 2 * width))]
    return run_kernel(
        kernel,
        "norm_backward",
        4,
        [values, straight, *parts, vectors],
        [block] * 5 + [fixed(vectors.shape)],
        shapes,
        specs,
        [],
        {},
        later,
    )


def fixed(shape):
    return pl.BlockSpec(shape, lambda i: (0,) * len(shape))


def moving(shape, first):
    return pl.BlockSpec(shape, lambda i: (first + i,) + (0,) * (len(shape) - 1))


def anywhere(count):
    return [pl.BlockSpec(memory_space=pl.ANY)] * count


def run_kernel(
    kernel, name, blocks, inputs, in_specs, shapes, out_specs, scratch, aliases, later=(), us=None
):
    given, used = len(later), kernel
    if given:

        def used(*refs):
            kernel(*refs[given:])

    aliases = {k + given: v for k, v in aliases.items()}
    return pl.pallas_call(
        used,
        grid=(blocks,),
        out_shape=shapes,
        in_specs=anywhere(given) + in_specs,
        out_specs=out_specs,
        scratch_shapes=scratch,
        input_output_aliases=aliases,
        compiler_params=pltpu.CompilerParams(vmem_limit_bytes=VMEM_BYTES),
        cost_estimate=cost(name) if us is None else cost_of(us),
        name=name,
    )(*later, *inputs)


def after(value, *others):
    return pl.pallas_call(
        lambda *refs: None,
        out_shape=jax.ShapeDtypeStruct(value.shape, value.dtype),
        in_specs=anywhere(1 + len(others)),
        out_specs=pl.BlockSpec(memory_space=pl.ANY),
        input_output_aliases={0: 0},
        cost_estimate=cost("after"),
        name="after",
    )(value, *others)


def part_types(first):
    return jnp.bfloat16 if first >= 2 else jnp.float32


def attention_forward(first, slots, vectors, weights, docs, table, carried, later=()):
    length, width = slots[0].shape
    cols = weights[0][1].shape[0]
    shape = jax.ShapeDtypeStruct
    shapes = [
        shape((4 * length, width), jnp.bfloat16),
        shape((4 * length, 6 * cols), jnp.bfloat16),
        shape((4 * length, 128), jnp.float32),
        shape((4 * length, 2 * cols), jnp.bfloat16),
    ] + [shape((length, width), part_types(first))] * 2
    inputs = [*slots, vectors, *docs, table, *weights[0], *weights[1], *carried]
    in_specs = (
        [fixed((length, width))] * 2
        + [fixed(vectors.shape)]
        + [moving((1, length, 1), first), moving((1, 1, length), first)]
        + [moving((length, table.shape[1]), first)]
        + anywhere(4 + len(carried))
    )
    out_specs = [moving((length, s.shape[1]), first) for s in shapes[:4]]
    out_specs += [fixed((length, width))] * 2
    scratch = [
        pltpu.VMEM((length, width), jnp.bfloat16),
        pltpu.VMEM((2,) + weights[0][0].shape, jnp.bfloat16),
        pltpu.VMEM((2,) + weights[0][1].shape, jnp.bfloat16),
        pltpu.SemaphoreType.DMA((2, 2)),
    ]
    aliases = {len(inputs) - len(carried) + i: i for i in range(len(carried))}

    def kernel(*refs):
        forward_kernel(first, *refs)

    return run_kernel(
        kernel,
        "attention_forward",
        2,
        inputs,
        in_specs,
        shapes,
        out_specs,
        scratch,
        aliases,
        later,
    )


def attention_backward(
    first, slots, tokens, weights, docs, table, kept, sums, carried, later=()
):
    length, width = slots[0].shape
    cols, count = weights[0][1].shape[0], len(slots)
    shape = jax.ShapeDtypeStruct
    shapes = [shape((4 * length, 3 * cols), jnp.bfloat16), shape(sums.shape, jnp.float32)]
    shapes += [shape((length, 3 * cols), jnp.bfloat16)] * count
    shapes += [shape((length, width), part_types(first))] * count
    inputs = [*slots, *tokens, *docs, table, *kept, sums, *weights[0], *weights[1], *carried]
    in_specs = (
        [fixed((length, width))] * (2 * count)
        + [moving((1, length, 1), first), moving((1, 1, length), first)]
        + [moving((length, table.shape[1]), first)]
        + [moving((length, k.shape[1]), first) for k in kept]
        + [fixed(sums.shape)]
        + anywhere(4 + len(carried))
    )
    out_specs = [moving((length, 3 * cols), first)] + [fixed(s.shape) for s in shapes[1:]]
    scratch = [pltpu.VMEM((length, width), jnp.bfloat16)] * 2 + [
        pltpu.VMEM((2,) + weights[0][0].shape, jnp.bfloat16),
        pltpu.VMEM((2,) + weights[0][1].shape, jnp.bfloat16),
        pltpu.SemaphoreType.DMA((2, 2)),
    ]

    def kernel(*refs):
        backward_kernel(count, *refs)

    return run_kernel(
        kernel,
        "attention_backward",
        count,
        inputs,
        in_specs,
        shapes,
        out_specs,
        scratch,
        {len(inputs) - len(carried): 0} if carried else {},
        later,
    )


def token_product(pairs, rows, cols, later=(), extra=None, us=None):
    by_rows, step = rows % 512 == 0, 512
    if extra is not None:
        step = rows * EXTRA_ROWS // extra.shape[0]
    grid = (rows if by_rows else cols) // step

    def fixed_columns(length, size, window):
        return pl.BlockSpec((length, size), lambda i: (0, window))

    def step_columns(length, window):
        return pl.BlockSpec((length, step), lambda i: (0, window * grid + i))

    sides, inputs, specs = [[], []], [], []
    for pair in pairs:
        for side, (blocks, window) in enumerate(pair):
            for block in blocks:
                sides[side].append((len(inputs), block.shape[0]))
                inputs.append(block)
                if by_rows == (side == 0):
                    specs.append(step_columns(block.shape[0], window))
                else:
                    specs.append(fixed_columns(block.shape[0], (rows, cols)[side], window))
    tokens = sum(length for _, length in sides[0])
    shape, place = (rows, cols), pl.BlockSpec((step, cols), lambda i: (i, 0))
    if not by_rows:
        place = pl.BlockSpec((rows, step), lambda i: (0, i))
    if extra is not None:
        inputs, specs = inputs + [extra], specs + [moving((EXTRA_ROWS, cols), 0)]
        place = moving((step + EXTRA_ROWS, cols), 0)
        shape = (rows + extra.shape[0], cols)

    def kernel(*refs):
        out, left, right = refs[-3:]

        def fill(side, whole):
            start = 0
            for k, length in sides[side]:
                whole[start : start + length, :] = refs[k][...]
                start += length

        moved, kept = (0, 1) if by_rows else (1, 0)
        wholes = (left, right)
        fill(moved, wholes[moved])

        @pl.when(pl.program_id(0) == 0)
        def _():
            fill(kept, wholes[kept])

        total = contract_first(left[...], right[...]).astype(out.dtype)
        if extra is None:
            out[...] = total
        else:
            out[:step, :] = total
            out[step:, :] = refs[-4][...]

    left_cols, right_cols = (step, cols) if by_rows else (rows, step)
    return run_kernel(
        kernel,
        "token_product",
        grid,
        inputs,
        specs,
        jax.ShapeDtypeStruct(shape, jnp.bfloat16),
        place,
        [pltpu.VMEM((tokens, size), jnp.bfloat16) for size in (left_cols, right_cols)],
        {},
        later,
        us,
    )


def spread_columns(half, other, x_index, split, outer, size):
    blocks, rows, cols = half.shape
    width = 8 * outer * size
    outs = len(split(jnp.zeros((8, cols), jnp.float32)))
    step = min(rows, 32)

    def kernel(x_ref, half_ref, other_ref, *out_refs):
        here = x_ref[0]
        for t in range(blocks):
            mine, theirs = half_ref[t].astype(jnp.float32), other_ref[t].astype(jnp.float32)
            for x in range(2):
                columns = split(jnp.where(here == x, mine, theirs))
                for out, values in zip(out_refs, columns):
                    for k in range(outer):
                        start = ((k * blocks + t) * 2 + x) * size
                        out[:, start : start + size] = values[:, k * size : (k + 1) * size]

    block = pl.BlockSpec((blocks, step, cols), lambda i: (0, i, 0))
    return run_kernel(
        kernel,
        "spread_columns",
        rows // step,
        [scalar(x_index), half, other],
        [pl.BlockSpec(memory_space=pltpu.SMEM), block, block],
        [jax.ShapeDtypeStruct((rows, width), jnp.float32)] * outs,
        [pl.BlockSpec((step, width), lambda i: (i, 0))] * outs,
        [],
        {},
    )


def last_tile(values, start):
    tile = values[:, start:]
    return tile, pltpu.roll(tile, HEAD_DIM, 1)


def hidden_kernel(*refs):
    slots, weights, refs = refs[:4], refs[4:6], refs[6:]
    raw, mixed, mixed_there, (place, weight, sems) = refs[0], refs[1], refs[2:6], refs[6:]
    step = pl.program_id(0)
    wait = loader(step, [weights[:1], weights[1:]], [weight], sems)
    pick_slot(step, slots, place)
    cols, hidden = weight.shape[2], mixed.shape[1]
    main = hidden // 128 * 128

    def mix(gate, up):
        return (gate * jax.nn.sigmoid(gate) * up).astype(jnp.bfloat16)

    for which in range(2):
        wait(which)
        both = dot(place[...], weight[which])
        raw[:, which * cols : (which + 1) * cols] = both
        pieces = [mix(both[:, :main], both[:, main : 2 * main])]
        if main < hidden:
            pieces.append(mix(*last_tile(both, 2 * main))[:, : hidden - main])
        low = jnp.concatenate(pieces, 1)
        if which == 0:
            mixed[...] = low
        else:
            put_slot(step, low, mixed_there)


def hidden_back_kernel(*refs):
    slots, raw, refs = refs[:2], refs[2], refs[3:]
    weights = [refs[0:2], refs[2:4]]
    grads, grads_there, outs = refs[-9], refs[-8:-6], refs[-6:-4]
    grad_out, weight, weight_down, sems = refs[-4:]
    step = pl.program_id(0)
    wait = loader(step, weights, [weight, weight_down], sems)
    pick_slot(step, slots, grad_out)
    cols, hidden = weight.shape[2], weight_down.shape[1]
    main = hidden // 128 * 128

    def gradients(gate, up, dm):
        sig = jax.nn.sigmoid(gate)
        return dm * up * sig * (1.0 + gate * (1.0 - sig)), dm * gate * sig

    partial = 0.0
    for which in range(2):
        wait(which)
        dmixed = contract_last(grad_out[...], weight_down[which])
        both = raw[:, which * cols : (which + 1) * cols]
        pieces = list(gradients(both[:, :main], both[:, main : 2 * main], dmixed[:, :main]))
        if main < hidden:
            gate, up = last_tile(both, 2 * main)
            rest = dmixed[:, main:]
            dgate, dup = gradients(gate, up, jnp.concatenate([rest, rest], 1))
            lane = lax.broadcasted_iota(jnp.int32, dgate.shape, 1)
            pieces.append(jnp.where(lane < HEAD_DIM, dgate, pltpu.roll(dup, HEAD_DIM, 1)))
        low = jnp.concatenate(pieces, 1).astype(jnp.bfloat16)
        if which == 0:
            grads[...] = low
        else:
            put_slot(step, low, grads_there)
        partial += contract_last(low, weight[which])
    put_slot(step, partial, outs)


def mlp_forward(slots, weights):
    length, width = slots[0].shape
    both = weights[0].shape[1]
    shape = jax.ShapeDtypeStruct
    shapes = [
        shape((4 * length, 2 * both), jnp.float32),
        shape((4 * length, both // 2), jnp.bfloat16),
    ] + [shape((length, both // 2), jnp.bfloat16)] * 4
    scratch = [
        pltpu.VMEM((length, width), jnp.bfloat16),
        pltpu.VMEM((2,) + weights[0].shape, jnp.bfloat16),
        pltpu.SemaphoreType.DMA((2, 1)),
    ]
    return run_kernel(
        hidden_kernel,
        "mlp_forward",
        4,
        [*slots, *weights],
        [fixed((length, width))] * 4 + anywhere(2),
        shapes,
        [moving((length, s.shape[1]), 0) for s in shapes[:2]] + [fixed(s.shape) for s in shapes[2:]],
        scratch,
        {},
    )


def mlp_backward(first, slots, raw, weights, carried, later=()):
    length, width = slots[0].shape
    both = weights[0][0].shape[1]
    shape = jax.ShapeDtypeStruct
    shapes = [shape((4 * length, both), jnp.bfloat16)]
    shapes += [shape((length, both), jnp.bfloat16)] * 2
    shapes += [shape((length, width), part_types(first))] * 2
    inputs = [*slots, raw, *weights[0], *weights[1], *carried]
    scratch = [
        pltpu.VMEM((length, width), jnp.bfloat16),
        pltpu.VMEM((2,) + weights[0][0].shape, jnp.bfloat16),
        pltpu.VMEM((2,) + weights[0][1].shape, jnp.bfloat16),
        pltpu.SemaphoreType.DMA((2, 2)),
    ]

    def kernel(*refs):
        hidden_back_kernel(*refs[:7], *refs[7 + len(carried) :])

    return run_kernel(
        kernel,
        "mlp_backward",
        2,
        inputs,
        [fixed((length, width))] * 2
        + [moving((length, 2 * both), first)]
        + anywhere(4 + len(carried)),
        shapes,
        [moving((length, both), first)] + [fixed(s.shape) for s in shapes[1:]],
        scratch,
        {7 + i: i for i in range(len(carried))},
        later,
    )


def mlp_output(mixed, mixed_there, weights, later=()):
    hidden, width = weights[0].shape
    length = mixed.shape[0] // 4

    def kernel(*refs):
        slots, outs, (place, weight, sems) = refs[1:5], refs[7:11], refs[11:]
        step = pl.program_id(0)
        wait = loader(step, [refs[5:6], refs[6:7]], [weight], sems)
        pick_slot(step, slots, place)
        partial = 0.0
        for which, values in enumerate((refs[0], place)):
            wait(which)
            partial += dot(values[...], weight[which])
        put_slot(step, partial, outs)

    return run_kernel(
        kernel,
        "mlp_output",
        4,
        [mixed, *mixed_there, *weights],
        [moving((length, hidden), 0)] + [fixed((length, hidden))] * 4 + anywhere(2),
        [jax.ShapeDtypeStruct((length, width), part_types(k)) for k in range(4)],
        [fixed((length, width))] * 4,
        [
            pltpu.VMEM((length, hidden), jnp.bfloat16),
            pltpu.VMEM((2, hidden, width), jnp.bfloat16),
            pltpu.SemaphoreType.DMA((2, 1)),
        ],
        {},
        later,
    )


def scalar(value):
    return value.reshape(1).astype(jnp.int32)


def place_blocks(parts, index):
    length, width = parts[0].shape

    def kernel(index_ref, *refs):
        for k, part in enumerate(refs[:-1]):
            start = pl.multiple_of((index_ref[0] ^ k) * length, length)
            refs[-1][pl.ds(start, length), :] = part[...]

    return run_kernel(
        kernel,
        "place_blocks",
        1,
        [scalar(index), *parts],
        [pl.BlockSpec(memory_space=pltpu.SMEM)] + [fixed((length, width))] * len(parts),
        jax.ShapeDtypeStruct((len(parts) * length, width), parts[0].dtype),
        fixed((len(parts) * length, width)),
        [],
        {},
    )


def split_blocks(values, index, length):
    width = values.shape[1]

    def kernel(index_ref, ref, *outs):
        for k, out in enumerate(outs):
            start = pl.multiple_of((index_ref[0] ^ k) * length, length)
            out[...] = ref[pl.ds(start, length), :]

    return run_kernel(
        kernel,
        "split_blocks",
        1,
        [scalar(index), values],
        [pl.BlockSpec(memory_space=pltpu.SMEM), fixed(values.shape)],
        [jax.ShapeDtypeStruct((length, width), values.dtype)] * 4,
        [fixed((length, width))] * 4,
        [],
        {},
    )


def pick_columns(weights, x_index, yc_index, outer, size, merge):
    rows, width = weights[0].shape
    cols = merge(*([jnp.zeros((8, outer * size), jnp.float32)] * len(weights))).shape[1]
    step, kind = min(rows, 32), weights[0].dtype

    def kernel(x_ref, yc_ref, *refs):
        sources, outs, stage = refs[: len(weights)], refs[len(weights) : -1], refs[-1]
        here = x_ref[0]
        for t in range(4):
            picked = []
            for source in sources:
                pieces = []
                for k in range(outer):
                    start = (k * 4 + t) * 2 * size
                    both = source[:, start : start + 2 * size].astype(jnp.float32)
                    pieces.append(jnp.where(here == 0, both[:, :size], both[:, size:]))
                picked.append(jnp.concatenate(pieces, 1))
            stage[t ^ yc_ref[0]] = merge(*picked).astype(kind)
        for k, out in enumerate(outs):
            out[...] = stage[k]

    return run_kernel(
        kernel,
        "pick_columns",
        rows // step,
        [scalar(x_index), scalar(yc_index), *weights],
        [pl.BlockSpec(memory_space=pltpu.SMEM)] * 2 + [moving((step, width), 0)] * len(weights),
        [jax.ShapeDtypeStruct((rows, cols), kind)] * 4,
        [moving((step, cols), 0)] * 4,
        [pltpu.VMEM((4, step, cols), kind)],
        {},
    )


def unpack_vectors(packed, shards, x_index, yc_index, outer, size):
    rows = packed.shape[1]
    width, cols = rows * shards, outer * size

    def kernel(x_ref, yc_ref, ref, out, whole, stage):
        for shard in range(shards):
            for k in range(7):
                line = jnp.broadcast_to(ref[shard * 8 + k : shard * 8 + k + 1, :], (8, rows))
                if k < 4:
                    start = k * width + shard * rows
                    out[:, start : start + rows] = line
                else:
                    start = (3 * shard + k - 4) * rows
                    whole[:, start : start + rows] = line
        for t in range(4):
            pieces = []
            for k in range(outer):
                start = (k * 4 + t) * 2 * size
                both = whole[:, start : start + 2 * size]
                pieces.append(jnp.where(x_ref[0] == 0, both[:, :size], both[:, size:]))
            stage[t ^ yc_ref[0]] = jnp.concatenate(pieces, 1)
        for k in range(2):
            start = 4 * width + k * cols
            out[:, start : start + cols] = stage[k]

    shape = (8, 4 * width + 2 * cols)
    return run_kernel(
        kernel,
        "unpack_vectors",
        1,
        [scalar(x_index), scalar(yc_index), packed],
        [pl.BlockSpec(memory_space=pltpu.SMEM)] * 2 + [fixed(packed.shape)],
        jax.ShapeDtypeStruct(shape, jnp.float32),
        fixed(shape),
        [pltpu.VMEM((8, 3 * width), jnp.float32), pltpu.VMEM((4, 8, cols), jnp.float32)],
        {},
    )


def gather_z(values):
    return lax.all_gather(values, "z", axis=0, tiled=True)


def scatter_z(values):
    return lax.psum_scatter(values, "z", scatter_dimension=0, tiled=True)


def per_device(
    tokens,
    doc_ids,
    cotangent,
    ln1_gain,
    ln1_bias,
    w_qkv,
    b_qkv,
    w_out,
    ln2_gain,
    ln2_bias,
    w_gate,
    w_up,
    w_down,
):
    x_index, z_index = lax.axis_index("x"), lax.axis_index("z")
    y_index, c_index = lax.axis_index("y"), lax.axis_index("c")
    yc_index = 2 * y_index + c_index
    planes = lax.axis_size("z")
    shards = 4 * planes
    rows = w_qkv.shape[0]
    width = rows * shards
    hidden_dim = w_gate.shape[1]
    piece = hidden_dim // (2 * shards)
    mlp = piece * planes
    head_cols = width // 8
    spread = rows % (2 * HEAD_DIM) == 0
    groups = planes if spread else 1
    unit = head_cols // groups
    length = tokens.shape[0]

    def pick_x(values, axis):
        return lax.dynamic_index_in_dim(values, x_index, axis, keepdims=False)

    def pick_yc(values, axis):
        return lax.dynamic_index_in_dim(values, yc_index, axis, keepdims=False)

    def plane_rows(blocks, later=()):
        return place_blocks(exchange(blocks, later), yc_index)

    main = mlp // 128 * 128

    def pair(gate, up):
        return jnp.concatenate([gate[:, :main], up[:, :main], gate[:, main:], up[:, main:]], 1)

    def unpair(both):
        rest = both[..., 2 * main :]
        return (
            jnp.concatenate([both[..., :main], rest[..., : mlp - main]], -1),
            jnp.concatenate([both[..., main : 2 * main], rest[..., mlp - main :]], -1),
        )

    blocks = pick_columns([w_qkv], x_index, yc_index, 3 * groups, unit, lambda v: v)
    block_qkv = plane_rows(blocks)
    lines = [v[None] for v in (ln1_gain, ln1_bias, ln2_gain, ln2_bias)]
    lines += [b_qkv.reshape(3, rows), jnp.zeros((1, rows), jnp.bfloat16)]
    packed = after(jnp.concatenate(lines, 0).astype(jnp.float32), blocks[1])
    packed = gather_direct(gather_direct(packed, ("y", "c"), 4), "z", planes)
    if spread:
        full_out = gather_z(pick_x(w_out.reshape(2, rows // 2, width), 0))
    else:
        full_out = lax.all_gather(w_out, ("z", "y", "c"), axis=0, tiled=True)
        full_out = pick_x(pick_yc(full_out.reshape(4, 2, unit, width), 0), 0)
    docs = jnp.stack(plane_gather(doc_ids))
    full_qkv = gather_z(after(block_qkv, full_out))
    token_slots = plane_gather(after(tokens, block_qkv))
    blocks = pick_columns([w_gate, w_up], x_index, yc_index, planes, piece, pair)
    block_both = plane_rows(blocks, (*token_slots[1:3], packed, docs))
    full_both = gather_z(block_both)
    full_down = gather_z(pick_x(w_down.reshape(2, piece, width), 0))

    vectors = unpack_vectors(packed, shards, x_index, yc_index, 3 * groups, unit)
    indices = jnp.arange(length, dtype=jnp.int32)
    same_doc = docs[:, :, None] == docs[:, None, :]
    first_row = jnp.min(jnp.where(same_doc, indices[None, None, :], length), axis=2)
    table = spread_rotary((indices[None] - first_row).reshape(-1))
    docs = (docs[:, :, None], docs[:, None, :])

    full_qkv = after(full_qkv, full_out, block_both, *token_slots[1:], table, *docs, vectors)
    weights = list(zip(with_sibling(full_qkv), with_sibling(full_out)))
    cot_late = after(cotangent, block_both)
    cot_near, cot_side = swap(cot_late, FIRST), swap(cot_late, SECOND)
    *carried, side_part, far_part = attention_forward(
        2, token_slots[2:], vectors, weights, docs, table, ()
    )
    normed_low, proj, lse, attended_low, own_part, near_part = attention_forward(
        0, token_slots[:2], vectors, weights, docs, table, carried, (cot_near, cot_side)
    )
    _, parts = plane_sum(own_part, near_part, side_part, far_part)
    hidden, normed_two = norm_forward(tokens, parts, vectors)

    two_slots = plane_gather(normed_two)
    both_weights = with_sibling(after(full_both, two_slots[3]))
    cot_far = swap(after(cot_near, two_slots[3]), SECOND)
    raw, mixed, *mixed_there = mlp_forward(two_slots, both_weights)
    cot_far = after(cot_far, raw)
    cot_slots = [cotangent, cot_near, cot_side, cot_far]
    def across(blocks):
        return [swap(block, SIBLING) for block in blocks]

    pairs = [(([mixed], 0), (cot_slots, 0)), ((across(mixed_there), 0), (across(cot_slots), 0))]
    down_grad = token_product(pairs, mlp, width)
    down_sum = scatter_z(down_grad)
    down_weights = with_sibling(after(full_down, down_grad))
    mlp_weights = list(zip(both_weights, down_weights))
    both_grads, *far_grads, side_part, far_part = mlp_backward(
        2, cot_slots[2:], raw, mlp_weights, (), (down_grad,)
    )
    both_grads, *near_grads, own_part, near_part = mlp_backward(
        0, cot_slots[:2], raw, mlp_weights, (both_grads,)
    )
    near_low, parts = plane_sum(own_part, near_part, side_part, far_part)
    pairs = [
        ((two_slots, 0), ([both_grads], 0)),
        ((across(two_slots), 0), (across([*near_grads, *far_grads]), 0)),
    ]
    both_grad = token_product(pairs, width, 2 * mlp, (near_low,))
    both_sum = scatter_z(both_grad)
    def whole_rows(half):
        other = swap(half, ACROSS_X)
        odd = x_index == 1
        return jnp.concatenate(
            [jnp.where(odd, other, half), jnp.where(odd, half, other)], 0
        ).astype(jnp.float32)

    grad_hidden, hidden_low, norm_sums = norm_backward(
        hidden, cotangent, parts, vectors, 1, True, (both_grad,)
    )
    near_hidden = swap(hidden_low, FIRST)
    out_parts = mlp_output(mixed, mixed_there, down_weights, (hidden_low,))

    near_hidden = after(near_hidden, out_parts[0])
    side_hidden = swap(after(hidden_low, near_hidden), SECOND)
    far_hidden = swap(near_hidden, SECOND)
    hidden_slots = [hidden_low, near_hidden, side_hidden, far_hidden]
    sums = jnp.zeros((1, 2 * width + 6 * head_cols), jnp.float32)
    common = (weights, docs, table, (proj, lse))
    grad_proj, sums, *near_proj, own_part, near_part = attention_backward(
        0, hidden_slots[:2], token_slots[:2], *common, sums, (), (out_parts[0],)
    )
    done = (own_part, *hidden_slots[2:])
    out_parts = [*out_parts[:2], *(after(part, *done) for part in out_parts[2:])]
    out_near, out_sum = plane_sum(*out_parts)
    grad_proj, sums, *far_proj, side_part, far_part = attention_backward(
        2, hidden_slots[2:], token_slots[2:], *common, sums, (grad_proj,)
    )

    placed = jnp.zeros((3 * groups, 4, 2, unit), jnp.float32)
    for k in range(2):
        piece_sum = sums[0, 2 * width + 3 * head_cols * k :][: 3 * head_cols]
        placed = lax.dynamic_update_slice(
            placed,
            piece_sum.reshape(3 * groups, 1, 1, unit),
            (0, yc_index ^ k, x_index, 0),
        )
    lines = [v[0, i * width : (i + 1) * width] for v in (sums, norm_sums) for i in range(2)]
    lines = [v.reshape(planes, 4, rows) for v in lines] + [placed.reshape(planes, 4, 3 * rows)]
    extra = jnp.concatenate(lines, 2).reshape(planes, 28 * rows)
    extra = jnp.pad(extra, ((0, 0), (0, EXTRA_ROWS * 3 * head_cols - 28 * rows)))
    extra = extra.reshape(planes * EXTRA_ROWS, 3 * head_cols).astype(jnp.bfloat16)
    pairs = [
        (([normed_low], 0), ([grad_proj], 0)),
        ((across([normed_low]), 0), (across([*near_proj, *far_proj]), 0)),
    ]
    qkv_grad = token_product(pairs, width, 3 * head_cols, (out_near,), extra)
    qkv_sum = scatter_z(qkv_grad)
    own, side, near = (part.astype(jnp.float32) for part in out_sum)
    activations = (hidden + (own + side + near)).astype(jnp.bfloat16)
    far_part, side_part = (after(part, qkv_grad) for part in (far_part, side_part))
    norm_near, parts = plane_sum(own_part, near_part, side_part, far_part)
    (d_tokens,) = norm_backward(tokens, grad_hidden, parts, vectors, 0, False)
    def whole_columns(summed):
        half = plane_rows(split_blocks(summed, yc_index, rows))
        other = swap(half, ACROSS_X)
        return [v.reshape(4, rows, summed.shape[1]) for v in (half, other)]

    owned_down = whole_rows(after(down_sum, out_near))
    gate_half, other = whole_columns(after(both_sum, owned_down))
    def out_product(window, later):
        pairs = [(([attended_low], window), (hidden_slots, 0))]
        return token_product(pairs, head_cols, width, later, us=40)

    out_there = swap(out_product(1, (gate_half, norm_near)), SIBLING)
    out_grad = out_product(0, ()).astype(jnp.float32) + out_there.astype(jnp.float32)
    out_grad = out_grad.astype(jnp.bfloat16)

    if spread:
        owned_out = whole_rows(scatter_z(out_grad))
    else:
        placed_out = lax.dynamic_update_slice(
            jnp.zeros((4, 2, unit, width), jnp.bfloat16),
            out_grad[None, None],
            (yc_index, x_index, 0, 0),
        )
        owned_out = lax.psum_scatter(
            placed_out.reshape(width, width), ("z", "y", "c"), scatter_dimension=0, tiled=True
        )
        owned_out = lax.psum(owned_out, "x").astype(jnp.float32)

    owned_gate, owned_up = spread_columns(gate_half, other, x_index, unpair, planes, piece)
    small = qkv_sum[4 * rows :].reshape(-1)[: 28 * rows].reshape(4, 7 * rows).astype(jnp.float32)
    for axis in ("c", "y", "x"):
        small = small + meet(small, axis, 1, 2)
    small = pick_yc(small, 0)
    half, other = whole_columns(after(qkv_sum, other, parts[2], out_sum[2]))
    (owned_qkv,) = spread_columns(half, other, x_index, lambda v: (v,), 3 * groups, unit)

    return (
        activations,
        d_tokens,
        small[:rows],
        small[rows : 2 * rows],
        owned_qkv,
        small[4 * rows :],
        owned_out,
        small[2 * rows : 3 * rows],
        small[3 * rows : 4 * rows],
        owned_gate,
        owned_up,
        owned_down,
    )


def solution(mesh):
    reps, shards = mesh.shape["rep"], mesh.shape["shard"]
    grid = Mesh(mesh.devices.reshape(reps, shards // 4, 2, 2), EVERY)
    tokens, rows, vector = P(EVERY, None), P(("z", "y", "c"), None), P(("z", "y", "c"))
    return jax.shard_map(
        per_device,
        mesh=grid,
        in_specs=(
            tokens,
            P(EVERY),
            tokens,
            vector,
            vector,
            rows,
            vector,
            rows,
            vector,
            vector,
            rows,
            rows,
            rows,
        ),
        out_specs=(
            tokens,
            tokens,
            vector,
            vector,
            rows,
            vector,
            rows,
            vector,
            vector,
            rows,
            rows,
            rows,
        ),
        check_vma=False,
    )
```

time: 726 us -> 635 us (0.87)
  Pallas kernels: 155 us -> 230 us
  waiting for transfers between devices: 281 us -> 220 us
  matrix products: 57.7 us -> 0 us
  other arithmetic: 56.8 us -> 33.6 us
  local copies, waits for them, and re-layouts: 85.8 us -> 70.4 us
    pallas_call x8 -> x29, Pallas kernels: 155 us -> 230 us  [run_kernel(): pl.pallas_call(used, grid=(blocks,), out_shape=shapes, in_specs=anywhere(...]
    dot_general x8 -> x0, matrix products: 57.7 us -> none  [the longest x6 48.5 us: contract_first(): lax.dot_general(left, right, (((0,), (0,)), ((), ())), preferred_element_...]
    ppermute x12 -> x9, waiting for transfers between devices: 45.7 us -> 3.89 us  [meet(): return lax.ppermute(values, axis, [(i, i ^ bit) for i in range(size)])]
    unnamed x183 -> x240, local copies, waits for them, and re-layouts: 36.7 us -> 61.7 us
    convert_element_type x5 -> x2, local copies, waits for them, and re-layouts: 16.2 us -> 0.06 us  [the longest x1 0.05 us: per_device(): extra.reshape(planes * EXTRA_ROWS, 3 * head_cols).astype(jnp.bfloat16)]
    select_n x13 -> x1, other arithmetic: 13.6 us -> 3.07 us  [spread_rotary(): from_right = jnp.where(lane < half_rot, -sine, 0.0)]
    ppermute x51 -> x69, waiting for transfers between devices: 203 us -> 192 us  [swap(): return lax.ppermute(values, PLANE, pairs)]
    ppermute x12 -> x9, starting transfers between devices: 17.2 us -> 7.03 us  [meet(): return lax.ppermute(values, axis, [(i, i ^ bit) for i in range(size)])]
  transfers between devices with their start and end apart: 70 -> 86, of which waited for: 32 -> 38; matrix products, arithmetic and copies ran while one was open for 24% -> 7% of each run, Pallas kernels for 19% -> 37%
where the time goes in v3:
time: 635 us; the launch traced here: 629 us
  Pallas kernels  230 us (36%)
  waiting for transfers between devices  220 us (35%)
  local copies, waits for them, and re-layouts  70.4 us (11%)
  starting transfers between devices  59.2 us (9%)
  other arithmetic  33.6 us (5%)
  between operations  15.3 us (2%)
    pallas_call x29, Pallas kernels, run_kernel(): pl.pallas_call(used, grid=(blocks,), out_shape=shapes, in_specs=anywhere(...  230 us
    ppermute x69, waiting for transfers between devices, swap(): return lax.ppermute(values, PLANE, pairs)  192 us
    unnamed x240, local copies, waits for them, and re-layouts  61.7 us
    ppermute x69, starting transfers between devices, swap(): return lax.ppermute(values, PLANE, pairs)  51.2 us
    all_gather x4, waiting for transfers between devices, gather_z(): return lax.all_gather(values, 'z', axis=0, tiled=True)  23.9 us
  transfers between devices with their start and end apart: 86, of which 38 were waited for; matrix products, arithmetic and copies ran while one was open for 7% of the time, Pallas kernels for 37%

profile of v3, /device:TPU:0, one launch (start us, length us, event | category | flops | bytes accessed | tf_op | source)
XLA Modules:
  0.0 628.9 jit_solution(13851311229765070515)
XLA Ops:
  12.6 2.6 collective-permute-start.1
  16.2 4.7 collective-permute-done.1.refs_2_
  20.9 3.7 collective-permute-done.2.refs_3_
  25.6 15.2 %all-gather.11.cloned.1.call-done = bf16[1,256,2048]{2,1,0:T(8,128)(2,1)} async-done(((bf16[1,64,2048]{2,1,0:T(8,128)(2,1)}), bf16[1,256,2048]{2,1,0:T(8,128)(2,1)}) %all-gather.11.cloned.1.call-update) | async-done | bytes 1048592 | tf_op jit(solution)/shard_map/all_gather | solution.py:916
  50.3 3.3 pick_columns.2
  57.1 10.2 %collective-permute-done.11.refs_0_ = s32[256]{0:T(256)} collective-permute-done((s32[256]{0:T(256)}, s32[256]{0:T(256)}, u32[]{:S(2)}, u32[]{:S(2)}) %collective-permute-start.11) | collective-permute-done | bytes 1056 | tf_op jit(solution)/shard_map/ppermute | solution.py:49
  88.3 3.1 fusion.2
  96.4 3.4 collective-permute-done.15.refs_2_
  99.8 5.7 collective-permute-done.16.refs_3_
  115.1 15.0 %attention_forward.2 = (bf16[1024,2048]{1,0:T(8,128)(2,1)}, bf16[1024,1536]{1,0:T(8,128)(2,1)}, f32[1024,128]{1,0:T(8,128)S(1)}, bf16[1024,512]{1,0:T(8,128)(2,1...) custom-call(bf16[256,2048]{1,0:T(8,128)(2,1)S(1)} %copy-done.3, ...), custom_call_target="tpu_custom_call" | custom-call | flops 17251000320 | bytes 1024 | tf_op jit(solution)/shard_map/attention_forward/pallas_call | solution.py:417
  132.1 3.0 collective-permute-done.17.refs_0_.refs_2_.refs_1_
  135.4 16.8 %attention_forward.3 = (bf16[1024,2048]{1,0:T(8,128)(2,1)}, bf16[1024,1536]{1,0:T(8,128)(2,1)}, f32[1024,128]{1,0:T(8,128)S(1)}, bf16[1024,512]{1,0:T(8,128)(2,1...) custom-call(bf16[256,2048]{1,0:T(8,128)(2,1)S(1)} %collective-permut, ...), custom_call_target="tpu_custom_call", output_to_operand_aliasing={{0}: (12, {}), {1}: (13, {}), {2}: (14, {}), {3}: (15, {})} | custom-call | flops 17251000320 | bytes 1024 | tf_op jit(solution)/shard_map/attention_forward/pallas_call | solution.py:417
  152.2 5.6 collective-permute-done.23
  157.9 2.8 add_convert_fusion.5.refs_0_
  163.2 13.5 %collective-permute-done.24.near = bf16[256,2048]{1,0:T(8,128)(2,1)S(1)} collective-permute-done((bf16[256,2048]{1,0:T(8,128)(2,1)}, bf16[256,2048]{1,0:T(8,128)(2,1)S(1)}, u32[]{:S(2)}, u32[]{:S(2)}) %collective-permute-start.24) | collective-permute-done | bytes 1048608 | tf_op jit(solution)/shard_map/ppermute | solution.py:49
  179.2 4.2 norm_forward.1
  187.3 22.2 %collective-permute-done.25.refs_0_ = bf16[256,2048]{1,0:T(8,128)(2,1)} collective-permute-done((bf16[256,2048]{1,0:T(8,128)(2,1)S(1)}, bf16[256,2048]{1,0:T(8,128)(2,1)}, u32[]{:S(2)}, u32[]{:S(2)}) %collective-permute-start.25) | collective-permute-done | bytes 1048608 | tf_op jit(solution)/shard_map/ppermute | solution.py:49
  211.3 3.5 all-gather.9.cloned.1.call-done.refs_0_
  214.8 10.7 %collective-permute-done.27.refs_1_.refs_3_.refs_4_ = bf16[256,2048]{1,0:T(8,128)(2,1)S(1)} collective-permute-done((bf16[256,2048]{1,0:T(8,128)(2,1)}, bf16[256,2048]{1,0:T(8,128)(2,1)S(1)}, u32[]{:S(2)}, u32[]{:S(2)}) %collective-permute-start.27) | collective-permute-done | bytes 1048608 | tf_op jit(solution)/shard_map/ppermute | solution.py:49
  230.7 7.1 %collective-permute-done.28.refs_5_.refs_6_ = bf16[2048,1408]{1,0:T(8,128)(2,1)} collective-permute-done((bf16[2048,1408]{1,0:T(8,128)(2,1)}, bf16[2048,1408]{1,0:T(8,128)(2,1)}, u32[]{:S(2)}, u32[]{:S(2)}) %collective-permute-start.28) | collective-permute-done | bytes 5767200 | tf_op jit(solution)/shard_map/ppermute | solution.py:49
  239.0 21.0 %mlp_forward.1 = (f32[1024,2816]{1,0:T(8,128)}, bf16[1024,704]{1,0:T(8,128)(2,1)}, bf16[256,704]{1,0:T(8,128)(2,1)S(1)}, bf16[256,704]{1,0:T(8,128)(2,1)S(1)}, b...) custom-call(bf16[256,2048]{1,0:T(8,128)(2,1)S(1)} %copy-done.71, bf16[256,2048]{1,0:T(8,128)(2,1)} %after.39.refs_1_.refs_2_, ...), custom_call_target="tpu_custom_call" | custom-call | flops 24150999040 | bytes 1024 | tf_op jit(solution)/shard_map/mlp_forward/pallas_call | solution.py:417
  270.8 10.5 %token_product.5.refs_1_.refs_0_ = bf16[704,2048]{1,0:T(8,128)(2,1)} custom-call(bf16[1024,704]{1,0:T(8,128)(2,1)} %get-tuple-element.98.refs_0_.refs_1_, bf16[256,2048]{1,0:T(8,128)(2,1)S(1)} %copy-done.36, bf16[256,2048]{1,0:T(8,128)(2,1)S(1)} %copy-done.47, bf16[256,2048]{1,0:T(8,128)(2,1)S(1)} %copy-done.75, bf16[256,2048]{1,0:T(8,128)(2,1)} %after.42.refs_4_.refs_2_, ...), custom_call_target="tpu_custom_call" | custom-call | flops 16101000192 | bytes 1024 | tf_op jit(solution)/shard_map/token_product/pallas_call | solution.py:417
  281.3 4.6 all-gather.13.cloned.1.call-done
  288.2 3.3 collective-permute-done.38.refs_7_.refs_6_
  292.8 22.1 %mlp_backward.2 = (bf16[1024,1408]{1,0:T(8,128)(2,1)}, bf16[256,1408]{1,0:T(8,128)(2,1)}, bf16[256,1408]{1,0:T(8,128)(2,1)}, bf16[256,2048]{1,0:T(8,128)(2,1)S(1)}, bf16[256,2048]{1,0:T(8,128)(2,1)S(1)}) custom-call(bf16[704,2048]{1,0:T(8,128)(2,1)} %token_product.5.refs_1_.refs_0_, bf16[256,2048]{1,0:T(8,128)(2,1)S(1)} %copy-done.76, ...), custom_call_target="tpu_custom_call" | custom-call | flops 24150999040 | bytes 1024 | tf_op jit(solution)/shard_map/mlp_backward/pallas_call | solution.py:417
  317.0 22.3 %mlp_backward.3 = (bf16[1024,1408]{1,0:T(8,128)(2,1)}, bf16[256,1408]{1,0:T(8,128)(2,1)}, bf16[256,1408]{1,0:T(8,128)(2,1)}, f32[256,2048]{1,0:T(8,128)S(1)}, f32[256,2048]{1,0:T(8,128)}) custom-call(bf16[256,2048]{1,0:T(8,128)(2,1)S(1)} %copy-done.37, bf16[256,2048]{1,0:T(8,128)(2,1)S(1)} %copy-done.48, ...), custom_call_target="tpu_custom_call", output_to_operand_aliasing={{0}: (7, {})} | custom-call | flops 24150999040 | bytes 1024 | tf_op jit(solution)/shard_map/mlp_backward/pallas_call | solution.py:417
  341.7 2.9 add_convert_fusion.4.refs_0_
  347.5 19.4 %token_product.6.refs_0_ = bf16[2048,1408]{1,0:T(8,128)(2,1)} custom-call(bf16[256,2048]{1,0:T(8,128)(2,1)S(1)} %copy-done.13, bf16[256,2048]{1,0:T(8,128)(2,1)S(1)} %copy-done.73, bf16[256,2048]{1,0:T(8,128)(2,1)} %after.39.refs_1_.refs_2_, bf16[256,2048]{1,0:T(8,128)(2,1)} %copy-done.24, bf16[256,2048]{1,0:T(8,128)(2,1)} %copy-done.8, ...), custom_call_target="tpu_custom_call" | custom-call | flops 16101000192 | bytes 1024 | tf_op jit(solution)/shard_map/token_product/pallas_call | solution.py:417
  369.7 13.2 %collective-permute-done.49.refs_5_ = bf16[256,2048]{1,0:T(8,128)(2,1)} collective-permute-done((bf16[256,2048]{1,0:T(8,128)(2,1)S(1)}, bf16[256,2048]{1,0:T(8,128)(2,1)}, u32[]{:S(2)}, u32[]{:S(2)}) %collective-permute-start.49) | collective-permute-done | bytes 1048608 | tf_op jit(solution)/shard_map/ppermute | solution.py:49
  383.0 5.2 norm_backward.2
  391.0 14.2 %mlp_output.1 = (f32[256,2048]{1,0:T(8,128)}, f32[256,2048]{1,0:T(8,128)}, bf16[256,2048]{1,0:T(8,128)(2,1)S(1)}, bf16[256,2048]{1,0:T(8,128)(2,1)S(1)}) custom-call(bf16[256,2048]{1,0:T(8,128)(2,1)S(1)} %get-tuple-element.113.refs_0_.refs_1_.refs_3_, bf16[1024,704]{1,0:T(8,128)(2,1)} %get-tuple-element.98.refs_0_.refs_1_, bf16[256,704]{1,0:T(8,128)(2,1)S(1)} %copy-done.78, ...), custom_call_target="tpu_custom_call" | custom-call | flops 14951000064 | bytes 1024 | tf_op jit(solution)/shard_map/mlp_output/pallas_call | solution.py:417
  413.6 19.0 %attention_backward.2 = (bf16[1024,768]{1,0:T(8,128)(2,1)}, f32[1,5632]{1,0:T(1,128)S(1)}, bf16[256,768]{1,0:T(8,128)(2,1)}, bf16[256,768]{1,0:T(8,128)(2,1)}, f32[256,2048]{1,0:T(8,128)}, /*index=5*/f32[256,2048]{1,0:T(8,128)}) custom-call(f32[256,2048]{1,0:T(8,128)} %get-tuple-element.114.refs_1_.refs_0_, bf16[256,2048]{1,0:T(8,128)(2,1)S(1)} %copy-done.43, ...), custom_call_target="tpu_custom_call" | custom-call | flops 20700999680 | bytes 1024 | tf_op jit(solution)/shard_map/attention_backward/pallas_call | solution.py:417
  442.2 17.9 %attention_backward.3 = (bf16[1024,768]{1,0:T(8,128)(2,1)}, f32[1,5632]{1,0:T(1,128)S(1)}, bf16[256,768]{1,0:T(8,128)(2,1)S(1)}, bf16[256,768]{1,0:T(8,128)(2,1)...) custom-call(bf16[256,2048]{1,0:T(8,128)(2,1)S(1)} %copy-done.18, ...), custom_call_target="tpu_custom_call", output_to_operand_aliasing={{0}: (14, {})} | custom-call | flops 20700999680 | bytes 1024 | tf_op jit(solution)/shard_map/attention_backward/pallas_call | solution.py:417
  464.1 3.1 add_convert_fusion.3.refs_0_
  469.9 10.8 %token_product.7.refs_1_ = bf16[2112,768]{1,0:T(8,128)(2,1)} custom-call(bf16[256,2048]{1,0:T(8,128)(2,1)S(1)} %copy-done.6, bf16[1024,2048]{1,0:T(8,128)(2,1)} %get-tuple-element.125.refs_1_, bf16[1024,768]{1,0:T(8,128)(2,1)S(1)} %copy-done.94, bf16[1024,2048]{1,0:T(8,128)(2,1)} %collective-permute-done.56.refs_3_, ...), custom_call_target="tpu_custom_call" | custom-call | flops 16101000192 | bytes 1024 | tf_op jit(solution)/shard_map/token_product/pallas_call | solution.py:417
  483.8 2.8 collective-permute-done.67
  493.8 13.2 %collective-permute-done.62 = bf16[256,2048]{1,0:T(8,128)(2,1)} collective-permute-done((bf16[256,2048]{1,0:T(8,128)(2,1)}, bf16[256,2048]{1,0:T(8,128)(2,1)}, u32[]{:S(2)}, u32[]{:S(2)}) %collective-permute-start.62) | collective-permute-done | bytes 1048608 | tf_op jit(solution)/shard_map/ppermute | solution.py:49
  510.1 15.4 %collective-permute-done.61.refs_1_.side = bf16[256,2048]{1,0:T(8,128)(2,1)S(1)} collective-permute-done((bf16[256,2048]{1,0:T(8,128)(2,1)}, bf16[256,2048]{1,0:T(8,128)(2,1)S(1)}, u32[]{:S(2)}, u32[]{:S(2)}) %collective-permute-start.61) | collective-permute-done | bytes 1048608 | tf_op jit(solution)/shard_map/ppermute | solution.py:49
  536.9 5.0 token_product.9
  543.7 3.8 token_product.8
  550.3 2.9 add_convert_fusion
  553.3 4.4 add_convert_fusion.2
  558.5 23.2 %collective-permute-done.63.near.refs_2_ = bf16[256,2048]{1,0:T(8,128)(2,1)S(1)} collective-permute-done((bf16[256,2048]{1,0:T(8,128)(2,1)S(1)}, bf16[256,2048]{1,0:T(8,128)(2,1)S(1)}, u32[]{:S(2)}, u32[]{:S(2)}) %collective-permute-start.63) | collective-permute-done | bytes 1048608 | tf_op jit(solution)/shard_map/ppermute | solution.py:49
  586.0 4.6 norm_backward.3
  592.5 2.7 collective-permute-done.74.refs_3_
  597.6 5.5 spread_columns.3
  604.0 11.7 %collective-permute-done.75 = bf16[512,768]{1,0:T(8,128)(2,1)S(1)} collective-permute-done((bf16[512,768]{1,0:T(8,128)(2,1)S(1)}, bf16[512,768]{1,0:T(8,128)(2,1)S(1)}, u32[]{:S(2)}, u32[]{:S(2)}) %collective-permute-start.75) | collective-permute-done | bytes 786464 | tf_op jit(solution)/shard_map/ppermute | solution.py:49
  615.7 2.7 spread_columns.2
  (480 shorter events, 169.8 us)
Async XLA Ops:
  7.2 33.6 %all-gather.11.cloned.1.call-start = ((), (), s32[]{:S(2)}) async-start(), calls=%async_computation.10 | async-start | bytes 1310720 | tf_op jit(solution)/shard_map/all_gather | solution.py:916
  25.6 81.8 %all-gather.7.cloned.1.call-start = ((), (), s32[]{:S(2)}) async-start(), calls=%async_computation.4 | async-start | bytes 3932160 | tf_op jit(solution)/shard_map/all_gather | solution.py:916
  40.9 173.9 %all-gather.9.cloned.1.call-start = ((), (), s32[]{:S(2)}) async-start(), calls=%async_computation.5 | async-start | bytes 7208960 | tf_op jit(solution)/shard_map/all_gather | solution.py:916
  40.9 33.1 %collective-permute-start.3 = (bf16[256,2048]{1,0:T(8,128)(2,1)}, bf16[256,2048]{1,0:T(8,128)(2,1)S(1)}, u32[]{:S(2)}, u32[]{:S(2)}) collective-permute-start(bf16[256,2048]{1,0:T(8,128)(2,1)} %after.28.refs_2_.refs_3_), channel_id=1, source_target_pairs={{0,16},{1,3},{2,18},{3,1},{16,0},{17,19},{18,2},{19,17},{4,20},{5,... | collective-permute-start | bytes 3145736 | tf_op jit(solution)/shard_map/ppermute | solution.py:49
  42.4 31.5 %collective-permute-start.4 = (bf16[256,2048]{1,0:T(8,128)(2,1)}, bf16[256,2048]{1,0:T(8,128)(2,1)S(1)}, u32[]{:S(2)}, u32[]{:S(2)}) collective-permute-start(bf16[256,2048]{1,0:T(8,128)(2,1)} %after.28.refs_2_.refs_3_), channel_id=1, source_target_pairs={{0,2},{1,17},{2,0},{3,19},{16,18},{17,1},{18,16},{19,3},{4,6},{5,2... | collective-permute-start | bytes 3145736 | tf_op jit(solution)/shard_map/ppermute | solution.py:49
  43.9 23.3 %collective-permute-start.11 = (s32[256]{0:T(256)}, s32[256]{0:T(256)}, u32[]{:S(2)}, u32[]{:S(2)}) collective-permute-start(s32[256]{0:T(256)} %param.14), channel_id=1, source_target_pairs={{0,16},{1,3},{2,18},{3,1},{16,0},{17,19},{18,2},{19,17},{4,20},{5,... | collective-permute-start | bytes 3080 | tf_op jit(solution)/shard_map/ppermute | solution.py:49
  44.5 23.3 %collective-permute-start.12 = (s32[256]{0:T(256)}, s32[256]{0:T(256)}, u32[]{:S(2)}, u32[]{:S(2)}) collective-permute-start(s32[256]{0:T(256)} %param.14), channel_id=1, source_target_pairs={{0,2},{1,17},{2,0},{3,19},{16,18},{17,1},{18,16},{19,3},{4,6},{5,2... | collective-permute-start | bytes 3080 | tf_op jit(solution)/shard_map/ppermute | solution.py:49
  46.9 30.6 %collective-permute-start.5 = (f32[8,128]{1,0:T(8,128)}, f32[8,128]{1,0:T(8,128)S(1)}, u32[]{:S(2)}, u32[]{:S(2)}) collective-permute-start(f32[8,128]{1,0:T(8,128)} %after.30.refs_0_), channel_id=1, source_target_pairs={{0,1},{1,0},{2,3},{3,2},{4,5},{5,4},{6,7},{7,6},{8,9},{9,8},{10,11... | collective-permute-start | bytes 12296 | tf_op jit(solution)/shard_map/ppermute | solution.py:78
  75.9 30.8 %collective-permute-start.19 = (bf16[256,2048]{1,0:T(8,128)(2,1)}, bf16[256,2048]{1,0:T(8,128)(2,1)}, u32[]{:S(2)}, u32[]{:S(2)}) collective-permute-start(bf16[256,2048]{1,0:T(8,128)(2,1)} %after.29.refs_1_.refs_3_.refs_4_), channel_id=1, source_target_pairs={{0,2},{1,17},{2,0},{3,19},{16,18},{17,1},{18,16},{19,3},{4,6},{5,2... | collective-permute-start | bytes 3145736 | tf_op jit(solution)/shard_map/ppermute | solution.py:49
  107.9 178.0 %all-gather.13.cloned.1.call-start = ((), (), s32[]{:S(2)}) async-start(), calls=%async_computation.11 | async-start | bytes 3604480 | tf_op jit(solution)/shard_map/all_gather | solution.py:916
  109.5 25.6 %collective-permute-start.17 = (bf16[256,2048]{1,0:T(8,128)(2,1)}, bf16[256,2048]{1,0:T(8,128)(2,1)S(1)}, u32[]{:S(2)}, u32[]{:S(2)}) collective-permute-start(bf16[256,2048]{1,0:T(8,128)(2,1)} %after.35), channel_id=1, source_target_pairs={{0,16},{1,3},{2,18},{3,1},{16,0},{17,19},{18,2},{19,17},{4,20},{5,... | collective-permute-start | bytes 3145736 | tf_op jit(solution)/shard_map/ppermute | solution.py:49
  111.1 24.3 %collective-permute-start.18 = (bf16[256,2048]{1,0:T(8,128)(2,1)}, bf16[256,2048]{1,0:T(8,128)(2,1)S(1)}, u32[]{:S(2)}, u32[]{:S(2)}) collective-permute-start(bf16[256,2048]{1,0:T(8,128)(2,1)} %after.35), channel_id=1, source_target_pairs={{0,2},{1,17},{2,0},{3,19},{16,18},{17,1},{18,16},{19,3},{4,6},{5,2... | collective-permute-start | bytes 3145736 | tf_op jit(solution)/shard_map/ppermute | solution.py:49
  130.0 30.7 %collective-permute-start.22 = (bf16[256,2048]{1,0:T(8,128)(2,1)S(1)}, bf16[256,2048]{1,0:T(8,128)(2,1)S(1)}, u32[]{:S(2)}, u32[]{:S(2)}) collective-permute-start(bf16[256,2048]{1,0:T(8,128)(2,1)S(1)} %get-tuple-element.92), channel_id=1, source_target_pairs={{0,2},{1,17},{2,0},{3,19},{16,18},{17,1},{18,16},{19,3},{4,6},{5,2... | collective-permute-start | bytes 3145736 | tf_op jit(solution)/shard_map/ppermute | solution.py:49
  131.6 26.3 %collective-permute-start.23 = (bf16[256,2048]{1,0:T(8,128)(2,1)S(1)}, bf16[256,2048]{1,0:T(8,128)(2,1)S(1)}, u32[]{:S(2)}, u32[]{:S(2)}) collective-permute-start(bf16[256,2048]{1,0:T(8,128)(2,1)S(1)} %get-tuple-element.94), channel_id=1, source_target_pairs={{0,2},{1,17},{2,0},{3,19},{16,18},{17,1},{18,16},{19,3},{4,6},{5,2... | collective-permute-start | bytes 3145736 | tf_op jit(solution)/shard_map/ppermute | solution.py:49
  183.4 26.1 %collective-permute-start.25 = (bf16[256,2048]{1,0:T(8,128)(2,1)S(1)}, bf16[256,2048]{1,0:T(8,128)(2,1)}, u32[]{:S(2)}, u32[]{:S(2)}) collective-permute-start(bf16[256,2048]{1,0:T(8,128)(2,1)S(1)} %get-tuple-element.96.refs_0_.refs_1_), channel_id=1, source_target_pairs={{0,16},{1,3},{2,18},{3,1},{16,0},{17,19},{18,2},{19,17},{4,20},{5,... | collective-permute-start | bytes 3145736 | tf_op jit(solution)/shard_map/ppermute | solution.py:49
  184.8 24.7 %collective-permute-start.26 = (bf16[256,2048]{1,0:T(8,128)(2,1)S(1)}, bf16[256,2048]{1,0:T(8,128)(2,1)S(1)}, u32[]{:S(2)}, u32[]{:S(2)}) collective-permute-start(bf16[256,2048]{1,0:T(8,128)(2,1)S(1)} %get-tuple-element.96.refs_0_.refs_1_), channel_id=1, source_target_pairs={{0,2},{1,17},{2,0},{3,19},{16,18},{17,1},{18,16},{19,3},{4,6},{5,2... | collective-permute-start | bytes 3145736 | tf_op jit(solution)/shard_map/ppermute | solution.py:49
  226.5 36.7 %collective-permute-start.34 = (bf16[256,2048]{1,0:T(8,128)(2,1)S(1)}, bf16[256,2048]{1,0:T(8,128)(2,1)}, u32[]{:S(2)}, u32[]{:S(2)}) collective-permute-start(bf16[256,2048]{1,0:T(8,128)(2,1)S(1)} %copy-done.36), channel_id=1, source_target_pairs={{0,1},{1,0},{2,3},{3,2},{16,17},{17,16},{18,19},{19,18},{4,5},{5,4... | collective-permute-start | bytes 3145736 | tf_op jit(solution)/shard_map/ppermute | solution.py:49
  228.0 239.3 %reduce-scatter.9.cloned.1.call-start = ((), (), s32[]{:S(2)}) async-start(), calls=%async_computation.8 | async-start | bytes 3604480 | tf_op jit(solution)/shard_map/reduce_scatter | solution.py:920
  229.4 34.2 %collective-permute-start.35 = (bf16[256,2048]{1,0:T(8,128)(2,1)}, bf16[256,2048]{1,0:T(8,128)(2,1)}, u32[]{:S(2)}, u32[]{:S(2)}) collective-permute-start(bf16[256,2048]{1,0:T(8,128)(2,1)} %copy-done.45), channel_id=1, source_target_pairs={{0,1},{1,0},{2,3},{3,2},{16,17},{17,16},{18,19},{19,18},{4,5},{5,4... | collective-permute-start | bytes 3145736 | tf_op jit(solution)/shard_map/ppermute | solution.py:49
  229.5 34.2 %collective-permute-start.36 = (bf16[256,2048]{1,0:T(8,128)(2,1)}, bf16[256,2048]{1,0:T(8,128)(2,1)}, u32[]{:S(2)}, u32[]{:S(2)}) collective-permute-start(bf16[256,2048]{1,0:T(8,128)(2,1)} %copy-done.74), channel_id=1, source_target_pairs={{0,1},{1,0},{2,3},{3,2},{16,17},{17,16},{18,19},{19,18},{4,5},{5,4... | collective-permute-start | bytes 3145736 | tf_op jit(solution)/shard_map/ppermute | solution.py:49
  229.9 32.4 %collective-permute-start.29 = (bf16[256,2048]{1,0:T(8,128)(2,1)}, bf16[256,2048]{1,0:T(8,128)(2,1)}, u32[]{:S(2)}, u32[]{:S(2)}) collective-permute-start(bf16[256,2048]{1,0:T(8,128)(2,1)} %after.41), channel_id=1, source_target_pairs={{0,2},{1,17},{2,0},{3,19},{16,18},{17,1},{18,16},{19,3},{4,6},{5,2... | collective-permute-start | bytes 3145736 | tf_op jit(solution)/shard_map/ppermute | solution.py:49
  287.1 29.5 %collective-permute-start.41 = (bf16[256,2048]{1,0:T(8,128)(2,1)S(1)}, bf16[256,2048]{1,0:T(8,128)(2,1)}, u32[]{:S(2)}, u32[]{:S(2)}) collective-permute-start(bf16[256,2048]{1,0:T(8,128)(2,1)S(1)} %copy-done.72), channel_id=1, source_target_pairs={{0,1},{1,0},{2,3},{3,2},{16,17},{17,16},{18,19},{19,18},{4,5},{5,4... | collective-permute-start | bytes 3145736 | tf_op jit(solution)/shard_map/ppermute | solution.py:49
  287.1 53.5 %collective-permute-start.42 = (bf16[256,2048]{1,0:T(8,128)(2,1)}, bf16[256,2048]{1,0:T(8,128)(2,1)}, u32[]{:S(2)}, u32[]{:S(2)}) collective-permute-start(bf16[256,2048]{1,0:T(8,128)(2,1)} %after.39.refs_1_.refs_2_), channel_id=1, source_target_pairs={{0,1},{1,0},{2,3},{3,2},{16,17},{17,16},{18,19},{19,18},{4,5},{5,4... | collective-permute-start | bytes 3145736 | tf_op jit(solution)/shard_map/ppermute | solution.py:49
  287.6 53.0 %collective-permute-start.43 = (bf16[256,2048]{1,0:T(8,128)(2,1)S(1)}, bf16[256,2048]{1,0:T(8,128)(2,1)}, u32[]{:S(2)}, u32[]{:S(2)}) collective-permute-start(bf16[256,2048]{1,0:T(8,128)(2,1)S(1)} %copy-done.25), channel_id=1, source_target_pairs={{0,1},{1,0},{2,3},{3,2},{16,17},{17,16},{18,19},{19,18},{4,5},{5,4... | collective-permute-start | bytes 3145736 | tf_op jit(solution)/shard_map/ppermute | solution.py:49
  287.6 56.9 %collective-permute-start.44 = (bf16[256,2048]{1,0:T(8,128)(2,1)S(1)}, bf16[256,2048]{1,0:T(8,128)(2,1)}, u32[]{:S(2)}, u32[]{:S(2)}) collective-permute-start(bf16[256,2048]{1,0:T(8,128)(2,1)S(1)} %copy-done.9), channel_id=1, source_target_pairs={{0,1},{1,0},{2,3},{3,2},{16,17},{17,16},{18,19},{19,18},{4,5},{5,4... | collective-permute-start | bytes 3145736 | tf_op jit(solution)/shard_map/ppermute | solution.py:49
  288.2 202.1 %reduce-scatter.7.cloned.1.call-start = ((), (), s32[]{:S(2)}) async-start(), calls=%async_computation.7 | async-start | bytes 7208960 | tf_op jit(solution)/shard_map/reduce_scatter | solution.py:920
  314.9 26.3 %collective-permute-start.39 = (bf16[256,2048]{1,0:T(8,128)(2,1)S(1)}, bf16[256,2048]{1,0:T(8,128)(2,1)S(1)}, u32[]{:S(2)}, u32[]{:S(2)}) collective-permute-start(bf16[256,2048]{1,0:T(8,128)(2,1)S(1)} %get-tuple-element.105), channel_id=1, source_target_pairs={{0,2},{1,17},{2,0},{3,19},{16,18},{17,1},{18,16},{19,3},{4,6},{5,2... | collective-permute-start | bytes 3145736 | tf_op jit(solution)/shard_map/ppermute | solution.py:49
  316.6 24.6 %collective-permute-start.40 = (bf16[256,2048]{1,0:T(8,128)(2,1)S(1)}, bf16[256,2048]{1,0:T(8,128)(2,1)S(1)}, u32[]{:S(2)}, u32[]{:S(2)}) collective-permute-start(bf16[256,2048]{1,0:T(8,128)(2,1)S(1)} %get-tuple-element.106), channel_id=1, source_target_pairs={{0,2},{1,17},{2,0},{3,19},{16,18},{17,1},{18,16},{19,3},{4,6},{5,2... | collective-permute-start | bytes 3145736 | tf_op jit(solution)/shard_map/ppermute | solution.py:49
  366.9 182.5 %reduce-scatter.5.cloned.1.call-start = ((), (), s32[]{:S(2)}) async-start(), calls=%async_computation.6 | async-start | bytes 4055040 | tf_op jit(solution)/shard_map/reduce_scatter | solution.py:920
  369.7 97.5 %collective-permute-start.56 = (bf16[1024,2048]{1,0:T(8,128)(2,1)}, bf16[1024,2048]{1,0:T(8,128)(2,1)}, u32[]{:S(2)}, u32[]{:S(2)}) collective-permute-start(bf16[1024,2048]{1,0:T(8,128)(2,1)} %get-tuple-element.125.refs_1_), channel_id=1, source_target_pairs={{0,1},{1,0},{2,3},{3,2},{16,17},{17,16},{18,19},{19,18},{4,5},{5,4... | collective-permute-start | bytes 12582920 | tf_op jit(solution)/shard_map/ppermute | solution.py:49
  408.2 26.2 %collective-permute-start.52 = (bf16[256,2048]{1,0:T(8,128)(2,1)}, bf16[256,2048]{1,0:T(8,128)(2,1)S(1)}, u32[]{:S(2)}, u32[]{:S(2)}) collective-permute-start(bf16[256,2048]{1,0:T(8,128)(2,1)} %after.45.refs_2_.refs_1_.refs_4_), channel_id=1, source_target_pairs={{0,2},{1,17},{2,0},{3,19},{16,18},{17,1},{18,16},{19,3},{4,6},{5,2... | collective-permute-start | bytes 3145736 | tf_op jit(solution)/shard_map/ppermute | solution.py:49
  409.6 24.8 %collective-permute-start.51 = (bf16[256,2048]{1,0:T(8,128)(2,1)}, bf16[256,2048]{1,0:T(8,128)(2,1)S(1)}, u32[]{:S(2)}, u32[]{:S(2)}) collective-permute-start(bf16[256,2048]{1,0:T(8,128)(2,1)} %after.46), channel_id=1, source_target_pairs={{0,2},{1,17},{2,0},{3,19},{16,18},{17,1},{18,16},{19,3},{4,6},{5,2... | collective-permute-start | bytes 3145736 | tf_op jit(solution)/shard_map/ppermute | solution.py:49
  433.1 35.1 %collective-permute-start.57 = (bf16[256,768]{1,0:T(8,128)(2,1)}, bf16[256,768]{1,0:T(8,128)(2,1)}, u32[]{:S(2)}, u32[]{:S(2)}) collective-permute-start(bf16[256,768]{1,0:T(8,128)(2,1)} %get-tuple-element.127), channel_id=1, source_target_pairs={{0,1},{1,0},{2,3},{3,2},{16,17},{17,16},{18,19},{19,18},{4,5},{5,4... | collective-permute-start | bytes 1179656 | tf_op jit(solution)/shard_map/ppermute | solution.py:49
  433.1 35.1 %collective-permute-start.58 = (bf16[256,768]{1,0:T(8,128)(2,1)}, bf16[256,768]{1,0:T(8,128)(2,1)}, u32[]{:S(2)}, u32[]{:S(2)}) collective-permute-start(bf16[256,768]{1,0:T(8,128)(2,1)} %get-tuple-element.128), channel_id=1, source_target_pairs={{0,1},{1,0},{2,3},{3,2},{16,17},{17,16},{18,19},{19,18},{4,5},{5,4... | collective-permute-start | bytes 1179656 | tf_op jit(solution)/shard_map/ppermute | solution.py:49
  436.3 27.2 %collective-permute-start.54 = (bf16[256,2048]{1,0:T(8,128)(2,1)}, bf16[256,2048]{1,0:T(8,128)(2,1)}, u32[]{:S(2)}, u32[]{:S(2)}) collective-permute-start(bf16[256,2048]{1,0:T(8,128)(2,1)} %after.48), channel_id=1, source_target_pairs={{0,2},{1,17},{2,0},{3,19},{16,18},{17,1},{18,16},{19,3},{4,6},{5,2... | collective-permute-start | bytes 3145736 | tf_op jit(solution)/shard_map/ppermute | solution.py:49
  437.8 25.8 %collective-permute-start.53 = (bf16[256,2048]{1,0:T(8,128)(2,1)}, bf16[256,2048]{1,0:T(8,128)(2,1)}, u32[]{:S(2)}, u32[]{:S(2)}) collective-permute-start(bf16[256,2048]{1,0:T(8,128)(2,1)} %after.47), channel_id=1, source_target_pairs={{0,2},{1,17},{2,0},{3,19},{16,18},{17,1},{18,16},{19,3},{4,6},{5,2... | collective-permute-start | bytes 3145736 | tf_op jit(solution)/shard_map/ppermute | solution.py:49
  467.2 19.4 %collective-permute-start.67 = (bf16[176,2048]{1,0:T(8,128)(2,1)}, bf16[176,2048]{1,0:T(8,128)(2,1)}, u32[]{:S(2)}, u32[]{:S(2)}) collective-permute-start(bf16[176,2048]{1,0:T(8,128)(2,1)} %after.53), channel_id=1, source_target_pairs={{0,16},{1,17},{2,18},{3,19},{16,0},{17,1},{18,2},{19,3},{4,20},{5,... | collective-permute-start | bytes 2162696 | tf_op jit(solution)/shard_map/ppermute | solution.py:49
  480.7 26.3 %collective-permute-start.62 = (bf16[256,2048]{1,0:T(8,128)(2,1)}, bf16[256,2048]{1,0:T(8,128)(2,1)}, u32[]{:S(2)}, u32[]{:S(2)}) collective-permute-start(bf16[256,2048]{1,0:T(8,128)(2,1)} %after.51), channel_id=1, source_target_pairs={{0,2},{1,17},{2,0},{3,19},{16,18},{17,1},{18,16},{19,3},{4,6},{5,2... | collective-permute-start | bytes 3145736 | tf_op jit(solution)/shard_map/ppermute | solution.py:49
  481.3 72.0 %collective-permute-start.55 = (bf16[256,2048]{1,0:T(8,128)(2,1)S(1)}, bf16[256,2048]{1,0:T(8,128)(2,1)}, u32[]{:S(2)}, u32[]{:S(2)}) collective-permute-start(bf16[256,2048]{1,0:T(8,128)(2,1)S(1)} %copy-done.6), channel_id=1, source_target_pairs={{0,16},{1,3},{2,18},{3,1},{16,0},{17,19},{18,2},{19,17},{4,20},{5,... | collective-permute-start | bytes 3145736 | tf_op jit(solution)/shard_map/ppermute | solution.py:49
  482.2 43.3 %collective-permute-start.61 = (bf16[256,2048]{1,0:T(8,128)(2,1)}, bf16[256,2048]{1,0:T(8,128)(2,1)S(1)}, u32[]{:S(2)}, u32[]{:S(2)}) collective-permute-start(bf16[256,2048]{1,0:T(8,128)(2,1)} %after.50), channel_id=1, source_target_pairs={{0,2},{1,17},{2,0},{3,19},{16,18},{17,1},{18,16},{19,3},{4,6},{5,2... | collective-permute-start | bytes 3145736 | tf_op jit(solution)/shard_map/ppermute | solution.py:49
  483.7 119.4 %reduce-scatter.11.cloned.1.call-start = ((), (), s32[]{:S(2)}) async-start(), calls=%async_computation.9 | async-start | bytes 1310720 | tf_op jit(solution)/shard_map/reduce_scatter | solution.py:920
  493.6 32.9 %collective-permute-start.68 = (bf16[128,1408]{1,0:T(8,128)(2,1)}, bf16[128,1408]{1,0:T(8,128)(2,1)S(1)}, u32[]{:S(2)}, u32[]{:S(2)}) collective-permute-start(bf16[128,1408]{1,0:T(8,128)(2,1)} %get-tuple-element.136), channel_id=1, source_target_pairs={{0,1},{1,0},{2,3},{3,2},{16,17},{17,16},{18,19},{19,18},{4,5},{5,4... | collective-permute-start | bytes 1081352 | tf_op jit(solution)/shard_map/ppermute | solution.py:49
  493.6 35.9 %collective-permute-start.69 = (bf16[128,1408]{1,0:T(8,128)(2,1)}, bf16[128,1408]{1,0:T(8,128)(2,1)}, u32[]{:S(2)}, u32[]{:S(2)}) collective-permute-start(bf16[128,1408]{1,0:T(8,128)(2,1)} %get-tuple-element.137), channel_id=1, source_target_pairs={{0,2},{1,3},{2,0},{3,1},{16,18},{17,19},{18,16},{19,17},{4,6},{5,7... | collective-permute-start | bytes 1081352 | tf_op jit(solution)/shard_map/ppermute | solution.py:49
  507.0 24.4 %collective-permute-start.70 = (bf16[128,1408]{1,0:T(8,128)(2,1)}, bf16[128,1408]{1,0:T(8,128)(2,1)}, u32[]{:S(2)}, u32[]{:S(2)}) collective-permute-start(bf16[128,1408]{1,0:T(8,128)(2,1)} %get-tuple-element.138), channel_id=1, source_target_pairs={{0,3},{1,2},{2,1},{3,0},{16,19},{17,18},{18,17},{19,16},{4,7},{5,6... | collective-permute-start | bytes 1081352 | tf_op jit(solution)/shard_map/ppermute | solution.py:49
  535.8 45.9 %collective-permute-start.71 = (bf16[512,1408]{1,0:T(8,128)(2,1)}, bf16[512,1408]{1,0:T(8,128)(2,1)}, u32[]{:S(2)}, u32[]{:S(2)}) collective-permute-start(bf16[512,1408]{1,0:T(8,128)(2,1)} %place_blocks.10), channel_id=1, source_target_pairs={{0,16},{1,17},{2,18},{3,19},{16,0},{17,1},{18,2},{19,3},{4,20},{5,... | collective-permute-start | bytes 4325384 | tf_op jit(solution)/shard_map/ppermute | solution.py:49
  548.5 33.3 %collective-permute-start.63 = (bf16[256,2048]{1,0:T(8,128)(2,1)S(1)}, bf16[256,2048]{1,0:T(8,128)(2,1)S(1)}, u32[]{:S(2)}, u32[]{:S(2)}) collective-permute-start(bf16[256,2048]{1,0:T(8,128)(2,1)S(1)} %copy-done.12), channel_id=1, source_target_pairs={{0,16},{1,3},{2,18},{3,1},{16,0},{17,19},{18,2},{19,17},{4,20},{5,... | collective-permute-start | bytes 3145736 | tf_op jit(solution)/shard_map/ppermute | solution.py:49
  557.6 33.0 %collective-permute-start.65 = (f32[4,896]{1,0:T(4,128)S(1)}, f32[4,896]{1,0:T(4,128)}, u32[]{:S(2)}, u32[]{:S(2)}) collective-permute-start(f32[4,896]{1,0:T(4,128)S(1)} %add.89), channel_id=1, source_target_pairs={{0,2},{2,0},{1,3},{3,1},{4,6},{6,4},{5,7},{7,5},{8,10},{10,8},{9,1... | collective-permute-start | bytes 43016 | tf_op jit(solution)/shard_map/ppermute | solution.py:78
  595.3 20.4 %collective-permute-start.75 = (bf16[512,768]{1,0:T(8,128)(2,1)S(1)}, bf16[512,768]{1,0:T(8,128)(2,1)S(1)}, u32[]{:S(2)}, u32[]{:S(2)}) collective-permute-start(bf16[512,768]{1,0:T(8,128)(2,1)S(1)} %place_blocks.11), channel_id=1, source_target_pairs={{0,16},{1,17},{2,18},{3,19},{16,0},{17,1},{18,2},{19,3},{4,20},{5,... | collective-permute-start | bytes 2359304 | tf_op jit(solution)/shard_map/ppermute | solution.py:49
  (153 other events, 1027.6 us)
Sparse Core Ops, SparseCore 0:
  10.2 30.6 all-gather.10
  43.0 64.3 all-gather.6
  109.5 105.2 all-gather.8
  228.1 57.7 all-gather.12
  288.6 54.8 reduce-scatter.8
  367.0 101.0 reduce-scatter.6
  483.8 59.1 reduce-scatter.4
  553.4 24.5 reduce-scatter.10

commit v4 on v3

--- a/solution.py
+++ b/solution.py
@@ -19,10 +19,10 @@
 EXTRA_ROWS = 16
 MICROSECONDS = {
     "attention_forward": 15,
-    "attention_backward": 18,
-    "mlp_forward": 21,
+    "attention_backward": 27,
+    "mlp_forward": 8,
     "mlp_backward": 21,
-    "mlp_output": 13,
+    "mlp_output": 18,
     "token_product": 14,
     "norm_forward": 5,
     "norm_backward": 5,
@@ -188,24 +188,20 @@
             slot[...] = value.astype(slot.dtype)
 
 
-def loader(step, sources, places, sems):
-    def copies(which):
-        return [
-            pltpu.make_async_copy(sources[which][k], places[k].at[which], sems.at[which, k])
-            for k in range(len(places))
-        ]
+def loader(step, sources, places, sems, order=(0,)):
+    def fetch(which, k):
+        return pltpu.make_async_copy(sources[which][k], places[k].at[which], sems.at[which, k])
 
     @pl.when(step == 0)
     def _():
         for which in range(2):
-            for copy in copies(which):
-                copy.start()
-
-    def wait(which):
+            for k in order:
+                fetch(which, k).start()
+
+    def wait(which, k=0):
         @pl.when(step == 0)
         def _():
-            for copy in copies(which):
-                copy.wait()
+            fetch(which, k).wait()
 
     return wait
 
@@ -217,7 +213,7 @@
     outs, (place, weight, weight_out, sems) = refs[-10:-4], refs[-4:]
     normed, proj, lse, attended = outs[:4]
     step = pl.program_id(0)
-    wait = loader(step, weights, [weight, weight_out], sems)
+    wait = loader(step, weights, [weight, weight_out], sems, (0, 1))
     pick_slot(step, slots, place)
     width = normed.shape[1]
     gain, bias = vectors[:1, :width], vectors[:1, width : 2 * width]
@@ -255,6 +251,7 @@
             logs = jnp.where(lane == heads * which + head, part, logs)
         low_joined = joined.astype(jnp.bfloat16)
         attended[:, cols * which : cols * (which + 1)] = low_joined
+        wait(which, 1)
         partial += dot(low_joined, weight_out[which])
     lse[...] = logs
     put_slot(step, partial, outs[4:])
@@ -267,7 +264,7 @@
     outs, (place, inputs, weight, weight_out, sems) = refs[-7 - 2 * count : -5], refs[-5:]
     dproj, sums, dproj_there = outs[0], outs[1], outs[2 : 2 + count]
     step = pl.program_id(0)
-    wait = loader(step, weights, [weight, weight_out], sems)
+    wait = loader(step, weights, [weight, weight_out], sems, (1, 0))
     pick_slot(step, slots, place)
     pick_slot(step, tokens, inputs)
 
@@ -283,7 +280,7 @@
     width = grad.shape[1]
     dnorm = 0.0
     for which in range(2):
-        wait(which)
+        wait(which, 1)
         datt = contract_last(grad, weight_out[which]).astype(jnp.bfloat16)
         start = 3 * cols * which
         query, key, value = (
@@ -307,6 +304,7 @@
             dproj[...] = low
         else:
             put_slot(step, low, dproj_there)
+        wait(which)
         dnorm += contract_last(low, weight[which])
         start += 2 * width
         sums[:, start : start + 3 * cols] += jnp.sum(low.astype(jnp.float32), 0, keepdims=True)
@@ -428,14 +426,14 @@
     )(*later, *inputs)
 
 
-def after(value, *others):
+def after(value, *others, us=0):
     return pl.pallas_call(
         lambda *refs: None,
         out_shape=jax.ShapeDtypeStruct(value.shape, value.dtype),
         in_specs=anywhere(1 + len(others)),
         out_specs=pl.BlockSpec(memory_space=pl.ANY),
         input_output_aliases={0: 0},
-        cost_estimate=cost("after"),
+        cost_estimate=cost_of(us),
         name="after",
     )(value, *others)
 
@@ -670,7 +668,7 @@
     grads, grads_there, outs = refs[-9], refs[-8:-6], refs[-6:-4]
     grad_out, weight, weight_down, sems = refs[-4:]
     step = pl.program_id(0)
-    wait = loader(step, weights, [weight, weight_down], sems)
+    wait = loader(step, weights, [weight, weight_down], sems, (1, 0))
     pick_slot(step, slots, grad_out)
     cols, hidden = weight.shape[2], weight_down.shape[1]
     main = hidden // 128 * 128
@@ -681,7 +679,7 @@
 
     partial = 0.0
     for which in range(2):
-        wait(which)
+        wait(which, 1)
         dmixed = contract_last(grad_out[...], weight_down[which])
         both = raw[:, which * cols : (which + 1) * cols]
         pieces = list(gradients(both[:, :main], both[:, main : 2 * main], dmixed[:, :main]))
@@ -696,6 +694,7 @@
             grads[...] = low
         else:
             put_slot(step, low, grads_there)
+        wait(which)
         partial += contract_last(low, weight[which])
     put_slot(step, partial, outs)
 
@@ -1012,7 +1011,7 @@
     hidden, normed_two = norm_forward(tokens, parts, vectors)
 
     two_slots = plane_gather(normed_two)
-    both_weights = with_sibling(after(full_both, two_slots[3]))
+    both_weights = with_sibling(after(full_both, two_slots[1]))
     cot_far = swap(after(cot_near, two_slots[3]), SECOND)
     raw, mixed, *mixed_there = mlp_forward(two_slots, both_weights)
     cot_far = after(cot_far, raw)
@@ -1021,7 +1020,7 @@
         return [swap(block, SIBLING) for block in blocks]
 
     pairs = [(([mixed], 0), (cot_slots, 0)), ((across(mixed_there), 0), (across(cot_slots), 0))]
-    down_grad = token_product(pairs, mlp, width)
+    down_grad = token_product(pairs, mlp, width, us=10)
     down_sum = scatter_z(down_grad)
     down_weights = with_sibling(after(full_down, down_grad))
     mlp_weights = list(zip(both_weights, down_weights))
@@ -1036,7 +1035,7 @@
         ((two_slots, 0), ([both_grads], 0)),
         ((across(two_slots), 0), (across([*near_grads, *far_grads]), 0)),
     ]
-    both_grad = token_product(pairs, width, 2 * mlp, (near_low,))
+    both_grad = token_product(pairs, width, 2 * mlp, (near_low,), us=25)
     both_sum = scatter_z(both_grad)
     def whole_rows(half):
         other = swap(half, ACROSS_X)
@@ -1097,12 +1096,12 @@
         return [v.reshape(4, rows, summed.shape[1]) for v in (half, other)]
 
     owned_down = whole_rows(after(down_sum, out_near))
-    gate_half, other = whole_columns(after(both_sum, owned_down))
+    gate_half, other = whole_columns(both_sum)
     def out_product(window, later):
         pairs = [(([attended_low], window), (hidden_slots, 0))]
         return token_product(pairs, head_cols, width, later, us=40)
 
-    out_there = swap(out_product(1, (gate_half, norm_near)), SIBLING)
+    out_there = swap(out_product(1, (gate_half, norm_near, owned_down)), SIBLING)
     out_grad = out_product(0, ()).astype(jnp.float32) + out_there.astype(jnp.float32)
     out_grad = out_grad.astype(jnp.bfloat16)
 

time: 635 us -> 608 us (0.957)
  waiting for transfers between devices: 220 us -> 200 us
    ppermute x69, waiting for transfers between devices: 192 us -> 176 us  [swap(): return lax.ppermute(values, PLANE, pairs)]
    unnamed x240 -> x228, local copies, waits for them, and re-layouts: 61.7 us -> 58.5 us
  transfers between devices with their start and end apart: 86 -> 86, of which waited for: 38 -> 35; matrix products, arithmetic and copies ran while one was open for 7% -> 7% of each run, Pallas kernels for 37% -> 37%
where the time goes in v4:
time: 608 us; the launch traced here: 602 us
  Pallas kernels  225 us (37%)
  waiting for transfers between devices  200 us (33%)
  local copies, waits for them, and re-layouts  67.2 us (11%)
  starting transfers between devices  60.9 us (10%)
  other arithmetic  33.3 us (5%)
  between operations  15.2 us (2%)
    pallas_call x29, Pallas kernels, run_kernel(): pl.pallas_call(used, grid=(blocks,), out_shape=shapes, in_specs=anywhere(...  225 us
    ppermute x69, waiting for transfers between devices, swap(): return lax.ppermute(values, PLANE, pairs)  176 us
    unnamed x228, local copies, waits for them, and re-layouts  58.5 us
    ppermute x69, starting transfers between devices, swap(): return lax.ppermute(values, PLANE, pairs)  53.1 us
    all_gather x4, waiting for transfers between devices, gather_z(): return lax.all_gather(values, 'z', axis=0, tiled=True)  19.3 us
  transfers between devices with their start and end apart: 86, of which 35 were waited for; matrix products, arithmetic and copies ran while one was open for 7% of the time, Pallas kernels for 37%

profile of v4, /device:TPU:0, one launch (start us, length us, event | category | flops | bytes accessed | tf_op | source)
XLA Modules:
  0.0 601.7 jit_solution(5660114987954368180)
XLA Ops:
  12.6 2.6 collective-permute-start.1
  16.2 4.7 collective-permute-done.1.refs_2_
  20.9 3.7 collective-permute-done.2.refs_3_
  25.6 15.2 %all-gather.11.cloned.1.call-done = bf16[1,256,2048]{2,1,0:T(8,128)(2,1)} async-done(((bf16[1,64,2048]{2,1,0:T(8,128)(2,1)}), bf16[1,256,2048]{2,1,0:T(8,128)(2,1)}) %all-gather.11.cloned.1.call-update) | async-done | bytes 1048592 | tf_op jit(solution)/shard_map/all_gather | solution.py:915
  50.3 3.3 pick_columns.2
  57.1 10.2 %collective-permute-done.11.refs_0_ = s32[256]{0:T(256)} collective-permute-done((s32[256]{0:T(256)}, s32[256]{0:T(256)}, u32[]{:S(2)}, u32[]{:S(2)}) %collective-permute-start.11) | collective-permute-done | bytes 1056 | tf_op jit(solution)/shard_map/ppermute | solution.py:49
  88.3 3.1 fusion.2
  93.0 2.5 pad_maximum_fusion.refs_6_.refs_5_.refs_7_
  96.4 3.4 collective-permute-done.15.refs_2_
  99.8 5.7 collective-permute-done.16.refs_3_
  112.6 2.5 collective-permute-done.21.refs_9_.refs_11_.refs_14_.refs_13_
  115.1 14.8 %attention_forward.2 = (bf16[1024,2048]{1,0:T(8,128)(2,1)}, bf16[1024,1536]{1,0:T(8,128)(2,1)}, f32[1024,128]{1,0:T(8,128)S(1)}, bf16[1024,512]{1,0:T(8,128)(2,1...) custom-call(bf16[256,2048]{1,0:T(8,128)(2,1)S(1)} %copy-done.3, ...), custom_call_target="tpu_custom_call" | custom-call | flops 17251000320 | bytes 1024 | tf_op jit(solution)/shard_map/attention_forward/pallas_call | solution.py:415
  132.0 3.2 collective-permute-done.17.refs_0_.refs_2_.refs_1_
  135.4 16.7 %attention_forward.3 = (bf16[1024,2048]{1,0:T(8,128)(2,1)}, bf16[1024,1536]{1,0:T(8,128)(2,1)}, f32[1024,128]{1,0:T(8,128)S(1)}, bf16[1024,512]{1,0:T(8,128)(2,1...) custom-call(bf16[256,2048]{1,0:T(8,128)(2,1)S(1)} %collective-permut, ...), custom_call_target="tpu_custom_call", output_to_operand_aliasing={{0}: (12, {}), {1}: (13, {}), {2}: (14, {}), {3}: (15, {})} | custom-call | flops 17251000320 | bytes 1024 | tf_op jit(solution)/shard_map/attention_forward/pallas_call | solution.py:415
  152.2 5.7 collective-permute-done.23
  157.9 2.8 add_convert_fusion.5.refs_0_
  163.2 13.5 %collective-permute-done.24.near = bf16[256,2048]{1,0:T(8,128)(2,1)S(1)} collective-permute-done((bf16[256,2048]{1,0:T(8,128)(2,1)}, bf16[256,2048]{1,0:T(8,128)(2,1)S(1)}, u32[]{:S(2)}, u32[]{:S(2)}) %collective-permute-start.24) | collective-permute-done | bytes 1048608 | tf_op jit(solution)/shard_map/ppermute | solution.py:49
  179.2 4.2 norm_forward.1
  187.3 22.1 %collective-permute-done.25.refs_0_ = bf16[256,2048]{1,0:T(8,128)(2,1)S(1)} collective-permute-done((bf16[256,2048]{1,0:T(8,128)(2,1)S(1)}, bf16[256,2048]{1,0:T(8,128)(2,1)S(1)}, u32[]{:S(2)}, u32[]{:S(2)}) %collective-permute-start.25) | collective-permute-done | bytes 1048608 | tf_op jit(solution)/shard_map/ppermute | solution.py:49
  211.3 3.5 all-gather.9.cloned.1.call-done.refs_0_
  218.8 12.5 %collective-permute-done.27.refs_3_.refs_1_.refs_4_ = bf16[256,2048]{1,0:T(8,128)(2,1)} collective-permute-done((bf16[256,2048]{1,0:T(8,128)(2,1)S(1)}, bf16[256,2048]{1,0:T(8,128)(2,1)}, u32[]{:S(2)}, u32[]{:S(2)}) %collective-permute-start.27) | collective-permute-done | bytes 1048608 | tf_op jit(solution)/shard_map/ppermute | solution.py:49
  234.5 21.1 %mlp_forward.1 = (f32[1024,2816]{1,0:T(8,128)}, bf16[1024,704]{1,0:T(8,128)(2,1)}, bf16[256,704]{1,0:T(8,128)(2,1)S(1)}, bf16[256,704]{1,0:T(8,128)(2,1)S(1)}, b...) custom-call(bf16[256,2048]{1,0:T(8,128)(2,1)S(1)} %copy-done.66, bf16[256,2048]{1,0:T(8,128)(2,1)S(1)} %copy-done.9, ...), custom_call_target="tpu_custom_call" | custom-call | flops 9201000448 | bytes 1024 | tf_op jit(solution)/shard_map/mlp_forward/pallas_call | solution.py:415
  266.5 10.5 %token_product.5.refs_1_.refs_0_ = bf16[704,2048]{1,0:T(8,128)(2,1)} custom-call(bf16[1024,704]{1,0:T(8,128)(2,1)} %get-tuple-element.98.refs_0_.refs_1_, bf16[256,2048]{1,0:T(8,128)(2,1)S(1)} %copy-done.32, bf16[256,2048]{1,0:T(8,128)(2,1)S(1)} %copy-done.41, bf16[256,2048]{1,0:T(8,128)(2,1)S(1)} %copy-done.69, bf16[256,2048]{1,0:T(8,128)(2,1)} %after.41.refs_4_.refs_2_, ...), custom_call_target="tpu_custom_call" | custom-call | flops 11500999680 | bytes 1024 | tf_op jit(solution)/shard_map/token_product/pallas_call | solution.py:415
  278.5 4.1 collective-permute-done.38.refs_7_.refs_6_
  283.9 20.3 %mlp_backward.2 = (bf16[1024,1408]{1,0:T(8,128)(2,1)}, bf16[256,1408]{1,0:T(8,128)(2,1)}, bf16[256,1408]{1,0:T(8,128)(2,1)}, bf16[256,2048]{1,0:T(8,128)(2,1)S(1)}, bf16[256,2048]{1,0:T(8,128)(2,1)S(1)}) custom-call(bf16[704,2048]{1,0:T(8,128)(2,1)} %token_product.5.refs_1_.refs_0_, bf16[256,2048]{1,0:T(8,128)(2,1)S(1)} %copy-done.70, ...), custom_call_target="tpu_custom_call" | custom-call | flops 24150999040 | bytes 1024 | tf_op jit(solution)/shard_map/mlp_backward/pallas_call | solution.py:415
  306.3 20.8 %mlp_backward.3 = (bf16[1024,1408]{1,0:T(8,128)(2,1)}, bf16[256,1408]{1,0:T(8,128)(2,1)}, bf16[256,1408]{1,0:T(8,128)(2,1)}, f32[256,2048]{1,0:T(8,128)S(1)}, f32[256,2048]{1,0:T(8,128)}) custom-call(bf16[256,2048]{1,0:T(8,128)(2,1)S(1)} %copy-done.32, bf16[256,2048]{1,0:T(8,128)(2,1)S(1)} %copy-done.42, ...), custom_call_target="tpu_custom_call", output_to_operand_aliasing={{0}: (7, {})} | custom-call | flops 24150999040 | bytes 1024 | tf_op jit(solution)/shard_map/mlp_backward/pallas_call | solution.py:415
  330.4 2.9 add_convert_fusion.4.refs_0_
  336.0 19.4 %token_product.6.refs_0_ = bf16[2048,1408]{1,0:T(8,128)(2,1)} custom-call(bf16[256,2048]{1,0:T(8,128)(2,1)S(1)} %copy-done.13, bf16[256,2048]{1,0:T(8,128)(2,1)S(1)} %copy-done.67, bf16[256,2048]{1,0:T(8,128)(2,1)S(1)} %copy-done.9, bf16[256,2048]{1,0:T(8,128)(2,1)} %copy-done.22, bf16[256,2048]{1,0:T(8,128)(2,1)} %collective-permute-done.27.refs_3_.refs_1_.refs_4_, ...), custom_call_target="tpu_custom_call" | custom-call | flops 28750999552 | bytes 1024 | tf_op jit(solution)/shard_map/token_product/pallas_call | solution.py:415
  356.4 6.2 %norm_backward.2 = (f32[256,2048]{1,0:T(8,128)}, bf16[256,2048]{1,0:T(8,128)(2,1)S(1)}, f32[1,4096]{1,0:T(1,128)S(1)}) custom-call(bf16[2048,1408]{1,0:T(8,128)(2,1)} %token_product.6.refs_0_, f32[256,2048]{1,0:T(8,128)} %get-tuple-element.95.refs_1_, bf16[256,2048]{1,0:T(8,128)(2,1)S(1)} %copy-done.32, f32[256,2048]{1,0:T(8,128)} %copy-done.87, ...), custom_call_target="tpu_custom_call" | custom-call | flops 5751000064 | bytes 1024 | tf_op jit(solution)/shard_map/norm_backward/pallas_call | solution.py:415
  364.6 14.2 %mlp_output.1 = (f32[256,2048]{1,0:T(8,128)}, f32[256,2048]{1,0:T(8,128)}, bf16[256,2048]{1,0:T(8,128)(2,1)S(1)}, bf16[256,2048]{1,0:T(8,128)(2,1)S(1)}) custom-call(bf16[256,2048]{1,0:T(8,128)(2,1)S(1)} %get-tuple-element.113.refs_0_.refs_1_.refs_4_, bf16[1024,704]{1,0:T(8,128)(2,1)} %get-tuple-element.98.refs_0_.refs_1_, bf16[256,704]{1,0:T(8,128)(2,1)S(1)} %copy-done.72, ...), custom_call_target="tpu_custom_call" | custom-call | flops 20700999680 | bytes 1024 | tf_op jit(solution)/shard_map/mlp_output/pallas_call | solution.py:415
  387.1 18.0 %attention_backward.2 = (bf16[1024,768]{1,0:T(8,128)(2,1)}, f32[1,5632]{1,0:T(1,128)S(1)}, bf16[256,768]{1,0:T(8,128)(2,1)}, bf16[256,768]{1,0:T(8,128)(2,1)}, f32[256,2048]{1,0:T(8,128)}, /*index=5*/f32[256,2048]{1,0:T(8,128)}) custom-call(f32[256,2048]{1,0:T(8,128)} %get-tuple-element.114.refs_1_.refs_0_, bf16[256,2048]{1,0:T(8,128)(2,1)S(1)} %copy-done.37, ...), custom_call_target="tpu_custom_call" | custom-call | flops 31050999808 | bytes 1024 | tf_op jit(solution)/shard_map/attention_backward/pallas_call | solution.py:415
  414.8 16.9 %attention_backward.3 = (bf16[1024,768]{1,0:T(8,128)(2,1)}, f32[1,5632]{1,0:T(1,128)S(1)}, bf16[256,768]{1,0:T(8,128)(2,1)S(1)}, bf16[256,768]{1,0:T(8,128)(2,1)...) custom-call(bf16[256,2048]{1,0:T(8,128)(2,1)S(1)} %copy-done.17, ...), custom_call_target="tpu_custom_call", output_to_operand_aliasing={{0}: (14, {})} | custom-call | flops 31050999808 | bytes 1024 | tf_op jit(solution)/shard_map/attention_backward/pallas_call | solution.py:415
  436.3 3.1 add_convert_fusion.3.refs_0_
  442.1 10.9 %token_product.7.refs_1_ = bf16[2112,768]{1,0:T(8,128)(2,1)} custom-call(bf16[256,2048]{1,0:T(8,128)(2,1)S(1)} %copy-done.6, bf16[1024,2048]{1,0:T(8,128)(2,1)} %get-tuple-element.125.refs_1_, bf16[1024,768]{1,0:T(8,128)(2,1)S(1)} %copy-done.88, bf16[1024,2048]{1,0:T(8,128)(2,1)} %collective-permute-done.56.refs_3_, ...), custom_call_target="tpu_custom_call" | custom-call | flops 16101000192 | bytes 1024 | tf_op jit(solution)/shard_map/token_product/pallas_call | solution.py:415
  456.1 2.6 collective-permute-done.75
  466.4 12.8 %collective-permute-done.62 = bf16[256,2048]{1,0:T(8,128)(2,1)} collective-permute-done((bf16[256,2048]{1,0:T(8,128)(2,1)}, bf16[256,2048]{1,0:T(8,128)(2,1)}, u32[]{:S(2)}, u32[]{:S(2)}) %collective-permute-start.62) | collective-permute-done | bytes 1048608 | tf_op jit(solution)/shard_map/ppermute | solution.py:49
  480.2 2.5 add_convert_fusion.1.refs_0_
  482.7 15.4 %collective-permute-done.61.refs_1_.side = bf16[256,2048]{1,0:T(8,128)(2,1)S(1)} collective-permute-done((bf16[256,2048]{1,0:T(8,128)(2,1)}, bf16[256,2048]{1,0:T(8,128)(2,1)S(1)}, u32[]{:S(2)}, u32[]{:S(2)}) %collective-permute-start.61) | collective-permute-done | bytes 1048608 | tf_op jit(solution)/shard_map/ppermute | solution.py:49
  509.5 5.0 token_product.9
  516.2 3.8 token_product.8
  522.9 2.9 add_convert_fusion
  525.9 4.4 add_convert_fusion.2
  531.1 23.4 %collective-permute-done.63.near.refs_2_ = bf16[256,2048]{1,0:T(8,128)(2,1)S(1)} collective-permute-done((bf16[256,2048]{1,0:T(8,128)(2,1)S(1)}, bf16[256,2048]{1,0:T(8,128)(2,1)S(1)}, u32[]{:S(2)}, u32[]{:S(2)}) %collective-permute-start.63) | collective-permute-done | bytes 1048608 | tf_op jit(solution)/shard_map/ppermute | solution.py:49
  558.8 4.6 norm_backward.3
  565.1 2.9 collective-permute-done.73.refs_3_
  570.2 5.5 spread_columns.3
  576.9 11.7 %collective-permute-done.74 = bf16[512,768]{1,0:T(8,128)(2,1)S(1)} collective-permute-done((bf16[512,768]{1,0:T(8,128)(2,1)S(1)}, bf16[512,768]{1,0:T(8,128)(2,1)S(1)}, u32[]{:S(2)}, u32[]{:S(2)}) %collective-permute-start.74) | collective-permute-done | bytes 786464 | tf_op jit(solution)/shard_map/ppermute | solution.py:49
  588.5 2.7 spread_columns.2
  (467 shorter events, 162.3 us)
Async XLA Ops:
  7.2 33.6 %all-gather.11.cloned.1.call-start = ((), (), s32[]{:S(2)}) async-start(), calls=%async_computation.10 | async-start | bytes 1310720 | tf_op jit(solution)/shard_map/all_gather | solution.py:915
  25.6 81.8 %all-gather.7.cloned.1.call-start = ((), (), s32[]{:S(2)}) async-start(), calls=%async_computation.4 | async-start | bytes 3932160 | tf_op jit(solution)/shard_map/all_gather | solution.py:915
  40.9 173.9 %all-gather.9.cloned.1.call-start = ((), (), s32[]{:S(2)}) async-start(), calls=%async_computation.5 | async-start | bytes 7208960 | tf_op jit(solution)/shard_map/all_gather | solution.py:915
  40.9 33.1 %collective-permute-start.3 = (bf16[256,2048]{1,0:T(8,128)(2,1)}, bf16[256,2048]{1,0:T(8,128)(2,1)S(1)}, u32[]{:S(2)}, u32[]{:S(2)}) collective-permute-start(bf16[256,2048]{1,0:T(8,128)(2,1)} %after.27.refs_2_.refs_3_), channel_id=1, source_target_pairs={{0,16},{1,3},{2,18},{3,1},{16,0},{17,19},{18,2},{19,17},{4,20},{5,... | collective-permute-start | bytes 3145736 | tf_op jit(solution)/shard_map/ppermute | solution.py:49
  42.4 31.5 %collective-permute-start.4 = (bf16[256,2048]{1,0:T(8,128)(2,1)}, bf16[256,2048]{1,0:T(8,128)(2,1)S(1)}, u32[]{:S(2)}, u32[]{:S(2)}) collective-permute-start(bf16[256,2048]{1,0:T(8,128)(2,1)} %after.27.refs_2_.refs_3_), channel_id=1, source_target_pairs={{0,2},{1,17},{2,0},{3,19},{16,18},{17,1},{18,16},{19,3},{4,6},{5,2... | collective-permute-start | bytes 3145736 | tf_op jit(solution)/shard_map/ppermute | solution.py:49
  43.9 23.3 %collective-permute-start.11 = (s32[256]{0:T(256)}, s32[256]{0:T(256)}, u32[]{:S(2)}, u32[]{:S(2)}) collective-permute-start(s32[256]{0:T(256)} %param.14), channel_id=1, source_target_pairs={{0,16},{1,3},{2,18},{3,1},{16,0},{17,19},{18,2},{19,17},{4,20},{5,... | collective-permute-start | bytes 3080 | tf_op jit(solution)/shard_map/ppermute | solution.py:49
  44.5 23.3 %collective-permute-start.12 = (s32[256]{0:T(256)}, s32[256]{0:T(256)}, u32[]{:S(2)}, u32[]{:S(2)}) collective-permute-start(s32[256]{0:T(256)} %param.14), channel_id=1, source_target_pairs={{0,2},{1,17},{2,0},{3,19},{16,18},{17,1},{18,16},{19,3},{4,6},{5,2... | collective-permute-start | bytes 3080 | tf_op jit(solution)/shard_map/ppermute | solution.py:49
  46.9 30.6 %collective-permute-start.5 = (f32[8,128]{1,0:T(8,128)}, f32[8,128]{1,0:T(8,128)S(1)}, u32[]{:S(2)}, u32[]{:S(2)}) collective-permute-start(f32[8,128]{1,0:T(8,128)} %after.29.refs_0_), channel_id=1, source_target_pairs={{0,1},{1,0},{2,3},{3,2},{4,5},{5,4},{6,7},{7,6},{8,9},{9,8},{10,11... | collective-permute-start | bytes 12296 | tf_op jit(solution)/shard_map/ppermute | solution.py:78
  75.9 30.8 %collective-permute-start.19 = (bf16[256,2048]{1,0:T(8,128)(2,1)}, bf16[256,2048]{1,0:T(8,128)(2,1)}, u32[]{:S(2)}, u32[]{:S(2)}) collective-permute-start(bf16[256,2048]{1,0:T(8,128)(2,1)} %after.28.refs_1_.refs_3_.refs_4_), channel_id=1, source_target_pairs={{0,2},{1,17},{2,0},{3,19},{16,18},{17,1},{18,16},{19,3},{4,6},{5,2... | collective-permute-start | bytes 3145736 | tf_op jit(solution)/shard_map/ppermute | solution.py:49
  107.9 169.1 %all-gather.13.cloned.1.call-start = ((), (), s32[]{:S(2)}) async-start(), calls=%async_computation.11 | async-start | bytes 3604480 | tf_op jit(solution)/shard_map/all_gather | solution.py:915
  109.5 25.6 %collective-permute-start.17 = (bf16[256,2048]{1,0:T(8,128)(2,1)}, bf16[256,2048]{1,0:T(8,128)(2,1)S(1)}, u32[]{:S(2)}, u32[]{:S(2)}) collective-permute-start(bf16[256,2048]{1,0:T(8,128)(2,1)} %after.34), channel_id=1, source_target_pairs={{0,16},{1,3},{2,18},{3,1},{16,0},{17,19},{18,2},{19,17},{4,20},{5,... | collective-permute-start | bytes 3145736 | tf_op jit(solution)/shard_map/ppermute | solution.py:49
  111.1 24.3 %collective-permute-start.18 = (bf16[256,2048]{1,0:T(8,128)(2,1)}, bf16[256,2048]{1,0:T(8,128)(2,1)S(1)}, u32[]{:S(2)}, u32[]{:S(2)}) collective-permute-start(bf16[256,2048]{1,0:T(8,128)(2,1)} %after.34), channel_id=1, source_target_pairs={{0,2},{1,17},{2,0},{3,19},{16,18},{17,1},{18,16},{19,3},{4,6},{5,2... | collective-permute-start | bytes 3145736 | tf_op jit(solution)/shard_map/ppermute | solution.py:49
  129.9 30.8 %collective-permute-start.22 = (bf16[256,2048]{1,0:T(8,128)(2,1)S(1)}, bf16[256,2048]{1,0:T(8,128)(2,1)S(1)}, u32[]{:S(2)}, u32[]{:S(2)}) collective-permute-start(bf16[256,2048]{1,0:T(8,128)(2,1)S(1)} %get-tuple-element.92), channel_id=1, source_target_pairs={{0,2},{1,17},{2,0},{3,19},{16,18},{17,1},{18,16},{19,3},{4,6},{5,2... | collective-permute-start | bytes 3145736 | tf_op jit(solution)/shard_map/ppermute | solution.py:49
  131.4 26.4 %collective-permute-start.23 = (bf16[256,2048]{1,0:T(8,128)(2,1)S(1)}, bf16[256,2048]{1,0:T(8,128)(2,1)S(1)}, u32[]{:S(2)}, u32[]{:S(2)}) collective-permute-start(bf16[256,2048]{1,0:T(8,128)(2,1)S(1)} %get-tuple-element.94), channel_id=1, source_target_pairs={{0,2},{1,17},{2,0},{3,19},{16,18},{17,1},{18,16},{19,3},{4,6},{5,2... | collective-permute-start | bytes 3145736 | tf_op jit(solution)/shard_map/ppermute | solution.py:49
  183.4 26.0 %collective-permute-start.25 = (bf16[256,2048]{1,0:T(8,128)(2,1)S(1)}, bf16[256,2048]{1,0:T(8,128)(2,1)S(1)}, u32[]{:S(2)}, u32[]{:S(2)}) collective-permute-start(bf16[256,2048]{1,0:T(8,128)(2,1)S(1)} %get-tuple-element.96.refs_0_.refs_1_), channel_id=1, source_target_pairs={{0,16},{1,3},{2,18},{3,1},{16,0},{17,19},{18,2},{19,17},{4,20},{5,... | collective-permute-start | bytes 3145736 | tf_op jit(solution)/shard_map/ppermute | solution.py:49
  184.8 24.5 %collective-permute-start.26 = (bf16[256,2048]{1,0:T(8,128)(2,1)S(1)}, bf16[256,2048]{1,0:T(8,128)(2,1)S(1)}, u32[]{:S(2)}, u32[]{:S(2)}) collective-permute-start(bf16[256,2048]{1,0:T(8,128)(2,1)S(1)} %get-tuple-element.96.refs_0_.refs_1_), channel_id=1, source_target_pairs={{0,2},{1,17},{2,0},{3,19},{16,18},{17,1},{18,16},{19,3},{4,6},{5,2... | collective-permute-start | bytes 3145736 | tf_op jit(solution)/shard_map/ppermute | solution.py:49
  215.8 223.6 %reduce-scatter.9.cloned.1.call-start = ((), (), s32[]{:S(2)}) async-start(), calls=%async_computation.8 | async-start | bytes 3604480 | tf_op jit(solution)/shard_map/reduce_scatter | solution.py:919
  231.2 26.6 %collective-permute-start.29 = (bf16[256,2048]{1,0:T(8,128)(2,1)}, bf16[256,2048]{1,0:T(8,128)(2,1)}, u32[]{:S(2)}, u32[]{:S(2)}) collective-permute-start(bf16[256,2048]{1,0:T(8,128)(2,1)} %after.40), channel_id=1, source_target_pairs={{0,2},{1,17},{2,0},{3,19},{16,18},{17,1},{18,16},{19,3},{4,6},{5,2... | collective-permute-start | bytes 3145736 | tf_op jit(solution)/shard_map/ppermute | solution.py:49
  232.7 26.4 %collective-permute-start.34 = (bf16[256,2048]{1,0:T(8,128)(2,1)S(1)}, bf16[256,2048]{1,0:T(8,128)(2,1)}, u32[]{:S(2)}, u32[]{:S(2)}) collective-permute-start(bf16[256,2048]{1,0:T(8,128)(2,1)S(1)} %copy-done.32), channel_id=1, source_target_pairs={{0,1},{1,0},{2,3},{3,2},{16,17},{17,16},{18,19},{19,18},{4,5},{5,4... | collective-permute-start | bytes 3145736 | tf_op jit(solution)/shard_map/ppermute | solution.py:49
  232.7 26.4 %collective-permute-start.35 = (bf16[256,2048]{1,0:T(8,128)(2,1)}, bf16[256,2048]{1,0:T(8,128)(2,1)}, u32[]{:S(2)}, u32[]{:S(2)}) collective-permute-start(bf16[256,2048]{1,0:T(8,128)(2,1)} %copy-done.39), channel_id=1, source_target_pairs={{0,1},{1,0},{2,3},{3,2},{16,17},{17,16},{18,19},{19,18},{4,5},{5,4... | collective-permute-start | bytes 3145736 | tf_op jit(solution)/shard_map/ppermute | solution.py:49
  233.2 26.4 %collective-permute-start.36 = (bf16[256,2048]{1,0:T(8,128)(2,1)}, bf16[256,2048]{1,0:T(8,128)(2,1)}, u32[]{:S(2)}, u32[]{:S(2)}) collective-permute-start(bf16[256,2048]{1,0:T(8,128)(2,1)} %copy-done.68), channel_id=1, source_target_pairs={{0,1},{1,0},{2,3},{3,2},{16,17},{17,16},{18,19},{19,18},{4,5},{5,4... | collective-permute-start | bytes 3145736 | tf_op jit(solution)/shard_map/ppermute | solution.py:49
  277.4 27.8 %collective-permute-start.41 = (bf16[256,2048]{1,0:T(8,128)(2,1)}, bf16[256,2048]{1,0:T(8,128)(2,1)}, u32[]{:S(2)}, u32[]{:S(2)}) collective-permute-start(bf16[256,2048]{1,0:T(8,128)(2,1)} %copy-done.65), channel_id=1, source_target_pairs={{0,1},{1,0},{2,3},{3,2},{16,17},{17,16},{18,19},{19,18},{4,5},{5,4... | collective-permute-start | bytes 3145736 | tf_op jit(solution)/shard_map/ppermute | solution.py:49
  277.5 50.9 %collective-permute-start.42 = (bf16[256,2048]{1,0:T(8,128)(2,1)S(1)}, bf16[256,2048]{1,0:T(8,128)(2,1)}, u32[]{:S(2)}, u32[]{:S(2)}) collective-permute-start(bf16[256,2048]{1,0:T(8,128)(2,1)S(1)} %copy-done.9), channel_id=1, source_target_pairs={{0,1},{1,0},{2,3},{3,2},{16,17},{17,16},{18,19},{19,18},{4,5},{5,4... | collective-permute-start | bytes 3145736 | tf_op jit(solution)/shard_map/ppermute | solution.py:49
  277.9 50.5 %collective-permute-start.43 = (bf16[256,2048]{1,0:T(8,128)(2,1)S(1)}, bf16[256,2048]{1,0:T(8,128)(2,1)}, u32[]{:S(2)}, u32[]{:S(2)}) collective-permute-start(bf16[256,2048]{1,0:T(8,128)(2,1)S(1)} %copy-done.23), channel_id=1, source_target_pairs={{0,1},{1,0},{2,3},{3,2},{16,17},{17,16},{18,19},{19,18},{4,5},{5,4... | collective-permute-start | bytes 3145736 | tf_op jit(solution)/shard_map/ppermute | solution.py:49
  278.0 55.3 %collective-permute-start.44 = (bf16[256,2048]{1,0:T(8,128)(2,1)}, bf16[256,2048]{1,0:T(8,128)(2,1)}, u32[]{:S(2)}, u32[]{:S(2)}) collective-permute-start(bf16[256,2048]{1,0:T(8,128)(2,1)} %collective-permute-done.27.refs_3_.refs_1_.refs_4_), channel_id=1, source_target_pairs={{0,1},{1,0},{2,3},{3,2},{16,17},{17,16},{18,19},{19,18},{4,5},{5,4... | collective-permute-start | bytes 3145736 | tf_op jit(solution)/shard_map/ppermute | solution.py:49
  278.4 183.6 %reduce-scatter.7.cloned.1.call-start = ((), (), s32[]{:S(2)}) async-start(), calls=%async_computation.7 | async-start | bytes 7208960 | tf_op jit(solution)/shard_map/reduce_scatter | solution.py:919
  304.2 24.7 %collective-permute-start.39 = (bf16[256,2048]{1,0:T(8,128)(2,1)S(1)}, bf16[256,2048]{1,0:T(8,128)(2,1)S(1)}, u32[]{:S(2)}, u32[]{:S(2)}) collective-permute-start(bf16[256,2048]{1,0:T(8,128)(2,1)S(1)} %get-tuple-element.105), channel_id=1, source_target_pairs={{0,2},{1,17},{2,0},{3,19},{16,18},{17,1},{18,16},{19,3},{4,6},{5,2... | collective-permute-start | bytes 3145736 | tf_op jit(solution)/shard_map/ppermute | solution.py:49
  305.1 25.2 %collective-permute-start.40 = (bf16[256,2048]{1,0:T(8,128)(2,1)S(1)}, bf16[256,2048]{1,0:T(8,128)(2,1)}, u32[]{:S(2)}, u32[]{:S(2)}) collective-permute-start(bf16[256,2048]{1,0:T(8,128)(2,1)S(1)} %get-tuple-element.106), channel_id=1, source_target_pairs={{0,2},{1,17},{2,0},{3,19},{16,18},{17,1},{18,16},{19,3},{4,6},{5,2... | collective-permute-start | bytes 3145736 | tf_op jit(solution)/shard_map/ppermute | solution.py:49
  333.3 22.5 %collective-permute-start.49 = (bf16[256,2048]{1,0:T(8,128)(2,1)}, bf16[256,2048]{1,0:T(8,128)(2,1)}, u32[]{:S(2)}, u32[]{:S(2)}) collective-permute-start(bf16[256,2048]{1,0:T(8,128)(2,1)} %after.43.refs_0_), channel_id=1, source_target_pairs={{0,16},{1,3},{2,18},{3,1},{16,0},{17,19},{18,2},{19,17},{4,20},{5,... | collective-permute-start | bytes 3145736 | tf_op jit(solution)/shard_map/ppermute | solution.py:49
  355.4 166.6 %reduce-scatter.5.cloned.1.call-start = ((), (), s32[]{:S(2)}) async-start(), calls=%async_computation.6 | async-start | bytes 4055040 | tf_op jit(solution)/shard_map/reduce_scatter | solution.py:919
  355.5 83.9 %collective-permute-start.56 = (bf16[1024,2048]{1,0:T(8,128)(2,1)}, bf16[1024,2048]{1,0:T(8,128)(2,1)}, u32[]{:S(2)}, u32[]{:S(2)}) collective-permute-start(bf16[1024,2048]{1,0:T(8,128)(2,1)} %get-tuple-element.125.refs_1_), channel_id=1, source_target_pairs={{0,1},{1,0},{2,3},{3,2},{16,17},{17,16},{18,19},{19,18},{4,5},{5,4... | collective-permute-start | bytes 12582920 | tf_op jit(solution)/shard_map/ppermute | solution.py:49
  381.7 26.2 %collective-permute-start.52 = (bf16[256,2048]{1,0:T(8,128)(2,1)}, bf16[256,2048]{1,0:T(8,128)(2,1)S(1)}, u32[]{:S(2)}, u32[]{:S(2)}) collective-permute-start(bf16[256,2048]{1,0:T(8,128)(2,1)} %after.44.refs_2_.refs_1_.refs_5_), channel_id=1, source_target_pairs={{0,2},{1,17},{2,0},{3,19},{16,18},{17,1},{18,16},{19,3},{4,6},{5,2... | collective-permute-start | bytes 3145736 | tf_op jit(solution)/shard_map/ppermute | solution.py:49
  382.1 25.9 %collective-permute-start.51 = (bf16[256,2048]{1,0:T(8,128)(2,1)}, bf16[256,2048]{1,0:T(8,128)(2,1)S(1)}, u32[]{:S(2)}, u32[]{:S(2)}) collective-permute-start(bf16[256,2048]{1,0:T(8,128)(2,1)} %after.45), channel_id=1, source_target_pairs={{0,2},{1,17},{2,0},{3,19},{16,18},{17,1},{18,16},{19,3},{4,6},{5,2... | collective-permute-start | bytes 3145736 | tf_op jit(solution)/shard_map/ppermute | solution.py:49
  405.7 34.9 %collective-permute-start.57 = (bf16[256,768]{1,0:T(8,128)(2,1)}, bf16[256,768]{1,0:T(8,128)(2,1)}, u32[]{:S(2)}, u32[]{:S(2)}) collective-permute-start(bf16[256,768]{1,0:T(8,128)(2,1)} %get-tuple-element.127), channel_id=1, source_target_pairs={{0,1},{1,0},{2,3},{3,2},{16,17},{17,16},{18,19},{19,18},{4,5},{5,4... | collective-permute-start | bytes 1179656 | tf_op jit(solution)/shard_map/ppermute | solution.py:49
  405.7 34.9 %collective-permute-start.58 = (bf16[256,768]{1,0:T(8,128)(2,1)}, bf16[256,768]{1,0:T(8,128)(2,1)}, u32[]{:S(2)}, u32[]{:S(2)}) collective-permute-start(bf16[256,768]{1,0:T(8,128)(2,1)} %get-tuple-element.128), channel_id=1, source_target_pairs={{0,1},{1,0},{2,3},{3,2},{16,17},{17,16},{18,19},{19,18},{4,5},{5,4... | collective-permute-start | bytes 1179656 | tf_op jit(solution)/shard_map/ppermute | solution.py:49
  409.9 25.2 %collective-permute-start.54 = (bf16[256,2048]{1,0:T(8,128)(2,1)}, bf16[256,2048]{1,0:T(8,128)(2,1)}, u32[]{:S(2)}, u32[]{:S(2)}) collective-permute-start(bf16[256,2048]{1,0:T(8,128)(2,1)} %after.47), channel_id=1, source_target_pairs={{0,2},{1,17},{2,0},{3,19},{16,18},{17,1},{18,16},{19,3},{4,6},{5,2... | collective-permute-start | bytes 3145736 | tf_op jit(solution)/shard_map/ppermute | solution.py:49
  410.3 26.0 %collective-permute-start.53 = (bf16[256,2048]{1,0:T(8,128)(2,1)}, bf16[256,2048]{1,0:T(8,128)(2,1)}, u32[]{:S(2)}, u32[]{:S(2)}) collective-permute-start(bf16[256,2048]{1,0:T(8,128)(2,1)} %after.46), channel_id=1, source_target_pairs={{0,2},{1,17},{2,0},{3,19},{16,18},{17,1},{18,16},{19,3},{4,6},{5,2... | collective-permute-start | bytes 3145736 | tf_op jit(solution)/shard_map/ppermute | solution.py:49
  452.9 26.2 %collective-permute-start.62 = (bf16[256,2048]{1,0:T(8,128)(2,1)}, bf16[256,2048]{1,0:T(8,128)(2,1)}, u32[]{:S(2)}, u32[]{:S(2)}) collective-permute-start(bf16[256,2048]{1,0:T(8,128)(2,1)} %after.50), channel_id=1, source_target_pairs={{0,2},{1,17},{2,0},{3,19},{16,18},{17,1},{18,16},{19,3},{4,6},{5,2... | collective-permute-start | bytes 3145736 | tf_op jit(solution)/shard_map/ppermute | solution.py:49
  453.9 72.0 %collective-permute-start.55 = (bf16[256,2048]{1,0:T(8,128)(2,1)S(1)}, bf16[256,2048]{1,0:T(8,128)(2,1)}, u32[]{:S(2)}, u32[]{:S(2)}) collective-permute-start(bf16[256,2048]{1,0:T(8,128)(2,1)S(1)} %copy-done.6), channel_id=1, source_target_pairs={{0,16},{1,3},{2,18},{3,1},{16,0},{17,19},{18,2},{19,17},{4,20},{5,... | collective-permute-start | bytes 3145736 | tf_op jit(solution)/shard_map/ppermute | solution.py:49
  455.0 43.1 %collective-permute-start.61 = (bf16[256,2048]{1,0:T(8,128)(2,1)}, bf16[256,2048]{1,0:T(8,128)(2,1)S(1)}, u32[]{:S(2)}, u32[]{:S(2)}) collective-permute-start(bf16[256,2048]{1,0:T(8,128)(2,1)} %after.49), channel_id=1, source_target_pairs={{0,2},{1,17},{2,0},{3,19},{16,18},{17,1},{18,16},{19,3},{4,6},{5,2... | collective-permute-start | bytes 3145736 | tf_op jit(solution)/shard_map/ppermute | solution.py:49
  456.1 119.7 %reduce-scatter.11.cloned.1.call-start = ((), (), s32[]{:S(2)}) async-start(), calls=%async_computation.9 | async-start | bytes 1310720 | tf_op jit(solution)/shard_map/reduce_scatter | solution.py:919
  465.3 33.8 %collective-permute-start.67 = (bf16[128,1408]{1,0:T(8,128)(2,1)}, bf16[128,1408]{1,0:T(8,128)(2,1)S(1)}, u32[]{:S(2)}, u32[]{:S(2)}) collective-permute-start(bf16[128,1408]{1,0:T(8,128)(2,1)} %get-tuple-element.136), channel_id=1, source_target_pairs={{0,1},{1,0},{2,3},{3,2},{16,17},{17,16},{18,19},{19,18},{4,5},{5,4... | collective-permute-start | bytes 1081352 | tf_op jit(solution)/shard_map/ppermute | solution.py:49
  465.3 36.8 %collective-permute-start.68 = (bf16[128,1408]{1,0:T(8,128)(2,1)}, bf16[128,1408]{1,0:T(8,128)(2,1)}, u32[]{:S(2)}, u32[]{:S(2)}) collective-permute-start(bf16[128,1408]{1,0:T(8,128)(2,1)} %get-tuple-element.137), channel_id=1, source_target_pairs={{0,2},{1,3},{2,0},{3,1},{16,18},{17,19},{18,16},{19,17},{4,6},{5,7... | collective-permute-start | bytes 1081352 | tf_op jit(solution)/shard_map/ppermute | solution.py:49
  479.1 25.1 %collective-permute-start.69 = (bf16[128,1408]{1,0:T(8,128)(2,1)}, bf16[128,1408]{1,0:T(8,128)(2,1)}, u32[]{:S(2)}, u32[]{:S(2)}) collective-permute-start(bf16[128,1408]{1,0:T(8,128)(2,1)} %get-tuple-element.138), channel_id=1, source_target_pairs={{0,3},{1,2},{2,1},{3,0},{16,19},{17,18},{18,17},{19,16},{4,7},{5,6... | collective-permute-start | bytes 1081352 | tf_op jit(solution)/shard_map/ppermute | solution.py:49
  508.6 45.9 %collective-permute-start.70 = (bf16[512,1408]{1,0:T(8,128)(2,1)}, bf16[512,1408]{1,0:T(8,128)(2,1)}, u32[]{:S(2)}, u32[]{:S(2)}) collective-permute-start(bf16[512,1408]{1,0:T(8,128)(2,1)} %place_blocks.10), channel_id=1, source_target_pairs={{0,16},{1,17},{2,18},{3,19},{16,0},{17,1},{18,2},{19,3},{4,20},{5,... | collective-permute-start | bytes 4325384 | tf_op jit(solution)/shard_map/ppermute | solution.py:49
  521.0 33.5 %collective-permute-start.63 = (bf16[256,2048]{1,0:T(8,128)(2,1)S(1)}, bf16[256,2048]{1,0:T(8,128)(2,1)S(1)}, u32[]{:S(2)}, u32[]{:S(2)}) collective-permute-start(bf16[256,2048]{1,0:T(8,128)(2,1)S(1)} %copy-done.12), channel_id=1, source_target_pairs={{0,16},{1,3},{2,18},{3,1},{16,0},{17,19},{18,2},{19,17},{4,20},{5,... | collective-permute-start | bytes 3145736 | tf_op jit(solution)/shard_map/ppermute | solution.py:49
  530.3 33.2 %collective-permute-start.65 = (f32[4,896]{1,0:T(4,128)S(1)}, f32[4,896]{1,0:T(4,128)}, u32[]{:S(2)}, u32[]{:S(2)}) collective-permute-start(f32[4,896]{1,0:T(4,128)S(1)} %add.89), channel_id=1, source_target_pairs={{0,2},{2,0},{1,3},{3,1},{4,6},{6,4},{5,7},{7,5},{8,10},{10,8},{9,1... | collective-permute-start | bytes 43016 | tf_op jit(solution)/shard_map/ppermute | solution.py:78
  568.1 20.4 %collective-permute-start.74 = (bf16[512,768]{1,0:T(8,128)(2,1)S(1)}, bf16[512,768]{1,0:T(8,128)(2,1)S(1)}, u32[]{:S(2)}, u32[]{:S(2)}) collective-permute-start(bf16[512,768]{1,0:T(8,128)(2,1)S(1)} %place_blocks.11), channel_id=1, source_target_pairs={{0,16},{1,17},{2,18},{3,19},{16,0},{17,1},{18,2},{19,3},{4,20},{5,... | collective-permute-start | bytes 2359304 | tf_op jit(solution)/shard_map/ppermute | solution.py:49
  (147 other events, 944.9 us)
Sparse Core Ops, SparseCore 0:
  10.2 30.6 all-gather.10
  43.0 64.3 all-gather.6
  109.5 105.2 all-gather.8
  216.8 57.4 all-gather.12
  278.5 53.5 reduce-scatter.8
  355.5 99.9 reduce-scatter.6
  457.9 62.2 reduce-scatter.4
  526.0 25.5 reduce-scatter.10

commit v5 on v4

--- a/solution.py
+++ b/solution.py
@@ -1097,12 +1097,15 @@
 
     owned_down = whole_rows(after(down_sum, out_near))
     gate_half, other = whole_columns(both_sum)
-    def out_product(window, later):
-        pairs = [(([attended_low], window), (hidden_slots, 0))]
-        return token_product(pairs, head_cols, width, later, us=40)
-
-    out_there = swap(out_product(1, (gate_half, norm_near, owned_down)), SIBLING)
-    out_grad = out_product(0, ()).astype(jnp.float32) + out_there.astype(jnp.float32)
+    out_grad = token_product(
+        [(([attended_low], 0), (hidden_slots, 0))],
+        2 * head_cols,
+        width,
+        (gate_half, norm_near, owned_down),
+        us=80,
+    )
+    out_there = swap(out_grad[head_cols:], SIBLING)
+    out_grad = out_grad[:head_cols].astype(jnp.float32) + out_there.astype(jnp.float32)
     out_grad = out_grad.astype(jnp.bfloat16)
 
     if spread:

time: 608 us -> 617 us (1.015)
  waiting for transfers between devices: 200 us -> 209 us
    reduce_scatter x4, waiting for transfers between devices: 0.01 us -> 10.4 us  [scatter_z(): return lax.psum_scatter(values, 'z', scatter_dimension=0, tiled=True)]
    pallas_call x29 -> x28, Pallas kernels: 225 us -> 223 us  [run_kernel(): pl.pallas_call(used, grid=(blocks,), out_shape=shapes, in_specs=anywhere(...]
    unnamed x228 -> x216, local copies, waits for them, and re-layouts: 58.5 us -> 60.9 us
  transfers between devices with their start and end apart: 86 -> 86, of which waited for: 35 -> 37; matrix products, arithmetic and copies ran while one was open for 7% -> 8% of each run, Pallas kernels for 37% -> 36%
where the time goes in v5:
time: 617 us; the launch traced here: 611 us
  Pallas kernels  223 us (36%)
  waiting for transfers between devices  209 us (34%)
  local copies, waits for them, and re-layouts  71.9 us (12%)
  starting transfers between devices  60.2 us (10%)
  other arithmetic  32.6 us (5%)
  between operations  15.2 us (2%)
    pallas_call x28, Pallas kernels, run_kernel(): pl.pallas_call(used, grid=(blocks,), out_shape=shapes, in_specs=anywhere(...  223 us
    ppermute x69, waiting for transfers between devices, swap(): return lax.ppermute(values, PLANE, pairs)  175 us
    unnamed x216, local copies, waits for them, and re-layouts  60.9 us
    ppermute x69, starting transfers between devices, swap(): return lax.ppermute(values, PLANE, pairs)  51.6 us
    all_gather x4, waiting for transfers between devices, gather_z(): return lax.all_gather(values, 'z', axis=0, tiled=True)  18.7 us
  transfers between devices with their start and end apart: 86, of which 37 were waited for; matrix products, arithmetic and copies ran while one was open for 8% of the time, Pallas kernels for 36%

profile of v5, /device:TPU:0, one launch (start us, length us, event | category | flops | bytes accessed | tf_op | source)
XLA Modules:
  0.0 611.2 jit_solution(14736902181974182098)
XLA Ops:
  12.6 2.6 collective-permute-start.1
  16.2 4.7 collective-permute-done.1.refs_2_
  20.9 3.7 collective-permute-done.2.refs_3_
  25.6 15.2 %all-gather.11.cloned.1.call-done = bf16[1,256,2048]{2,1,0:T(8,128)(2,1)} async-done(((bf16[1,64,2048]{2,1,0:T(8,128)(2,1)}), bf16[1,256,2048]{2,1,0:T(8,128)(2,1)}) %all-gather.11.cloned.1.call-update) | async-done | bytes 1048592 | tf_op jit(solution)/shard_map/all_gather | solution.py:915
  50.3 3.3 pick_columns.2
  57.1 10.2 %collective-permute-done.11.refs_0_ = s32[256]{0:T(256)} collective-permute-done((s32[256]{0:T(256)}, s32[256]{0:T(256)}, u32[]{:S(2)}, u32[]{:S(2)}) %collective-permute-start.11) | collective-permute-done | bytes 1056 | tf_op jit(solution)/shard_map/ppermute | solution.py:49
  81.9 2.4 collective-permute-done.9.refs_2_
  88.3 3.1 fusion.2
  93.0 2.4 pad_maximum_fusion.refs_6_.refs_5_.refs_7_
  96.4 3.5 collective-permute-done.15.refs_2_
  99.8 5.7 collective-permute-done.16.refs_3_
  115.0 14.8 %attention_forward.2 = (bf16[1024,2048]{1,0:T(8,128)(2,1)}, bf16[1024,1536]{1,0:T(8,128)(2,1)}, f32[1024,128]{1,0:T(8,128)S(1)}, bf16[1024,512]{1,0:T(8,128)(2,1...) custom-call(bf16[256,2048]{1,0:T(8,128)(2,1)S(1)} %copy-done.3, ...), custom_call_target="tpu_custom_call" | custom-call | flops 17251000320 | bytes 1024 | tf_op jit(solution)/shard_map/attention_forward/pallas_call | solution.py:415
  131.9 4.3 collective-permute-done.17.refs_0_.refs_2_.refs_1_
  136.5 16.2 %attention_forward.3 = (bf16[1024,2048]{1,0:T(8,128)(2,1)}, bf16[1024,1536]{1,0:T(8,128)(2,1)}, f32[1024,128]{1,0:T(8,128)S(1)}, bf16[1024,512]{1,0:T(8,128)(2,1...) custom-call(bf16[256,2048]{1,0:T(8,128)(2,1)} %collective-permute-do, ...), custom_call_target="tpu_custom_call", output_to_operand_aliasing={{0}: (12, {}), {1}: (13, {}), {2}: (14, {}), {3}: (15, {})} | custom-call | flops 17251000320 | bytes 1024 | tf_op jit(solution)/shard_map/attention_forward/pallas_call | solution.py:415
  152.7 6.1 %collective-permute-done.23 = bf16[256,2048]{1,0:T(8,128)(2,1)S(1)} collective-permute-done((bf16[256,2048]{1,0:T(8,128)(2,1)S(1)}, bf16[256,2048]{1,0:T(8,128)(2,1)S(1)}, u32[]{:S(2)}, u32[]{:S(2)}) %collective-permute-start.23) | collective-permute-done | bytes 1048608 | tf_op jit(solution)/shard_map/ppermute | solution.py:49
  158.8 2.8 add_convert_fusion.5.refs_0_
  164.1 13.5 %collective-permute-done.24.near = bf16[256,2048]{1,0:T(8,128)(2,1)S(1)} collective-permute-done((bf16[256,2048]{1,0:T(8,128)(2,1)}, bf16[256,2048]{1,0:T(8,128)(2,1)S(1)}, u32[]{:S(2)}, u32[]{:S(2)}) %collective-permute-start.24) | collective-permute-done | bytes 1048608 | tf_op jit(solution)/shard_map/ppermute | solution.py:49
  179.9 4.3 norm_forward.1
  187.2 23.3 %collective-permute-done.25.refs_0_ = bf16[256,2048]{1,0:T(8,128)(2,1)S(1)} collective-permute-done((bf16[256,2048]{1,0:T(8,128)(2,1)}, bf16[256,2048]{1,0:T(8,128)(2,1)S(1)}, u32[]{:S(2)}, u32[]{:S(2)}) %collective-permute-start.25) | collective-permute-done | bytes 1048608 | tf_op jit(solution)/shard_map/ppermute | solution.py:49
  220.1 11.1 %collective-permute-done.27.refs_3_.refs_1_.refs_4_ = bf16[256,2048]{1,0:T(8,128)(2,1)} collective-permute-done((bf16[256,2048]{1,0:T(8,128)(2,1)S(1)}, bf16[256,2048]{1,0:T(8,128)(2,1)}, u32[]{:S(2)}, u32[]{:S(2)}) %collective-permute-start.27) | collective-permute-done | bytes 1048608 | tf_op jit(solution)/shard_map/ppermute | solution.py:49
  233.2 21.4 %mlp_forward.1 = (f32[1024,2816]{1,0:T(8,128)}, bf16[1024,704]{1,0:T(8,128)(2,1)}, bf16[256,704]{1,0:T(8,128)(2,1)S(1)}, bf16[256,704]{1,0:T(8,128)(2,1)S(1)}, b...) custom-call(bf16[256,2048]{1,0:T(8,128)(2,1)} %get-tuple-element.96.refs_0_.refs_1_, ...), custom_call_target="tpu_custom_call" | custom-call | flops 9201000448 | bytes 1024 | tf_op jit(solution)/shard_map/mlp_forward/pallas_call | solution.py:415
  263.0 10.8 %token_product.4.refs_1_.refs_0_ = bf16[704,2048]{1,0:T(8,128)(2,1)} custom-call(bf16[1024,704]{1,0:T(8,128)(2,1)} %get-tuple-element.98.refs_0_.refs_1_, bf16[256,2048]{1,0:T(8,128)(2,1)} %refs_2_.1, bf16[256,2048]{1,0:T(8,128)(2,1)} %collective-permute-done.17.refs_0_.refs_2_.refs_1_, bf16[256,2048]{1,0:T(8,128)(2,1)} %collective-permute-done.18.refs_1_.refs_3_, ...), custom_call_target="tpu_custom_call" | custom-call | flops 11500999680 | bytes 1024 | tf_op jit(solution)/shard_map/token_product/pallas_call | solution.py:415
  275.4 4.5 collective-permute-done.38.refs_7_.refs_6_
  279.9 21.1 %mlp_backward.2 = (bf16[1024,1408]{1,0:T(8,128)(2,1)}, bf16[256,1408]{1,0:T(8,128)(2,1)}, bf16[256,1408]{1,0:T(8,128)(2,1)}, bf16[256,2048]{1,0:T(8,128)(2,1)S(1)}, bf16[256,2048]{1,0:T(8,128)(2,1)S(1)}) custom-call(bf16[704,2048]{1,0:T(8,128)(2,1)} %token_product.4.refs_1_.refs_0_, bf16[256,2048]{1,0:T(8,128)(2,1)} %collective-permute-done.18.refs_1_.refs_3_, ...), custom_call_target="tpu_custom_call" | custom-call | flops 24150999040 | bytes 1024 | tf_op jit(solution)/shard_map/mlp_backward/pallas_call | solution.py:415
  303.1 21.4 %mlp_backward.3 = (bf16[1024,1408]{1,0:T(8,128)(2,1)}, bf16[256,1408]{1,0:T(8,128)(2,1)}, bf16[256,1408]{1,0:T(8,128)(2,1)}, f32[256,2048]{1,0:T(8,128)S(1)}, f32[256,2048]{1,0:T(8,128)}) custom-call(bf16[256,2048]{1,0:T(8,128)(2,1)} %refs_2_.1, bf16[256,2048]{1,0:T(8,128)(2,1)} %collective-permute-done.17.refs_0_.refs_2_.refs_1_, ...), custom_call_target="tpu_custom_call", output_to_operand_aliasing={{0}: (7, {})} | custom-call | flops 24150999040 | bytes 1024 | tf_op jit(solution)/shard_map/mlp_backward/pallas_call | solution.py:415
  327.2 2.9 add_convert_fusion.4.refs_0_
  336.7 19.0 %token_product.5.refs_0_ = bf16[2048,1408]{1,0:T(8,128)(2,1)} custom-call(bf16[256,2048]{1,0:T(8,128)(2,1)S(1)} %copy-done.13, bf16[256,2048]{1,0:T(8,128)(2,1)} %get-tuple-element.96.refs_0_.refs_1_, bf16[256,2048]{1,0:T(8,128)(2,1)S(1)} %copy-done.9, bf16[256,2048]{1,0:T(8,128)(2,1)} %copy-done.22, ...), custom_call_target="tpu_custom_call" | custom-call | flops 28750999552 | bytes 1024 | tf_op jit(solution)/shard_map/token_product/pallas_call | solution.py:415
  356.7 6.2 %norm_backward.2 = (f32[256,2048]{1,0:T(8,128)}, bf16[256,2048]{1,0:T(8,128)(2,1)S(1)}, f32[1,4096]{1,0:T(1,128)S(1)}) custom-call(bf16[2048,1408]{1,0:T(8,128)(2,1)} %token_product.5.refs_0_, f32[256,2048]{1,0:T(8,128)} %get-tuple-element.95.refs_1_, bf16[256,2048]{1,0:T(8,128)(2,1)} %refs_2_.1, f32[256,2048]{1,0:T(8,128)} %copy-done.81, ...), custom_call_target="tpu_custom_call" | custom-call | flops 5751000064 | bytes 1024 | tf_op jit(solution)/shard_map/norm_backward/pallas_call | solution.py:415
  364.9 14.2 %mlp_output.1 = (f32[256,2048]{1,0:T(8,128)}, f32[256,2048]{1,0:T(8,128)}, bf16[256,2048]{1,0:T(8,128)(2,1)S(1)}, bf16[256,2048]{1,0:T(8,128)(2,1)S(1)}) custom-call(bf16[256,2048]{1,0:T(8,128)(2,1)S(1)} %get-tuple-element.113.refs_0_.refs_1_.refs_4_, bf16[1024,704]{1,0:T(8,128)(2,1)} %get-tuple-element.98.refs_0_.refs_1_, bf16[256,704]{1,0:T(8,128)(2,1)S(1)} %copy-done.64, ...), custom_call_target="tpu_custom_call" | custom-call | flops 20700999680 | bytes 1024 | tf_op jit(solution)/shard_map/mlp_output/pallas_call | solution.py:415
  387.5 18.0 %attention_backward.2 = (bf16[1024,768]{1,0:T(8,128)(2,1)}, f32[1,5632]{1,0:T(1,128)S(1)}, bf16[256,768]{1,0:T(8,128)(2,1)}, bf16[256,768]{1,0:T(8,128)(2,1)}, f32[256,2048]{1,0:T(8,128)}, /*index=5*/f32[256,2048]{1,0:T(8,128)}) custom-call(f32[256,2048]{1,0:T(8,128)} %get-tuple-element.114.refs_1_.refs_0_, bf16[256,2048]{1,0:T(8,128)(2,1)S(1)} %copy-done.34, ...), custom_call_target="tpu_custom_call" | custom-call | flops 31050999808 | bytes 1024 | tf_op jit(solution)/shard_map/attention_backward/pallas_call | solution.py:415
  415.9 16.9 %attention_backward.3 = (bf16[1024,768]{1,0:T(8,128)(2,1)}, f32[1,5632]{1,0:T(1,128)S(1)}, bf16[256,768]{1,0:T(8,128)(2,1)S(1)}, bf16[256,768]{1,0:T(8,128)(2,1)...) custom-call(bf16[256,2048]{1,0:T(8,128)(2,1)S(1)} %copy-done.17, ...), custom_call_target="tpu_custom_call", output_to_operand_aliasing={{0}: (14, {})} | custom-call | flops 31050999808 | bytes 1024 | tf_op jit(solution)/shard_map/attention_backward/pallas_call | solution.py:415
  436.8 3.1 add_convert_fusion.3.refs_0_
  442.6 10.9 %token_product.6.refs_1_ = bf16[2112,768]{1,0:T(8,128)(2,1)} custom-call(bf16[256,2048]{1,0:T(8,128)(2,1)S(1)} %copy-done.6, bf16[1024,2048]{1,0:T(8,128)(2,1)} %get-tuple-element.125.refs_1_, bf16[1024,768]{1,0:T(8,128)(2,1)S(1)} %copy-done.82, bf16[1024,2048]{1,0:T(8,128)(2,1)} %collective-permute-done.56.refs_3_, ...), custom_call_target="tpu_custom_call" | custom-call | flops 16101000192 | bytes 1024 | tf_op jit(solution)/shard_map/token_product/pallas_call | solution.py:415
  455.8 3.4 collective-permute-done.75
  468.5 2.5 add_convert_fusion.1.refs_0_
  471.0 16.4 %collective-permute-done.61.refs_1_.side = bf16[256,2048]{1,0:T(8,128)(2,1)S(1)} collective-permute-done((bf16[256,2048]{1,0:T(8,128)(2,1)}, bf16[256,2048]{1,0:T(8,128)(2,1)S(1)}, u32[]{:S(2)}, u32[]{:S(2)}) %collective-permute-start.61) | collective-permute-done | bytes 1048608 | tf_op jit(solution)/shard_map/ppermute | solution.py:49
  491.4 2.5 collective-permute-done.69.refs_3_
  495.8 2.5 place_blocks.10
  498.6 4.9 token_product.7
  510.3 10.4 %reduce-scatter.5.cloned.1.call-done.refs_0_ = bf16[528,768]{1,0:T(8,128)(2,1)} async-done(((bf16[2112,768]{1,0:T(8,128)(2,1)}), bf16[528,768]{1,0:T(8,128)(2,1)}) %reduce-scatter.5.cloned.1.call-update) | async-done | bytes 811024 | tf_op jit(solution)/shard_map/reduce_scatter | solution.py:919
  521.6 2.9 add_convert_fusion
  524.5 8.8 %collective-permute-done.55.refs_3_ = bf16[256,2048]{1,0:T(8,128)(2,1)} collective-permute-done((bf16[256,2048]{1,0:T(8,128)(2,1)S(1)}, bf16[256,2048]{1,0:T(8,128)(2,1)}, u32[]{:S(2)}, u32[]{:S(2)}) %collective-permute-start.55) | collective-permute-done | bytes 1048608 | tf_op jit(solution)/shard_map/ppermute | solution.py:49
  533.3 4.4 add_convert_fusion.2
  538.9 25.3 %collective-permute-done.63.near.refs_2_ = bf16[256,2048]{1,0:T(8,128)(2,1)S(1)} collective-permute-done((bf16[256,2048]{1,0:T(8,128)(2,1)S(1)}, bf16[256,2048]{1,0:T(8,128)(2,1)S(1)}, u32[]{:S(2)}, u32[]{:S(2)}) %collective-permute-start.63) | collective-permute-done | bytes 1048608 | tf_op jit(solution)/shard_map/ppermute | solution.py:49
  569.9 4.6 norm_backward.3
  579.8 5.5 spread_columns.3
  586.3 11.7 %collective-permute-done.74 = bf16[512,768]{1,0:T(8,128)(2,1)S(1)} collective-permute-done((bf16[512,768]{1,0:T(8,128)(2,1)S(1)}, bf16[512,768]{1,0:T(8,128)(2,1)S(1)}, u32[]{:S(2)}, u32[]{:S(2)}) %collective-permute-start.74) | collective-permute-done | bytes 786464 | tf_op jit(solution)/shard_map/ppermute | solution.py:49
  598.0 2.7 spread_columns.2
  (455 shorter events, 164.1 us)
Async XLA Ops:
  7.2 33.6 %all-gather.11.cloned.1.call-start = ((), (), s32[]{:S(2)}) async-start(), calls=%async_computation.10 | async-start | bytes 1310720 | tf_op jit(solution)/shard_map/all_gather | solution.py:915
  25.6 81.8 %all-gather.7.cloned.1.call-start = ((), (), s32[]{:S(2)}) async-start(), calls=%async_computation.4 | async-start | bytes 3932160 | tf_op jit(solution)/shard_map/all_gather | solution.py:915
  40.9 173.9 %all-gather.9.cloned.1.call-start = ((), (), s32[]{:S(2)}) async-start(), calls=%async_computation.5 | async-start | bytes 7208960 | tf_op jit(solution)/shard_map/all_gather | solution.py:915
  40.9 33.1 %collective-permute-start.3 = (bf16[256,2048]{1,0:T(8,128)(2,1)}, bf16[256,2048]{1,0:T(8,128)(2,1)S(1)}, u32[]{:S(2)}, u32[]{:S(2)}) collective-permute-start(bf16[256,2048]{1,0:T(8,128)(2,1)} %after.27.refs_2_.refs_3_), channel_id=1, source_target_pairs={{0,16},{1,3},{2,18},{3,1},{16,0},{17,19},{18,2},{19,17},{4,20},{5,... | collective-permute-start | bytes 3145736 | tf_op jit(solution)/shard_map/ppermute | solution.py:49
  42.4 31.6 %collective-permute-start.4 = (bf16[256,2048]{1,0:T(8,128)(2,1)}, bf16[256,2048]{1,0:T(8,128)(2,1)S(1)}, u32[]{:S(2)}, u32[]{:S(2)}) collective-permute-start(bf16[256,2048]{1,0:T(8,128)(2,1)} %after.27.refs_2_.refs_3_), channel_id=1, source_target_pairs={{0,2},{1,17},{2,0},{3,19},{16,18},{17,1},{18,16},{19,3},{4,6},{5,2... | collective-permute-start | bytes 3145736 | tf_op jit(solution)/shard_map/ppermute | solution.py:49
  43.9 23.3 %collective-permute-start.11 = (s32[256]{0:T(256)}, s32[256]{0:T(256)}, u32[]{:S(2)}, u32[]{:S(2)}) collective-permute-start(s32[256]{0:T(256)} %param.14), channel_id=1, source_target_pairs={{0,16},{1,3},{2,18},{3,1},{16,0},{17,19},{18,2},{19,17},{4,20},{5,... | collective-permute-start | bytes 3080 | tf_op jit(solution)/shard_map/ppermute | solution.py:49
  44.5 23.3 %collective-permute-start.12 = (s32[256]{0:T(256)}, s32[256]{0:T(256)}, u32[]{:S(2)}, u32[]{:S(2)}) collective-permute-start(s32[256]{0:T(256)} %param.14), channel_id=1, source_target_pairs={{0,2},{1,17},{2,0},{3,19},{16,18},{17,1},{18,16},{19,3},{4,6},{5,2... | collective-permute-start | bytes 3080 | tf_op jit(solution)/shard_map/ppermute | solution.py:49
  46.9 30.6 %collective-permute-start.5 = (f32[8,128]{1,0:T(8,128)}, f32[8,128]{1,0:T(8,128)S(1)}, u32[]{:S(2)}, u32[]{:S(2)}) collective-permute-start(f32[8,128]{1,0:T(8,128)} %after.29.refs_0_), channel_id=1, source_target_pairs={{0,1},{1,0},{2,3},{3,2},{4,5},{5,4},{6,7},{7,6},{8,9},{9,8},{10,11... | collective-permute-start | bytes 12296 | tf_op jit(solution)/shard_map/ppermute | solution.py:78
  76.0 30.8 %collective-permute-start.19 = (bf16[256,2048]{1,0:T(8,128)(2,1)}, bf16[256,2048]{1,0:T(8,128)(2,1)}, u32[]{:S(2)}, u32[]{:S(2)}) collective-permute-start(bf16[256,2048]{1,0:T(8,128)(2,1)} %after.28.refs_1_.refs_3_.refs_4_), channel_id=1, source_target_pairs={{0,2},{1,17},{2,0},{3,19},{16,18},{17,1},{18,16},{19,3},{4,6},{5,2... | collective-permute-start | bytes 3145736 | tf_op jit(solution)/shard_map/ppermute | solution.py:49
  107.9 166.4 %all-gather.13.cloned.1.call-start = ((), (), s32[]{:S(2)}) async-start(), calls=%async_computation.11 | async-start | bytes 3604480 | tf_op jit(solution)/shard_map/all_gather | solution.py:915
  110.5 25.7 %collective-permute-start.17 = (bf16[256,2048]{1,0:T(8,128)(2,1)}, bf16[256,2048]{1,0:T(8,128)(2,1)}, u32[]{:S(2)}, u32[]{:S(2)}) collective-permute-start(bf16[256,2048]{1,0:T(8,128)(2,1)} %after.34), channel_id=1, source_target_pairs={{0,16},{1,3},{2,18},{3,1},{16,0},{17,19},{18,2},{19,17},{4,20},{5,... | collective-permute-start | bytes 3145736 | tf_op jit(solution)/shard_map/ppermute | solution.py:49
  112.1 24.4 %collective-permute-start.18 = (bf16[256,2048]{1,0:T(8,128)(2,1)}, bf16[256,2048]{1,0:T(8,128)(2,1)}, u32[]{:S(2)}, u32[]{:S(2)}) collective-permute-start(bf16[256,2048]{1,0:T(8,128)(2,1)} %after.34), channel_id=1, source_target_pairs={{0,2},{1,17},{2,0},{3,19},{16,18},{17,1},{18,16},{19,3},{4,6},{5,2... | collective-permute-start | bytes 3145736 | tf_op jit(solution)/shard_map/ppermute | solution.py:49
  129.8 31.9 %collective-permute-start.22 = (bf16[256,2048]{1,0:T(8,128)(2,1)S(1)}, bf16[256,2048]{1,0:T(8,128)(2,1)S(1)}, u32[]{:S(2)}, u32[]{:S(2)}) collective-permute-start(bf16[256,2048]{1,0:T(8,128)(2,1)S(1)} %get-tuple-element.92), channel_id=1, source_target_pairs={{0,2},{1,17},{2,0},{3,19},{16,18},{17,1},{18,16},{19,3},{4,6},{5,2... | collective-permute-start | bytes 3145736 | tf_op jit(solution)/shard_map/ppermute | solution.py:49
  131.4 27.4 %collective-permute-start.23 = (bf16[256,2048]{1,0:T(8,128)(2,1)S(1)}, bf16[256,2048]{1,0:T(8,128)(2,1)S(1)}, u32[]{:S(2)}, u32[]{:S(2)}) collective-permute-start(bf16[256,2048]{1,0:T(8,128)(2,1)S(1)} %get-tuple-element.94), channel_id=1, source_target_pairs={{0,2},{1,17},{2,0},{3,19},{16,18},{17,1},{18,16},{19,3},{4,6},{5,2... | collective-permute-start | bytes 3145736 | tf_op jit(solution)/shard_map/ppermute | solution.py:49
  184.2 26.2 %collective-permute-start.25 = (bf16[256,2048]{1,0:T(8,128)(2,1)}, bf16[256,2048]{1,0:T(8,128)(2,1)S(1)}, u32[]{:S(2)}, u32[]{:S(2)}) collective-permute-start(bf16[256,2048]{1,0:T(8,128)(2,1)} %get-tuple-element.96.refs_0_.refs_1_), channel_id=1, source_target_pairs={{0,16},{1,3},{2,18},{3,1},{16,0},{17,19},{18,2},{19,17},{4,20},{5,... | collective-permute-start | bytes 3145736 | tf_op jit(solution)/shard_map/ppermute | solution.py:49
  185.7 24.7 %collective-permute-start.26 = (bf16[256,2048]{1,0:T(8,128)(2,1)}, bf16[256,2048]{1,0:T(8,128)(2,1)S(1)}, u32[]{:S(2)}, u32[]{:S(2)}) collective-permute-start(bf16[256,2048]{1,0:T(8,128)(2,1)} %get-tuple-element.96.refs_0_.refs_1_), channel_id=1, source_target_pairs={{0,2},{1,17},{2,0},{3,19},{16,18},{17,1},{18,16},{19,3},{4,6},{5,2... | collective-permute-start | bytes 3145736 | tf_op jit(solution)/shard_map/ppermute | solution.py:49
  215.8 224.1 %reduce-scatter.9.cloned.1.call-start = ((), (), s32[]{:S(2)}) async-start(), calls=%async_computation.8 | async-start | bytes 3604480 | tf_op jit(solution)/shard_map/reduce_scatter | solution.py:919
  231.2 25.7 %collective-permute-start.29 = (bf16[256,2048]{1,0:T(8,128)(2,1)}, bf16[256,2048]{1,0:T(8,128)(2,1)}, u32[]{:S(2)}, u32[]{:S(2)}) collective-permute-start(bf16[256,2048]{1,0:T(8,128)(2,1)} %after.40), channel_id=1, source_target_pairs={{0,2},{1,17},{2,0},{3,19},{16,18},{17,1},{18,16},{19,3},{4,6},{5,2... | collective-permute-start | bytes 3145736 | tf_op jit(solution)/shard_map/ppermute | solution.py:49
  232.7 25.5 %collective-permute-start.34 = (bf16[256,2048]{1,0:T(8,128)(2,1)}, bf16[256,2048]{1,0:T(8,128)(2,1)}, u32[]{:S(2)}, u32[]{:S(2)}) collective-permute-start(bf16[256,2048]{1,0:T(8,128)(2,1)} %refs_2_.1), channel_id=1, source_target_pairs={{0,1},{1,0},{2,3},{3,2},{16,17},{17,16},{18,19},{19,18},{4,5},{5,4... | collective-permute-start | bytes 3145736 | tf_op jit(solution)/shard_map/ppermute | solution.py:49
  232.7 25.9 %collective-permute-start.35 = (bf16[256,2048]{1,0:T(8,128)(2,1)}, bf16[256,2048]{1,0:T(8,128)(2,1)}, u32[]{:S(2)}, u32[]{:S(2)}) collective-permute-start(bf16[256,2048]{1,0:T(8,128)(2,1)} %collective-permute-done.17.refs_0_.refs_2_.refs_1_), channel_id=1, source_target_pairs={{0,1},{1,0},{2,3},{3,2},{16,17},{17,16},{18,19},{19,18},{4,5},{5,4... | collective-permute-start | bytes 3145736 | tf_op jit(solution)/shard_map/ppermute | solution.py:49
  233.2 25.5 %collective-permute-start.36 = (bf16[256,2048]{1,0:T(8,128)(2,1)}, bf16[256,2048]{1,0:T(8,128)(2,1)}, u32[]{:S(2)}, u32[]{:S(2)}) collective-permute-start(bf16[256,2048]{1,0:T(8,128)(2,1)} %collective-permute-done.18.refs_1_.refs_3_), channel_id=1, source_target_pairs={{0,1},{1,0},{2,3},{3,2},{16,17},{17,16},{18,19},{19,18},{4,5},{5,4... | collective-permute-start | bytes 3145736 | tf_op jit(solution)/shard_map/ppermute | solution.py:49
  274.3 28.2 %collective-permute-start.41 = (bf16[256,2048]{1,0:T(8,128)(2,1)}, bf16[256,2048]{1,0:T(8,128)(2,1)}, u32[]{:S(2)}, u32[]{:S(2)}) collective-permute-start(bf16[256,2048]{1,0:T(8,128)(2,1)} %get-tuple-element.96.refs_0_.refs_1_), channel_id=1, source_target_pairs={{0,1},{1,0},{2,3},{3,2},{16,17},{17,16},{18,19},{19,18},{4,5},{5,4... | collective-permute-start | bytes 3145736 | tf_op jit(solution)/shard_map/ppermute | solution.py:49
  274.8 51.0 %collective-permute-start.42 = (bf16[256,2048]{1,0:T(8,128)(2,1)S(1)}, bf16[256,2048]{1,0:T(8,128)(2,1)}, u32[]{:S(2)}, u32[]{:S(2)}) collective-permute-start(bf16[256,2048]{1,0:T(8,128)(2,1)S(1)} %copy-done.9), channel_id=1, source_target_pairs={{0,1},{1,0},{2,3},{3,2},{16,17},{17,16},{18,19},{19,18},{4,5},{5,4... | collective-permute-start | bytes 3145736 | tf_op jit(solution)/shard_map/ppermute | solution.py:49
  274.8 51.1 %collective-permute-start.43 = (bf16[256,2048]{1,0:T(8,128)(2,1)S(1)}, bf16[256,2048]{1,0:T(8,128)(2,1)}, u32[]{:S(2)}, u32[]{:S(2)}) collective-permute-start(bf16[256,2048]{1,0:T(8,128)(2,1)S(1)} %copy-done.23), channel_id=1, source_target_pairs={{0,1},{1,0},{2,3},{3,2},{16,17},{17,16},{18,19},{19,18},{4,5},{5,4... | collective-permute-start | bytes 3145736 | tf_op jit(solution)/shard_map/ppermute | solution.py:49
  275.3 54.8 %collective-permute-start.44 = (bf16[256,2048]{1,0:T(8,128)(2,1)}, bf16[256,2048]{1,0:T(8,128)(2,1)}, u32[]{:S(2)}, u32[]{:S(2)}) collective-permute-start(bf16[256,2048]{1,0:T(8,128)(2,1)} %collective-permute-done.27.refs_3_.refs_1_.refs_4_), channel_id=1, source_target_pairs={{0,1},{1,0},{2,3},{3,2},{16,17},{17,16},{18,19},{19,18},{4,5},{5,4... | collective-permute-start | bytes 3145736 | tf_op jit(solution)/shard_map/ppermute | solution.py:49
  275.4 187.2 %reduce-scatter.7.cloned.1.call-start = ((), (), s32[]{:S(2)}) async-start(), calls=%async_computation.7 | async-start | bytes 7208960 | tf_op jit(solution)/shard_map/reduce_scatter | solution.py:919
  301.0 25.4 %collective-permute-start.39 = (bf16[256,2048]{1,0:T(8,128)(2,1)S(1)}, bf16[256,2048]{1,0:T(8,128)(2,1)S(1)}, u32[]{:S(2)}, u32[]{:S(2)}) collective-permute-start(bf16[256,2048]{1,0:T(8,128)(2,1)S(1)} %get-tuple-element.105), channel_id=1, source_target_pairs={{0,2},{1,17},{2,0},{3,19},{16,18},{17,1},{18,16},{19,3},{4,6},{5,2... | collective-permute-start | bytes 3145736 | tf_op jit(solution)/shard_map/ppermute | solution.py:49
  302.5 24.8 %collective-permute-start.40 = (bf16[256,2048]{1,0:T(8,128)(2,1)S(1)}, bf16[256,2048]{1,0:T(8,128)(2,1)}, u32[]{:S(2)}, u32[]{:S(2)}) collective-permute-start(bf16[256,2048]{1,0:T(8,128)(2,1)S(1)} %get-tuple-element.106), channel_id=1, source_target_pairs={{0,2},{1,17},{2,0},{3,19},{16,18},{17,1},{18,16},{19,3},{4,6},{5,2... | collective-permute-start | bytes 3145736 | tf_op jit(solution)/shard_map/ppermute | solution.py:49
  330.1 25.9 %collective-permute-start.49 = (bf16[256,2048]{1,0:T(8,128)(2,1)}, bf16[256,2048]{1,0:T(8,128)(2,1)S(1)}, u32[]{:S(2)}, u32[]{:S(2)}) collective-permute-start(bf16[256,2048]{1,0:T(8,128)(2,1)} %after.43.refs_0_), channel_id=1, source_target_pairs={{0,16},{1,3},{2,18},{3,1},{16,0},{17,19},{18,2},{19,17},{4,20},{5,... | collective-permute-start | bytes 3145736 | tf_op jit(solution)/shard_map/ppermute | solution.py:49
  355.7 165.0 %reduce-scatter.5.cloned.1.call-start = ((), (), s32[]{:S(2)}) async-start(), calls=%async_computation.6 | async-start | bytes 4055040 | tf_op jit(solution)/shard_map/reduce_scatter | solution.py:919
  355.8 84.1 %collective-permute-start.56 = (bf16[1024,2048]{1,0:T(8,128)(2,1)}, bf16[1024,2048]{1,0:T(8,128)(2,1)}, u32[]{:S(2)}, u32[]{:S(2)}) collective-permute-start(bf16[1024,2048]{1,0:T(8,128)(2,1)} %get-tuple-element.125.refs_1_), channel_id=1, source_target_pairs={{0,1},{1,0},{2,3},{3,2},{16,17},{17,16},{18,19},{19,18},{4,5},{5,4... | collective-permute-start | bytes 12582920 | tf_op jit(solution)/shard_map/ppermute | solution.py:49
  382.1 26.2 %collective-permute-start.52 = (bf16[256,2048]{1,0:T(8,128)(2,1)}, bf16[256,2048]{1,0:T(8,128)(2,1)S(1)}, u32[]{:S(2)}, u32[]{:S(2)}) collective-permute-start(bf16[256,2048]{1,0:T(8,128)(2,1)} %after.44.refs_2_.refs_1_.refs_5_), channel_id=1, source_target_pairs={{0,2},{1,17},{2,0},{3,19},{16,18},{17,1},{18,16},{19,3},{4,6},{5,2... | collective-permute-start | bytes 3145736 | tf_op jit(solution)/shard_map/ppermute | solution.py:49
  383.4 25.0 %collective-permute-start.51 = (bf16[256,2048]{1,0:T(8,128)(2,1)}, bf16[256,2048]{1,0:T(8,128)(2,1)S(1)}, u32[]{:S(2)}, u32[]{:S(2)}) collective-permute-start(bf16[256,2048]{1,0:T(8,128)(2,1)} %after.45), channel_id=1, source_target_pairs={{0,2},{1,17},{2,0},{3,19},{16,18},{17,1},{18,16},{19,3},{4,6},{5,2... | collective-permute-start | bytes 3145736 | tf_op jit(solution)/shard_map/ppermute | solution.py:49
  406.1 35.0 %collective-permute-start.57 = (bf16[256,768]{1,0:T(8,128)(2,1)}, bf16[256,768]{1,0:T(8,128)(2,1)}, u32[]{:S(2)}, u32[]{:S(2)}) collective-permute-start(bf16[256,768]{1,0:T(8,128)(2,1)} %get-tuple-element.127), channel_id=1, source_target_pairs={{0,1},{1,0},{2,3},{3,2},{16,17},{17,16},{18,19},{19,18},{4,5},{5,4... | collective-permute-start | bytes 1179656 | tf_op jit(solution)/shard_map/ppermute | solution.py:49
  406.1 35.0 %collective-permute-start.58 = (bf16[256,768]{1,0:T(8,128)(2,1)}, bf16[256,768]{1,0:T(8,128)(2,1)}, u32[]{:S(2)}, u32[]{:S(2)}) collective-permute-start(bf16[256,768]{1,0:T(8,128)(2,1)} %get-tuple-element.128), channel_id=1, source_target_pairs={{0,1},{1,0},{2,3},{3,2},{16,17},{17,16},{18,19},{19,18},{4,5},{5,4... | collective-permute-start | bytes 1179656 | tf_op jit(solution)/shard_map/ppermute | solution.py:49
  410.3 25.9 %collective-permute-start.54 = (bf16[256,2048]{1,0:T(8,128)(2,1)}, bf16[256,2048]{1,0:T(8,128)(2,1)}, u32[]{:S(2)}, u32[]{:S(2)}) collective-permute-start(bf16[256,2048]{1,0:T(8,128)(2,1)} %after.47), channel_id=1, source_target_pairs={{0,2},{1,17},{2,0},{3,19},{16,18},{17,1},{18,16},{19,3},{4,6},{5,2... | collective-permute-start | bytes 3145736 | tf_op jit(solution)/shard_map/ppermute | solution.py:49
  411.6 25.1 %collective-permute-start.53 = (bf16[256,2048]{1,0:T(8,128)(2,1)}, bf16[256,2048]{1,0:T(8,128)(2,1)}, u32[]{:S(2)}, u32[]{:S(2)}) collective-permute-start(bf16[256,2048]{1,0:T(8,128)(2,1)} %after.46), channel_id=1, source_target_pairs={{0,2},{1,17},{2,0},{3,19},{16,18},{17,1},{18,16},{19,3},{4,6},{5,2... | collective-permute-start | bytes 3145736 | tf_op jit(solution)/shard_map/ppermute | solution.py:49
  439.9 19.3 %collective-permute-start.75 = (bf16[176,2048]{1,0:T(8,128)(2,1)}, bf16[176,2048]{1,0:T(8,128)(2,1)}, u32[]{:S(2)}, u32[]{:S(2)}) collective-permute-start(bf16[176,2048]{1,0:T(8,128)(2,1)} %after.53), channel_id=1, source_target_pairs={{0,16},{1,17},{2,18},{3,19},{16,0},{17,1},{18,2},{19,3},{4,20},{5,... | collective-permute-start | bytes 2162696 | tf_op jit(solution)/shard_map/ppermute | solution.py:49
  454.5 32.9 %collective-permute-start.61 = (bf16[256,2048]{1,0:T(8,128)(2,1)}, bf16[256,2048]{1,0:T(8,128)(2,1)S(1)}, u32[]{:S(2)}, u32[]{:S(2)}) collective-permute-start(bf16[256,2048]{1,0:T(8,128)(2,1)} %after.49), channel_id=1, source_target_pairs={{0,2},{1,17},{2,0},{3,19},{16,18},{17,1},{18,16},{19,3},{4,6},{5,2... | collective-permute-start | bytes 3145736 | tf_op jit(solution)/shard_map/ppermute | solution.py:49
  455.5 129.9 %reduce-scatter.11.cloned.1.call-start = ((), (), s32[]{:S(2)}) async-start(), calls=%async_computation.9 | async-start | bytes 1310720 | tf_op jit(solution)/shard_map/reduce_scatter | solution.py:919
  465.8 22.6 %collective-permute-start.67 = (bf16[128,1408]{1,0:T(8,128)(2,1)}, bf16[128,1408]{1,0:T(8,128)(2,1)S(1)}, u32[]{:S(2)}, u32[]{:S(2)}) collective-permute-start(bf16[128,1408]{1,0:T(8,128)(2,1)} %get-tuple-element.136), channel_id=1, source_target_pairs={{0,1},{1,0},{2,3},{3,2},{16,17},{17,16},{18,19},{19,18},{4,5},{5,4... | collective-permute-start | bytes 1081352 | tf_op jit(solution)/shard_map/ppermute | solution.py:49
  465.8 25.6 %collective-permute-start.68 = (bf16[128,1408]{1,0:T(8,128)(2,1)}, bf16[128,1408]{1,0:T(8,128)(2,1)}, u32[]{:S(2)}, u32[]{:S(2)}) collective-permute-start(bf16[128,1408]{1,0:T(8,128)(2,1)} %get-tuple-element.137), channel_id=1, source_target_pairs={{0,2},{1,3},{2,0},{3,1},{16,18},{17,19},{18,16},{19,17},{4,6},{5,7... | collective-permute-start | bytes 1081352 | tf_op jit(solution)/shard_map/ppermute | solution.py:49
  466.9 26.9 %collective-permute-start.69 = (bf16[128,1408]{1,0:T(8,128)(2,1)}, bf16[128,1408]{1,0:T(8,128)(2,1)}, u32[]{:S(2)}, u32[]{:S(2)}) collective-permute-start(bf16[128,1408]{1,0:T(8,128)(2,1)} %get-tuple-element.138), channel_id=1, source_target_pairs={{0,3},{1,2},{2,1},{3,0},{16,19},{17,18},{18,17},{19,16},{4,7},{5,6... | collective-permute-start | bytes 1081352 | tf_op jit(solution)/shard_map/ppermute | solution.py:49
  507.2 26.1 %collective-permute-start.55 = (bf16[256,2048]{1,0:T(8,128)(2,1)S(1)}, bf16[256,2048]{1,0:T(8,128)(2,1)}, u32[]{:S(2)}, u32[]{:S(2)}) collective-permute-start(bf16[256,2048]{1,0:T(8,128)(2,1)S(1)} %copy-done.6), channel_id=1, source_target_pairs={{0,16},{1,3},{2,18},{3,1},{16,0},{17,19},{18,2},{19,17},{4,20},{5,... | collective-permute-start | bytes 3145736 | tf_op jit(solution)/shard_map/ppermute | solution.py:49
  508.3 55.9 %collective-permute-start.70 = (bf16[512,1408]{1,0:T(8,128)(2,1)}, bf16[512,1408]{1,0:T(8,128)(2,1)}, u32[]{:S(2)}, u32[]{:S(2)}) collective-permute-start(bf16[512,1408]{1,0:T(8,128)(2,1)} %place_blocks.10), channel_id=1, source_target_pairs={{0,16},{1,17},{2,18},{3,19},{16,0},{17,1},{18,2},{19,3},{4,20},{5,... | collective-permute-start | bytes 4325384 | tf_op jit(solution)/shard_map/ppermute | solution.py:49
  509.2 54.9 %collective-permute-start.63 = (bf16[256,2048]{1,0:T(8,128)(2,1)S(1)}, bf16[256,2048]{1,0:T(8,128)(2,1)S(1)}, u32[]{:S(2)}, u32[]{:S(2)}) collective-permute-start(bf16[256,2048]{1,0:T(8,128)(2,1)S(1)} %copy-done.12), channel_id=1, source_target_pairs={{0,16},{1,3},{2,18},{3,1},{16,0},{17,19},{18,2},{19,17},{4,20},{5,... | collective-permute-start | bytes 3145736 | tf_op jit(solution)/shard_map/ppermute | solution.py:49
  537.7 36.8 %collective-permute-start.65 = (f32[4,896]{1,0:T(4,128)S(1)}, f32[4,896]{1,0:T(4,128)S(1)}, u32[]{:S(2)}, u32[]{:S(2)}) collective-permute-start(f32[4,896]{1,0:T(4,128)S(1)} %add.89), channel_id=1, source_target_pairs={{0,2},{2,0},{1,3},{3,1},{4,6},{6,4},{5,7},{7,5},{8,10},{10,8},{9,1... | collective-permute-start | bytes 43016 | tf_op jit(solution)/shard_map/ppermute | solution.py:78
  577.5 20.4 %collective-permute-start.74 = (bf16[512,768]{1,0:T(8,128)(2,1)S(1)}, bf16[512,768]{1,0:T(8,128)(2,1)S(1)}, u32[]{:S(2)}, u32[]{:S(2)}) collective-permute-start(bf16[512,768]{1,0:T(8,128)(2,1)S(1)} %place_blocks.11), channel_id=1, source_target_pairs={{0,16},{1,17},{2,18},{3,19},{16,0},{17,1},{18,2},{19,3},{4,20},{5,... | collective-permute-start | bytes 2359304 | tf_op jit(solution)/shard_map/ppermute | solution.py:49
  (141 other events, 867.5 us)
Sparse Core Ops, SparseCore 0:
  10.2 30.6 all-gather.10
  43.0 64.3 all-gather.6
  109.5 105.2 all-gather.8
  216.8 57.4 all-gather.12
  277.0 54.8 reduce-scatter.8
  355.9 100.1 reduce-scatter.6
  458.4 62.3 reduce-scatter.4
  524.7 27.3 reduce-scatter.10
